TPU v7x, 512 devices: a whole 4x8x8 slice. The times are simulated.
512 devices in a mesh: dp: 128 (over z, y, core), tensor: 4 (over x).
Axes of the slice: x: 4, y: 8, z: 8, core: 2. Of those that a mesh axis runs over, the one named last changes fastest.
Arguments:
- context: bfloat16 [65536, 3584], P('dp', 'tensor'), may hold values from -6 to 6
- residual: bfloat16 [65536, 3584], P(('dp', 'tensor')), may hold values from -6 to 6
- out_weight: bfloat16 [3584, 3584], P('tensor', 'dp'), may hold values from -0.09375 to 0.09375
- norm_gain: float32 [3584], replicated, may hold values from 0.25 to 1.75
- members: bfloat16 [128, 512, 3584], P('dp', None, 'tensor'), may hold values from -6 to 6
- doc_lengths: int32 [512, 32], P(('dp', 'tensor')), may hold values from 1 to 12, 128 in all within a row
- doc_cluster: int32 [16384, 1], P('dp'), may hold values from 0 to 127; in each aligned block of 128 rows (0 to 127, 128 to 255, ...) at most 2 rows name the same one
- owner_map: int32 [128], replicated, may hold values from 0 to 127, each once
- member_counts: int32 [128], replicated, may hold values from 128 to 512, as said below
Outputs:
- match_scores: float32 [16384, 512], P('dp', 'tensor')
- best_match: float32 [16384], P('dp')
Inputs may be any that keep to these rules, and one draw needn't show every extreme that they name: `doc_cluster`: among the documents of one index of dp (aligned blocks of 128 rows), at most 2 name the same cluster, and exactly 2 do so in some block. `member_counts`: each a multiple of 128; some cluster has exactly 512. `owner_map`: each index of dp appears once. `doc_lengths`: each row sums to 128; its largest entry is 12.
All inputs are finite; a program needn't handle non-finite values.
Results may differ from a plain program's by a relative error of at most 0.022.
Values may be sent and summed in bfloat16 or wider, within the bound.
No kernel may reach another device: no remote copies, remote signals or barrier semaphores. Data moves between devices by JAX's collectives and lax.ppermute only.
A program may use at most 64 MiB of HBM per device.

v0:
```python
import jax
import jax.numpy as jnp
from jax import lax
from jax.sharding import PartitionSpec as P


def body(
    context,
    residual,
    out_weight,
    norm_gain,
    members,
    doc_lengths,
    doc_cluster,
    owner_map,
    member_counts,
):
    local_rows = residual.shape[0]
    width = residual.shape[1]
    partial_term = jnp.dot(
        context,
        lax.all_gather(out_weight, "dp", axis=1, tiled=True),
        preferred_element_type=jnp.float32,
    )
    total_sum = lax.psum(partial_term.astype(jnp.bfloat16), "tensor").astype(jnp.float32)
    summed = lax.dynamic_slice_in_dim(
        total_sum, lax.axis_index("tensor") * local_rows, local_rows, 0
    )
    hidden = residual.astype(jnp.float32) + summed
    scale_rms = lax.rsqrt(jnp.mean(hidden * hidden, axis=-1, keepdims=True) + 1e-06)
    normed = (hidden * scale_rms * norm_gain).astype(jnp.bfloat16)
    pack_count = doc_lengths.shape[0]
    docs_pack = doc_lengths.shape[1]
    pack_tokens = local_rows // pack_count
    packed = normed.reshape(pack_count, pack_tokens, width)
    ends = jnp.cumsum(doc_lengths, axis=1)
    starts = ends - doc_lengths
    positions = jnp.arange(pack_tokens, dtype=jnp.int32)
    inside = (positions[None, None, :] >= starts[:, :, None]) & (
        positions[None, None, :] < ends[:, :, None]
    )
    pooled = jnp.einsum(
        "npk,nkd->npd", inside.astype(jnp.bfloat16), packed, preferred_element_type=jnp.float32
    )
    pooled = pooled / doc_lengths.astype(jnp.float32)[:, :, None]
    embedded = pooled * lax.rsqrt(jnp.sum(pooled * pooled, axis=-1, keepdims=True) + 1e-06)
    embedded = embedded.astype(jnp.bfloat16).reshape(pack_count * docs_pack, width)
    doc_quarter = lax.all_to_all(embedded, "tensor", split_axis=1, concat_axis=0, tiled=True)
    doc_count = doc_cluster.shape[0]
    quarter = doc_quarter.shape[1]
    group_count = lax.axis_size("dp")
    capacity = max(2, 2 * doc_count // group_count)
    cluster_ids = jnp.arange(owner_map.shape[0], dtype=jnp.int32)
    matches = doc_cluster[:, 0][:, None] == cluster_ids[None, :]
    doc_owner = jnp.sum(jnp.where(matches, owner_map[None, :], 0), axis=1)
    doc_members = jnp.sum(jnp.where(matches, member_counts[None, :], 0), axis=1)
    doc_order = jnp.arange(doc_count, dtype=jnp.int32)
    same_owner = (doc_owner[:, None] == doc_owner[None, :]) & (
        doc_order[:, None] > doc_order[None, :]
    )
    doc_rank = jnp.sum(same_owner.astype(jnp.int32), axis=1)
    doc_slot = doc_owner * capacity + doc_rank
    outgoing = (
        jnp.zeros((group_count * capacity, quarter), jnp.bfloat16).at[doc_slot].set(doc_quarter)
    )
    outgoing = outgoing.reshape(group_count, capacity, quarter)
    resident = members[0]
    member_rows = resident.shape[0]
    column_share = member_rows // lax.axis_size("tensor")
    own_count = jnp.sum(jnp.where(owner_map == lax.axis_index("dp"), member_counts, 0))
    resident_f = resident.astype(jnp.float32)
    member_partial = jnp.sum(resident_f * resident_f, axis=-1)
    columns = lax.axis_index("tensor") * column_share + jnp.arange(column_share, dtype=jnp.int32)
    full_width = quarter * lax.axis_size("tensor")
    arrived_rows = lax.all_to_all(outgoing, "dp", split_axis=0, concat_axis=0, tiled=True).reshape(
        -1, quarter
    )
    contract = (((1,), (1,)), ((), ()))
    dots = lax.dot_general(arrived_rows, resident, contract, preferred_element_type=jnp.float32)
    dots_share = lax.psum_scatter(
        dots.astype(jnp.bfloat16), "tensor", scatter_dimension=1, tiled=True
    ).astype(jnp.float32)
    square_share = lax.psum_scatter(
        member_partial.astype(jnp.bfloat16), "tensor", scatter_dimension=0, tiled=True
    ).astype(jnp.float32)
    scaled = dots_share * lax.rsqrt(square_share / full_width + 1e-06)[None, :]
    scaled = jnp.where(columns[None, :] < own_count, scaled, 0.0)
    scaled = scaled.reshape(group_count, -1, column_share)
    returned = lax.all_to_all(
        scaled.astype(jnp.bfloat16), "dp", split_axis=0, concat_axis=0, tiled=True
    ).astype(scaled.dtype)
    doc_scores = returned.reshape(group_count * capacity, column_share)[doc_slot]
    live_cols = columns[None, :] < doc_members[:, None]
    local_best = jnp.max(jnp.where(live_cols, doc_scores, -1000000000.0), axis=1)
    best_match = lax.pmax(local_best, "tensor")
    return (doc_scores, best_match)


def solution(mesh):
    in_specs = (
        P("dp", "tensor"),
        P(("dp", "tensor"), None),
        P("tensor", "dp"),
        P(),
        P("dp", None, "tensor"),
        P(("dp", "tensor"), None),
        P("dp", None),
        P(),
        P(),
    )
    out_specs = (P("dp", "tensor"), P("dp"))
    return jax.shard_map(body, mesh=mesh, in_specs=in_specs, out_specs=out_specs, check_vma=False)
```

profile of v0, /device:TPU:2, one launch (start us, length us, event | category | flops | bytes accessed | tf_op | source)
XLA Modules:
  0.0 324.2 jit_solution(17813395964027590042)
XLA Ops:
  7.2 0.7 all-gather.3.cloned.1.call-update
  8.0 95.2 %all-gather.3.cloned.1.call-done = bf16[128,28,896]{2,1,0:T(8,128)(2,1)} async-done(((bf16[1,28,896]{2,1,0:T(8,128)(2,1)}), bf16[128,28,896]{2,1,0:T(8,128)(2,1)}) %all-gather.3.cloned.1.call-update) | async-done | bytes 6422544 | tf_op jit(solution)/shard_map/all_gather | solution.py:22
  103.2 10.4 %reshape.159 = bf16[3584,896]{1,0:T(8,128)(2,1)} reshape(bf16[128,28,896]{2,1,0:T(8,128)(2,1)} %all-gather.3.cloned.1.call-done) | data formatting | bytes 12845056
  113.6 8.2 %convolution_convert_fusion = bf16[512,3584]{1,0:T(8,128)(2,1)} fusion(bf16[512,896]{1,0:T(8,128)(2,1)S(1)} %copy-done, bf16[3584,896]{1,0:T(8,128)(2,1)} %reshape.159), kind=kOutput, calls=%fused_computation.2 | convolution fusion | flops 3290169344 | bytes 11010048 | tf_op jit(solution)/shard_map/dot_general | solution.py:20
  121.9 0.6 copy-done.7
  122.5 0.2 reduce_window_sum.11
  122.9 0.2 convert_reduce_fusion
  123.1 89.5 %all-reduce.3.cloned.1.call-done = bf16[512,3584]{1,0:T(8,128)(2,1)} async-done(((bf16[512,3584]{1,0:T(8,128)(2,1)}), bf16[512,3584]{1,0:T(8,128)(2,1)}) %all-reduce.3.cloned.1.call-update) | async-done | bytes 3670032 | tf_op jit(solution)/shard_map/psum | solution.py:25
  212.6 1.6 multiply_reduce_fusion.1
  214.2 1.8 multiply_reduce_fusion.2
  216.1 0.7 copy.18
  216.8 5.2 %all-to-all-start = ((bf16[32,4,896]{2,0,1:T(8,128)(2,1)}), bf16[32,4,896]{2,0,1:T(8,128)(2,1)S(1)}, u32[]{:S(2)}, u32[]{:S(2)}) async-start(bf16[32,4,896]{2,0,1:T(8,128)(2,1)} %bitcast.32), calls=%async_computation | async-start | bytes 458752 | tf_op jit(solution)/shard_map/all_to_all | solution.py:48
  222.0 5.1 %all-to-all-done = bf16[32,4,896]{2,0,1:T(8,128)(2,1)S(1)} async-done(((bf16[32,4,896]{2,0,1:T(8,128)(2,1)}), bf16[32,4,896]{2,0,1:T(8,128)(2,1)S(1)}, u32[]{:S(2)}, u32[]{:S(2)}) %all-to-all-start) | async-done | bytes 229408 | tf_op jit(solution)/shard_map/all_to_all | solution.py:48
  227.1 1.3 scatter_custom_fusion
  228.4 0.2 reshape.136
  228.6 32.6 %all_to_all.29 = bf16[128,2,896]{2,1,0:T(2,128)(2,1)S(1)} all-to-all(bf16[128,2,896]{2,1,0:T(2,128)(2,1)S(1)} %reshape.136), channel_id=1, replica_groups=mesh['dp'=128,'tensor'=4] {'dp'}, dimensions={0} | all-to-all | bytes 917504 | tf_op jit(solution)/shard_map/all_to_all | solution.py:75
  261.2 0.2 reshape.137
  261.4 0.5 convolution_convert_fusion.1
  261.8 0.8 copy.14
  262.7 1.3 dynamic-slice
  264.6 0.3 multiply_reduce_fusion
  264.9 9.2 %all-reduce = bf16[512]{0:T(512)(128)(2,1)S(1)} all-reduce(bf16[512]{0:T(512)(128)(2,1)S(1)} %multiply_reduce_fusion), channel_id=3, replica_groups=mesh['dp'=128,'tensor'=4] {'tensor'}, use_global_device_ids=true, to_apply=%region_10.11.clone | all-reduce | flops 512 | bytes 2048
  274.1 0.6 fusion.11
  274.7 0.7 broadcast_compare_fusion
  275.4 4.4 %reduce-scatter.4.cloned.1.call-done = bf16[128,256]{1,0:T(8,128)(2,1)} async-done(((bf16[512,256]{1,0:T(8,128)(2,1)}), bf16[128,256]{1,0:T(8,128)(2,1)}) %reduce-scatter.4.cloned.1.call-update) | async-done | bytes 65552
  279.9 0.9 copy.15
  280.8 0.7 select_convert_fusion
  281.5 13.7 %all-to-all-start.2 = ((bf16[128,2,128]{2,1,0:T(2,128)(2,1)}), bf16[128,2,128]{2,1,0:T(2,128)(2,1)S(1)}, u32[]{:S(2)}, u32[]{:S(2)}) async-start(bf16[128,2,128]{2,1,0:T(2,128)(2,1)} %bitcast.11), calls=%async_computation.2 | async-start | bytes 131072 | tf_op jit(solution)/shard_map/all_to_all | solution.py:89
  295.2 11.0 %all-to-all-done.2 = bf16[128,2,128]{2,1,0:T(2,128)(2,1)S(1)} async-done(((bf16[128,2,128]{2,1,0:T(2,128)(2,1)}), bf16[128,2,128]{2,1,0:T(2,128)(2,1)S(1)}, u32[]{:S(2)}, u32[]{:S(2)}) %all-to-all-start.2) | async-done | bytes 65568 | tf_op jit(solution)/shard_map/all_to_all | solution.py:89
  306.3 0.6 gather_fusion
  306.9 0.2 select_reduce_fusion
  307.1 10.6 %pmax.7 = f32[128]{0:T(128)} all-reduce(f32[128]{0:T(128)S(1)} %select_reduce_fusion), channel_id=1, replica_groups=mesh['dp'=128,'tensor'=4] {'tensor'}, use_global_device_ids=true, to_apply=%region_13.14 | all-reduce | flops 128 | bytes 1024 | tf_op jit(solution)/shard_map/pmax | solution.py:95
  (32 shorter events, 0.6 us)
Async XLA Ops:
  7.2 106.5 %copy-start = (bf16[512,896]{1,0:T(8,128)(2,1)S(1)}, bf16[512,896]{1,0:T(8,128)(2,1)}, u32[]{:S(2)}) copy-start(bf16[512,896]{1,0:T(8,128)(2,1)} %param.9) | copy-start | bytes 2752516
  7.2 96.0 %all-gather.3.cloned.1.call-start = ((), (), s32[]{:S(2)}) async-start(), calls=%async_computation.5 | async-start | bytes 7397376 | tf_op jit(solution)/shard_map/all_gather | solution.py:22
  7.9 204.7 %all-reduce.3.cloned.1.call-start = ((), (), s32[]{:S(2)}) async-start(), calls=%async_computation.4 | async-start | bytes 7340032 | tf_op jit(solution)/shard_map/psum | solution.py:25
  121.9 0.7 copy-start.7
  121.9 0.9 copy-start.4
  121.9 0.9 copy-start.5
  121.9 0.9 copy-start.6
  121.9 90.7 %copy-start.2 = (bf16[128,3584]{1,0:T(8,128)(2,1)S(1)}, bf16[128,3584]{1,0:T(8,128)(2,1)}, u32[]{:S(2)}) copy-start(bf16[128,3584]{1,0:T(8,128)(2,1)} %param.10) | copy-start | bytes 2752516
  121.9 92.3 %copy-start.8 = (f32[3584]{0:T(1024)S(1)}, f32[3584]{0:T(1024)}, u32[]{:S(2)}) copy-start(f32[3584]{0:T(1024)} %param.12) | copy-start | bytes 43012
  216.8 44.6 %copy-start.1 = (bf16[1,512,896]{2,1,0:T(8,128)(2,1)S(1)}, bf16[1,512,896]{2,1,0:T(8,128)(2,1)}, u32[]{:S(2)}) copy-start(bf16[1,512,896]{2,1,0:T(8,128)(2,1)} %param.13) | copy-start | bytes 2752516
  216.8 10.3 %all-to-all-start = ((bf16[32,4,896]{2,0,1:T(8,128)(2,1)}), bf16[32,4,896]{2,0,1:T(8,128)(2,1)S(1)}, u32[]{:S(2)}, u32[]{:S(2)}) async-start(bf16[32,4,896]{2,0,1:T(8,128)(2,1)} %bitcast.32), calls=%async_computation | async-start | bytes 458752 | tf_op jit(solution)/shard_map/all_to_all | solution.py:48
  221.9 57.9 %reduce-scatter.4.cloned.1.call-start = ((), (), s32[]{:S(2)}) async-start(), calls=%async_computation.6 | async-start | bytes 327680
  281.5 24.8 %all-to-all-start.2 = ((bf16[128,2,128]{2,1,0:T(2,128)(2,1)}), bf16[128,2,128]{2,1,0:T(2,128)(2,1)S(1)}, u32[]{:S(2)}, u32[]{:S(2)}) async-start(bf16[128,2,128]{2,1,0:T(2,128)(2,1)} %bitcast.11), calls=%async_computation.2 | async-start | bytes 131072 | tf_op jit(solution)/shard_map/all_to_all | solution.py:89
  306.9 10.8 %copy-start.3 = (f32[128,128]{1,0:T(8,128)}, f32[128,128]{1,0:T(8,128)S(1)}, u32[]{:S(2)}) copy-start(f32[128,128]{1,0:T(8,128)S(1)} %gather_fusion) | copy-start | bytes 196612
Sparse Core Ops, SparseCore 0:
  11.1 91.9 all-gather.2
  122.0 90.5 all-reduce.2
  262.8 17.0 reduce-scatter.3
where the time goes:
time: 325 us; the launch traced here: 324 us
  waiting for transfers between devices  206 us (63%)
  blocking collectives  52.4 us (16%)
  starting transfers between devices  18.9 us (6%)
  local copies, waits for them, and re-layouts  17.1 us (5%)
  between operations  14.6 us (4%)
  matrix products  10.5 us (3%)
  other arithmetic  4.71 us (1%)
    all_gather x1, waiting for transfers between devices, body(): lax.all_gather(out_weight, 'dp', axis=1, tiled=True)  95.2 us
    psum x1, waiting for transfers between devices, body(): lax.psum(partial_term.astype(jnp.bfloat16), 'tensor').astype(jnp.float32)  89.5 us
    all_to_all x1, blocking collectives, body(): lax.all_to_all(outgoing, 'dp', split_axis=0, concat_axis=0, tiled=True)  32.6 us
    unnamed x22, local copies, waits for them, and re-layouts  14.1 us
    all_to_all x1, starting transfers between devices, body(): lax.all_to_all(scaled.astype(jnp.bfloat16), 'dp', split_axis=0, concat_ax...  13.7 us
    all_to_all x1, waiting for transfers between devices, body(): lax.all_to_all(scaled.astype(jnp.bfloat16), 'dp', split_axis=0, concat_ax...  11 us
    pmax x1, blocking collectives, body(): best_match = lax.pmax(local_best, 'tensor')  10.6 us
    unnamed x1, blocking collectives  9.2 us
  transfers between devices with their start and end apart: 5, of which 5 were waited for; matrix products, arithmetic and copies ran while one was open for 1% of the time, Pallas kernels for 0%

commit v1 on v0

v1 whole, which is shorter than its diff:
```python
import jax
import jax.numpy as jnp
from jax import lax
from jax.experimental import pallas as pl
from jax.experimental.pallas import tpu as pltpu
from jax.sharding import Mesh, PartitionSpec as P

DP = ("z", "y", "core")
ALL = ("z", "y", "core", "tensor")
SIZES = {"z": 8, "y": 8, "core": 2, "tensor": 4}
BF = jnp.bfloat16
F32 = jnp.float32
NT = (((1,), (1,)), ((), ()))
VMEM = pl.BlockSpec(memory_space=pltpu.VMEM)
SMEM = pl.BlockSpec(memory_space=pltpu.SMEM)
TOK, QUARTER, HALF, KPIECE, KSTEP = 512, 896, 448, 512, 384
DOCS, SLOTS, MEMBERS, SHARE = 128, 256, 512, 128


def params():
    return pltpu.CompilerParams(vmem_limit_bytes=40 * 1024 * 1024)


def cost(flops, nbytes):
    return pl.CostEstimate(flops=flops, bytes_accessed=nbytes, transcendentals=0)


def shift(value, axis, step):
    size = SIZES[axis]
    return lax.ppermute(value, axis, [(i, (i + step) % size) for i in range(size)])


def spread(flip):
    pairs = []
    for z in range(8):
        for y in range(8):
            for core in range(2):
                for x in range(4):
                    source = ((z * 8 + y) * 2 + core) * 4 + x
                    target = (((2 * x + z % 2) * 8 + y) * 2 + (core ^ flip)) * 4 + z // 2
                    pairs.append((source, target))
    return pairs


def others(value):
    return shift(value, "tensor", 1), shift(value, "tensor", -1), shift(value, "tensor", 2)


def project_kernel(place, ctx, res, *refs):
    own, swapped = refs[0:9], refs[9:18]
    hidden, squares, total = refs[18:]
    z, core = place[0], place[1]
    lane_own = pl.multiple_of(core * KSTEP, 128)
    lane_other = pl.multiple_of((1 - core) * KSTEP, 128)
    total[...] = jnp.zeros_like(total)
    steps = [0, -1, 1, -2, 2, -3, 3]
    for index, step in enumerate(steps):
        at = lax.rem(z + step + 8, 8)
        quarter, half = lax.div(at, 2), lax.rem(at, 2)
        total[half] += lax.dot_general(
            ctx[quarter, :, pl.ds(lane_own, KPIECE)], own[index][...], NT, preferred_element_type=F32
        ) + lax.dot_general(
            ctx[quarter, :, pl.ds(lane_other, KPIECE)], swapped[index][...], NT, preferred_element_type=F32
        )
    at = lax.rem(z + 4, 8)
    quarter, half = lax.div(at, 2), lax.rem(at, 2)
    last_own = jnp.concatenate([own[7][...], own[8][...]], axis=0)
    last_swapped = jnp.concatenate([swapped[7][...], swapped[8][...]], axis=0)
    total[half] += lax.dot_general(
        ctx[quarter, :, pl.ds(lane_own, KPIECE)], last_own, NT, preferred_element_type=F32
    ) + lax.dot_general(
        ctx[quarter, :, pl.ds(lane_other, KPIECE)], last_swapped, NT, preferred_element_type=F32
    )
    for pack in range(4):
        rows = pl.ds(pack * 128, 128)
        value = jnp.concatenate([total[0, rows, :], total[1, rows, :]], axis=1)
        value = value + res[rows, :].astype(F32)
        hidden[rows, :] = value
        sq = value * value
        part = sq[:, 0:128]
        for tile in range(1, 7):
            part = part + sq[:, tile * 128 : tile * 128 + 128]
        squares[pl.ds(pack, 1), :] = jnp.sum(part.T, axis=0, keepdims=True)
    squares[pl.ds(4, 4), :] = jnp.zeros((4, 128), F32)


def pool_kernel(hidden, gain, pool, inverse, sq0, sq1, sq2, sq3, slots, squares):
    total = (sq0[...] + sq1[...]) + (sq2[...] + sq3[...])
    scale = lax.rsqrt(total / 3584.0 + 1e-06)
    summed = None
    for pack in range(4):
        rows = pl.ds(pack * 128, 128)
        column = jnp.broadcast_to(scale[pack : pack + 1, :], (128, 128)).T
        column = jnp.concatenate([column] * 7, axis=1)
        normed = (hidden[rows, :] * column * gain[...]).astype(BF)
        term = jnp.dot(pool[:, pack * 128 : pack * 128 + 128], normed, preferred_element_type=F32)
        summed = term if summed is None else summed + term
    pooled = summed * jnp.concatenate([inverse[...]] * 7, axis=1)
    slots[...] = pooled.astype(BF)
    sq = pooled * pooled
    part = sq[:, 0:128]
    for tile in range(1, 7):
        part = part + sq[:, tile * 128 : tile * 128 + 128]
    squares[...] = jnp.zeros_like(squares)
    for block in range(2):
        squares[pl.ds(block, 1), :] = jnp.sum(
            part[block * 128 : block * 128 + 128, :].T, axis=0, keepdims=True
        )


def dots_kernel(place, arrived, members, factor, *outs):
    x = place[2]
    for step in range(4):
        at = lax.rem(x + step, 4)
        rows = pl.ds(pl.multiple_of(at * SHARE, SHARE), SHARE)
        dots = lax.dot_general(arrived[...], members[rows, :], NT, preferred_element_type=F32)
        outs[step][...] = (dots * factor[pl.ds(at, 1), :]).astype(BF)


def home_kernel(returned, pick, scale, live, scores, best):
    rows = jnp.dot(pick[...], returned[...], preferred_element_type=F32) * scale[...]
    scores[...] = rows
    masked = jnp.where(live[...] > 0.0, rows, -1000000000.0)
    best[...] = jnp.broadcast_to(jnp.max(masked.T, axis=0, keepdims=True), (8, 128))


def body(
    context,
    residual,
    out_weight,
    norm_gain,
    members,
    doc_lengths,
    doc_cluster,
    owner_map,
    member_counts,
):
    z, y = lax.axis_index("z"), lax.axis_index("y")
    core, x = lax.axis_index("core"), lax.axis_index("tensor")
    place = jnp.stack([z, core, x]).astype(jnp.int32)

    weight = out_weight.T
    lanes = lax.broadcasted_iota(jnp.int32, (28, KPIECE), 1)
    low = weight[:, :KPIECE]
    high = jnp.where(lanes < 128, 0, weight[:, KSTEP:])
    keep = lax.ppermute(jnp.where(core == 0, low, high), ALL, spread(0))
    cross = lax.ppermute(jnp.where(core == 0, high, low), ALL, spread(1))
    block = jnp.concatenate(
        [jnp.where(core == 0, keep, cross), jnp.where(core == 0, cross, keep)], axis=0
    )

    ctx_down, ctx_up = shift(context, "tensor", 1), shift(context, "tensor", -1)

    below, above = shift(block, "y", 1), shift(block, "y", -1)
    far_below = shift(jnp.concatenate([below, block, above], axis=0), "y", 3)
    far_above = shift(jnp.concatenate([below, block], axis=0), "y", -3)
    around = jnp.concatenate([far_below, below, block, above, far_above], axis=0)
    around = jnp.concatenate([around, around], axis=0)
    begin = lax.rem(4 - y + 8, 8) * 56
    plane = lax.dynamic_slice(around, (begin, 0), (HALF, KPIECE))

    res_parts = [
        lax.dynamic_slice(residual, (0, lax.rem(x + step, 4) * QUARTER), (128, QUARTER))
        for step in range(4)
    ]
    res_recv = [
        res_parts[0],
        shift(res_parts[1], "tensor", 1),
        shift(res_parts[2], "tensor", 2),
        shift(res_parts[3], "tensor", 3),
    ]
    res = jnp.zeros((TOK, QUARTER), BF)
    for step in range(4):
        res = lax.dynamic_update_slice(res, res_recv[step], (lax.rem(x - step + 4, 4) * 128, 0))

    resident = members[0]
    resident_f = resident.astype(F32)
    partial_sq = jnp.sum(resident_f * resident_f, axis=-1).reshape(4, 128)
    lens_row = jnp.pad(doc_lengths.astype(F32), ((0, 3), (0, 96)))
    small = jnp.concatenate([partial_sq, lens_row], axis=0)
    small_down, small_up, small_far = others(small)
    member_sq = (partial_sq + small_down[:4]) + (small_up[:4] + small_far[:4])
    lens = jnp.zeros((4, 32), F32)
    for step, value in ((0, small), (3, small_down), (1, small_up), (2, small_far)):
        lens = lax.dynamic_update_slice(lens, value[4:5, :32], (lax.rem(x + step, 4), 0))

    downs, ups = [], []
    down, up = plane, plane
    for _ in range(3):
        down, up = shift(down, "z", 1), shift(up, "z", -1)
        downs.append(down)
        ups.append(up)
    half_rows = HALF // 2
    last_a = shift(downs[2][:half_rows], "z", 1)
    last_b = shift(ups[2][half_rows:], "z", -1)
    own = [plane, downs[0], ups[0], downs[1], ups[1], downs[2], ups[2], last_a, last_b]
    swapped = [shift(value, "core", 1) for value in own]

    far_a = shift(ctx_down[: TOK // 2], "tensor", 1)
    far_b = shift(ctx_up[TOK // 2 :], "tensor", -1)
    ctx = jnp.zeros((4, TOK, QUARTER), BF)
    ctx = lax.dynamic_update_slice(ctx, context[None], (x, 0, 0))
    ctx = lax.dynamic_update_slice(ctx, ctx_down[None], (lax.rem(x + 3, 4), 0, 0))
    ctx = lax.dynamic_update_slice(ctx, ctx_up[None], (lax.rem(x + 1, 4), 0, 0))
    ctx = lax.dynamic_update_slice(ctx, far_a[None], (lax.rem(x + 2, 4), 0, 0))
    ctx = lax.dynamic_update_slice(ctx, far_b[None], (lax.rem(x + 2, 4), TOK // 2, 0))

    cluster_ids = jnp.arange(owner_map.shape[0], dtype=jnp.int32)
    matches = doc_cluster[:, 0][:, None] == cluster_ids[None, :]
    doc_owner = jnp.sum(jnp.where(matches, owner_map[None, :], 0), axis=1)
    doc_members = jnp.sum(jnp.where(matches, member_counts[None, :], 0), axis=1)
    doc_order = jnp.arange(DOCS, dtype=jnp.int32)
    same_owner = (doc_owner[:, None] == doc_owner[None, :]) & (
        doc_order[:, None] > doc_order[None, :]
    )
    doc_slot = doc_owner * 2 + jnp.sum(same_owner.astype(jnp.int32), axis=1)
    slot_ids = jnp.arange(SLOTS, dtype=jnp.int32)
    select = slot_ids[:, None] == doc_slot[None, :]
    pick = (doc_slot[:, None] == slot_ids[None, :]).astype(BF)
    lens_int = lens.astype(jnp.int32)
    ends = jnp.cumsum(lens_int, axis=1)
    offsets = 128 * jnp.arange(4, dtype=jnp.int32)[:, None]
    doc_begin = (ends - lens_int + offsets).reshape(DOCS)
    doc_end = (ends + offsets).reshape(DOCS)
    tokens = jnp.arange(TOK, dtype=jnp.int32)
    inside = (tokens[None, :] >= doc_begin[:, None]) & (tokens[None, :] < doc_end[:, None])
    pool = jnp.dot(select.astype(BF), inside.astype(BF), preferred_element_type=F32).astype(BF)
    slot_len = jnp.sum(jnp.where(select, lens.reshape(DOCS)[None, :], 0.0), axis=1)
    inverse = jnp.broadcast_to((1.0 / jnp.maximum(slot_len, 1.0))[:, None], (SLOTS, 128))
    columns = x * SHARE + jnp.arange(SHARE, dtype=jnp.int32)
    live = (columns[None, :] < doc_members[:, None]).astype(F32)

    own_dp = (z * 8 + y) * 2 + core
    own_count = jnp.sum(jnp.where(owner_map == own_dp, member_counts, 0))
    member_ids = jnp.arange(MEMBERS, dtype=jnp.int32).reshape(4, 128)
    factor = jnp.where(member_ids < own_count, lax.rsqrt(member_sq / 3584.0 + 1e-06), 0.0)

    hidden, squares = pl.pallas_call(
        project_kernel,
        out_shape=(
            jax.ShapeDtypeStruct((TOK, QUARTER), F32),
            jax.ShapeDtypeStruct((8, 128), F32),
        ),
        in_specs=[SMEM] + [VMEM] * 20,
        out_specs=(VMEM, VMEM),
        scratch_shapes=[pltpu.VMEM((2, TOK, HALF), F32)],
        compiler_params=params(),
        cost_estimate=cost(2 * TOK * QUARTER * 4096, 16_000_000),
        name="project",
    )(place, ctx, res, *own, *swapped)

    slots, doc_sq = pl.pallas_call(
        pool_kernel,
        out_shape=(
            jax.ShapeDtypeStruct((SLOTS, QUARTER), BF),
            jax.ShapeDtypeStruct((8, 128), F32),
        ),
        in_specs=[VMEM] * 8,
        out_specs=(VMEM, VMEM),
        compiler_params=params(),
        cost_estimate=cost(2 * SLOTS * TOK * QUARTER, 3_000_000),
        name="pool",
    )(hidden, gain_of(norm_gain, x), pool, inverse, squares, *others(squares))

    arrived = lax.all_to_all(
        slots.reshape(DOCS, 2, QUARTER), DP, split_axis=0, concat_axis=0, tiled=True
    ).reshape(SLOTS, QUARTER)

    doc_sq_all = [doc_sq, *others(doc_sq)]
    slot_sq = sum(doc_sq_all[1:], doc_sq_all[0])[:2].reshape(SLOTS)
    doc_total = jnp.sum(jnp.where(select, slot_sq[:, None], 0.0), axis=0)
    scale = jnp.broadcast_to(lax.rsqrt(doc_total + 1e-06)[:, None], (DOCS, SHARE))

    partials = pl.pallas_call(
        dots_kernel,
        out_shape=tuple(jax.ShapeDtypeStruct((SLOTS, SHARE), BF) for _ in range(4)),
        in_specs=[SMEM] + [VMEM] * 3,
        out_specs=(VMEM,) * 4,
        compiler_params=params(),
        cost_estimate=cost(2 * SLOTS * MEMBERS * QUARTER, 2_000_000),
        name="dots",
    )(place, arrived, resident, factor)
    received = [partials[0]] + [shift(partials[step], "tensor", step) for step in range(1, 4)]
    scored = sum((value.astype(F32) for value in received[1:]), received[0].astype(F32)).astype(BF)

    returned = lax.all_to_all(
        scored.reshape(DOCS, 2, SHARE), DP, split_axis=0, concat_axis=0, tiled=True
    ).reshape(SLOTS, SHARE)
    scores, best = pl.pallas_call(
        home_kernel,
        out_shape=(
            jax.ShapeDtypeStruct((DOCS, SHARE), F32),
            jax.ShapeDtypeStruct((8, 128), F32),
        ),
        in_specs=[VMEM] * 4,
        out_specs=(VMEM, VMEM),
        compiler_params=params(),
        cost_estimate=cost(2 * SLOTS * DOCS * SHARE, 400_000),
        name="home",
    )(returned, pick, scale, live)
    best_down, best_up, best_far = others(best)
    best = jnp.maximum(jnp.maximum(best, best_down), jnp.maximum(best_up, best_far))
    return scores, best[0]


def gain_of(norm_gain, x):
    return lax.dynamic_slice(norm_gain, (x * QUARTER,), (QUARTER,)).reshape(1, QUARTER)


def solution(mesh):
    split = Mesh(mesh.devices.reshape(8, 8, 2, 4), ALL)
    in_specs = (
        P(DP, "tensor"),
        P(ALL, None),
        P("tensor", DP),
        P(),
        P(DP, None, "tensor"),
        P(ALL, None),
        P(DP, None),
        P(),
        P(),
    )
    out_specs = (P(DP, "tensor"), P(DP))
    return jax.shard_map(body, mesh=split, in_specs=in_specs, out_specs=out_specs, check_vma=False)
```

time: 325 us -> 273 us (0.84)
  starting transfers between devices: 18.9 us -> 176 us
  waiting for transfers between devices: 206 us -> 57.2 us
  blocking collectives: 52.4 us -> 0 us
  between operations: 14.6 us -> 1.58 us
  Pallas kernels: 0 us -> 10.3 us
  matrix products: 10.5 us -> 0.33 us
    ppermute x0 -> x45, starting transfers between devices: none -> 156 us  [the longest x43 150 us: shift(): lax.ppermute(value, axis, [(i, (i + step) % size) for i in range(size)])]
    all_gather x1 -> x0, waiting for transfers between devices: 95.2 us -> none  [body(): lax.all_gather(out_weight, 'dp', axis=1, tiled=True)]
    psum x1 -> x0, waiting for transfers between devices: 89.5 us -> none  [body(): lax.psum(partial_term.astype(jnp.bfloat16), 'tensor').astype(jnp.float32)]
    ppermute x0 -> x45, waiting for transfers between devices: none -> 42.1 us  [the longest x43 40 us: shift(): lax.ppermute(value, axis, [(i, (i + step) % size) for i in range(size)])]
    all_to_all x1 -> x0, blocking collectives: 32.6 us -> none  [body(): lax.all_to_all(outgoing, 'dp', split_axis=0, concat_axis=0, tiled=True)]
    unnamed x22 -> x16, local copies, waits for them, and re-layouts: 14.1 us -> 0.04 us
    pmax x1 -> x0, blocking collectives: 10.6 us -> none  [body(): best_match = lax.pmax(local_best, 'tensor')]
    pallas_call x0 -> x4, Pallas kernels: none -> 10.3 us  [the longest x1 7.45 us: body(): pl.pallas_call(project_kernel, out_shape=(jax.ShapeDtypeStruct((TOK, QUAR...]
  transfers between devices with their start and end apart: 5 -> 47, of which waited for: 5 -> 12; matrix products, arithmetic and copies ran while one was open for 1% -> 8% of each run, Pallas kernels for 0% -> 0%
where the time goes in v1:
time: 273 us; the launch traced here: 271 us
  starting transfers between devices  176 us (64%)
  waiting for transfers between devices  57.2 us (21%)
  local copies, waits for them, and re-layouts  19 us (7%)
  Pallas kernels  10.3 us (4%)
  other arithmetic  6.58 us (2%)
    ppermute x43, starting transfers between devices, shift(): lax.ppermute(value, axis, [(i, (i + step) % size) for i in range(size)])  150 us
    ppermute x43, waiting for transfers between devices, shift(): lax.ppermute(value, axis, [(i, (i + step) % size) for i in range(size)])  40 us
    all_to_all x1, waiting for transfers between devices, body(): lax.all_to_all(scored.reshape(DOCS, 2, SHARE), DP, split_axis=0, concat_a...  11.1 us
    all_to_all x1, starting transfers between devices, body(): lax.all_to_all(slots.reshape(DOCS, 2, QUARTER), DP, split_axis=0, concat_...  10.4 us
    all_to_all x1, starting transfers between devices, body(): lax.all_to_all(scored.reshape(DOCS, 2, SHARE), DP, split_axis=0, concat_a...  9.6 us
    pallas_call x1, Pallas kernels, body(): pl.pallas_call(project_kernel, out_shape=(jax.ShapeDtypeStruct((TOK, QUAR...  7.45 us
  transfers between devices with their start and end apart: 47, of which 12 were waited for; matrix products, arithmetic and copies ran while one was open for 8% of the time, Pallas kernels for 0%

profile of v1, /device:TPU:2, one launch (start us, length us, event | category | flops | bytes accessed | tf_op | source)
XLA Modules:
  0.0 270.9 jit_solution(17875099051398432834)
XLA Ops:
  2.8 3.4 %collective-permute-start.30 = (f32[8,128]{1,0:T(8,128)S(1)}, f32[8,128]{1,0:T(8,128)S(1)}, u32[]{:S(2)}, u32[]{:S(2)}) collective-permute-start(f32[8,128]{1,0:T(8,128)S(1)} %select_maximum_fusion), channel_id=1, source_target_pairs={{0,1},{1,2},{2,3},{3,0},{4,5},{5,6},{6,7},{7,4},{8,9},{9,10},{10,1... | collective-permute-start | bytes 12296 | tf_op jit(solution)/shard_map/ppermute | solution.py:30
  6.2 6.3 %collective-permute-start.31 = (f32[8,128]{1,0:T(8,128)S(1)}, f32[8,128]{1,0:T(8,128)S(1)}, u32[]{:S(2)}, u32[]{:S(2)}) collective-permute-start(f32[8,128]{1,0:T(8,128)S(1)} %select_maximum_fusion), channel_id=1, source_target_pairs={{0,3},{1,0},{2,1},{3,2},{4,7},{5,4},{6,5},{7,6},{8,11},{9,8},{10,9... | collective-permute-start | bytes 12296 | tf_op jit(solution)/shard_map/ppermute | solution.py:30
  16.8 3.6 %collective-permute-start.7 = (bf16[28,512]{1,0:T(8,128)(2,1)S(1)}, bf16[28,512]{1,0:T(8,128)(2,1)S(1)}, u32[]{:S(2)}, u32[]{:S(2)}) collective-permute-start(bf16[28,512]{1,0:T(8,128)(2,1)S(1)} %get-tuple-element.30), channel_id=1, source_target_pairs={{0,0},{1,128},{2,256},{3,384},{4,4},{5,132},{6,260},{7,388},{8,8},... | collective-permute-start | bytes 86024 | tf_op jit(solution)/shard_map/ppermute | solution.py:146
  27.6 3.5 %collective-permute-start.9 = (bf16[56,512]{1,0:T(8,128)(2,1)S(1)}, bf16[56,512]{1,0:T(8,128)(2,1)S(1)}, u32[]{:S(2)}, u32[]{:S(2)}) collective-permute-start(bf16[56,512]{1,0:T(8,128)(2,1)S(1)} %pad_maximum_fusion.2), channel_id=1, source_target_pairs={{0,8},{8,16},{16,24},{24,32},{32,40},{40,48},{48,56},{56,0},{1,9},... | collective-permute-start | bytes 172040 | tf_op jit(solution)/shard_map/ppermute | solution.py:30
  31.1 3.8 %collective-permute-start.10 = (bf16[56,512]{1,0:T(8,128)(2,1)S(1)}, bf16[56,512]{1,0:T(8,128)(2,1)S(1)}, u32[]{:S(2)}, u32[]{:S(2)}) collective-permute-start(bf16[56,512]{1,0:T(8,128)(2,1)S(1)} %pad_maximum_fusion.2), channel_id=1, source_target_pairs={{0,56},{8,0},{16,8},{24,16},{32,24},{40,32},{48,40},{56,48},{1,57}... | collective-permute-start | bytes 172040 | tf_op jit(solution)/shard_map/ppermute | solution.py:30
  37.2 7.9 %collective-permute-start.11 = (bf16[168,512]{1,0:T(8,128)(2,1)S(1)}, bf16[168,512]{1,0:T(8,128)(2,1)S(1)}, u32[]{:S(2)}, u32[]{:S(2)}) collective-permute-start(bf16[168,512]{1,0:T(8,128)(2,1)S(1)} %pad_maximum_fusion), channel_id=1, source_target_pairs={{0,24},{8,32},{16,40},{24,48},{32,56},{40,0},{48,8},{56,16},{1,25}... | collective-permute-start | bytes 516104 | tf_op jit(solution)/shard_map/ppermute | solution.py:30
  47.3 7.9 %collective-permute-done.12 = bf16[112,512]{1,0:T(8,128)(2,1)S(1)} collective-permute-done((bf16[112,512]{1,0:T(8,128)(2,1)S(1)}, bf16[112,512]{1,0:T(8,128)(2,1)S(1)}, u32[]{:S(2)}, u32[]{:S(2)}) %collective-permute-start.12) | collective-permute-done | bytes 114720 | tf_op jit(solution)/shard_map/ppermute | solution.py:30
  55.7 5.2 %collective-permute-start.13 = (bf16[448,512]{1,0:T(8,128)(2,1)S(1)}, bf16[448,512]{1,0:T(8,128)(2,1)S(1)}, u32[]{:S(2)}, u32[]{:S(2)}) collective-permute-start(bf16[448,512]{1,0:T(8,128)(2,1)S(1)} %constant_dynamic-slice_fusion.refs_0_), channel_id=1, source_target_pairs={{0,64},{64,128},{128,192},{192,256},{256,320},{320,384},{384,448},... | collective-permute-start | bytes 1376264 | tf_op jit(solution)/shard_map/ppermute | solution.py:30
  60.9 10.7 %collective-permute-start.14 = (bf16[448,512]{1,0:T(8,128)(2,1)S(1)}, bf16[448,512]{1,0:T(8,128)(2,1)S(1)}, u32[]{:S(2)}, u32[]{:S(2)}) collective-permute-start(bf16[448,512]{1,0:T(8,128)(2,1)S(1)} %constant_dynamic-slice_fusion.refs_0_), channel_id=1, source_target_pairs={{0,448},{64,0},{128,64},{192,128},{256,192},{320,256},{384,320},{4... | collective-permute-start | bytes 1376264 | tf_op jit(solution)/shard_map/ppermute | solution.py:30
  75.9 4.3 %collective-permute-start.5 = (bf16[128,896]{1,0:T(8,128)(2,1)}, bf16[128,896]{1,0:T(8,128)(2,1)}, u32[]{:S(2)}, u32[]{:S(2)}) collective-permute-start(bf16[128,896]{1,0:T(8,128)(2,1)} %get-tuple-element.27), channel_id=1, source_target_pairs={{0,2},{1,3},{2,0},{3,1},{4,6},{5,7},{6,4},{7,5},{8,10},{9,11},{10,... | collective-permute-start | bytes 688136 | tf_op jit(solution)/shard_map/ppermute | solution.py:30
  82.5 4.9 %collective-permute-start.16 = (bf16[448,512]{1,0:T(8,128)(2,1)S(1)}, bf16[448,512]{1,0:T(8,128)(2,1)S(1)}, u32[]{:S(2)}, u32[]{:S(2)}) collective-permute-start(bf16[448,512]{1,0:T(8,128)(2,1)S(1)} %collective-permute-done.14.refs_2_), channel_id=1, source_target_pairs={{0,448},{64,0},{128,64},{192,128},{256,192},{320,256},{384,320},{4... | collective-permute-start | bytes 1376264 | tf_op jit(solution)/shard_map/ppermute | solution.py:30
  88.4 4.4 %collective-permute-start = (bf16[512,896]{1,0:T(8,128)(2,1)}, bf16[512,896]{1,0:T(8,128)(2,1)}, u32[]{:S(2)}, u32[]{:S(2)}) collective-permute-start(bf16[512,896]{1,0:T(8,128)(2,1)} %param.9), channel_id=1, source_target_pairs={{0,1},{1,2},{2,3},{3,0},{4,5},{5,6},{6,7},{7,4},{8,9},{9,10},{10,1... | collective-permute-start | bytes 2752520 | tf_op jit(solution)/shard_map/ppermute | solution.py:30
  96.0 3.7 %collective-permute-start.6 = (bf16[128,896]{1,0:T(8,128)(2,1)S(1)}, bf16[128,896]{1,0:T(8,128)(2,1)S(1)}, u32[]{:S(2)}, u32[]{:S(2)}) collective-permute-start(bf16[128,896]{1,0:T(8,128)(2,1)S(1)} %get-tuple-element.24), channel_id=1, source_target_pairs={{0,3},{1,0},{2,1},{3,2},{4,7},{5,4},{6,5},{7,6},{8,11},{9,8},{10,9... | collective-permute-start | bytes 688136 | tf_op jit(solution)/shard_map/ppermute | solution.py:30
  100.0 16.7 %collective-permute-done.6 = bf16[128,896]{1,0:T(8,128)(2,1)S(1)} collective-permute-done((bf16[128,896]{1,0:T(8,128)(2,1)S(1)}, bf16[128,896]{1,0:T(8,128)(2,1)S(1)}, u32[]{:S(2)}, u32[]{:S(2)}) %collective-permute-start.6) | collective-permute-done | bytes 229408 | tf_op jit(solution)/shard_map/ppermute | solution.py:30
  120.6 5.1 %collective-permute-start.18 = (bf16[448,512]{1,0:T(8,128)(2,1)S(1)}, bf16[448,512]{1,0:T(8,128)(2,1)S(1)}, u32[]{:S(2)}, u32[]{:S(2)}) collective-permute-start(bf16[448,512]{1,0:T(8,128)(2,1)S(1)} %collective-permute-done.16.refs_4_), channel_id=1, source_target_pairs={{0,448},{64,0},{128,64},{192,128},{256,192},{320,256},{384,320},{4... | collective-permute-start | bytes 1376264 | tf_op jit(solution)/shard_map/ppermute | solution.py:30
  136.8 3.4 %collective-permute-start.3 = (bf16[256,896]{1,0:T(8,128)(2,1)S(1)}, bf16[256,896]{1,0:T(8,128)(2,1)S(1)}, u32[]{:S(2)}, u32[]{:S(2)}) collective-permute-start(bf16[256,896]{1,0:T(8,128)(2,1)S(1)} %slice.58), channel_id=1, source_target_pairs={{0,3},{1,0},{2,1},{3,2},{4,7},{5,4},{6,5},{7,6},{8,11},{9,8},{10,9... | collective-permute-start | bytes 1376264 | tf_op jit(solution)/shard_map/ppermute | solution.py:30
  150.9 5.1 %collective-permute-start.20 = (bf16[224,512]{1,0:T(8,128)(2,1)S(1)}, bf16[224,512]{1,0:T(8,128)(2,1)S(1)}, u32[]{:S(2)}, u32[]{:S(2)}) collective-permute-start(bf16[224,512]{1,0:T(8,128)(2,1)S(1)} %slice.62), channel_id=1, source_target_pairs={{0,448},{64,0},{128,64},{192,128},{256,192},{320,256},{384,320},{4... | collective-permute-start | bytes 688136 | tf_op jit(solution)/shard_map/ppermute | solution.py:30
  166.7 7.5 %project.1 = (f32[512,896]{1,0:T(8,128)S(1)}, f32[8,128]{1,0:T(8,128)S(1)}) custom-call(s32[3]{0:T(128)S(1)} %pad_add_fusion.place, bf16[4,512,896]{2,1,0:T(8,128)(2,1)} %bitcast_dynamic-update-slice_fusion.3.ctx, bf16[512,896]{1,0:T(8,128)(2,1)S(1)} %constant_dynamic-update-slice_fusion.res, bf16[448,512]{1,0:T(8,128)(2,1)S(1)} %constant_dynamic-slice_fusion.refs_0_, ...), custom_call_target="tpu_custom_call" | custom-call | flops 3758096384 | bytes 16000000 | tf_op jit(solution)/shard_map/project/pallas_call | solution.py:238
  176.8 4.2 %collective-permute-start.34 = (f32[8,128]{1,0:T(8,128)S(1)}, f32[8,128]{1,0:T(8,128)S(1)}, u32[]{:S(2)}, u32[]{:S(2)}) collective-permute-start(f32[8,128]{1,0:T(8,128)S(1)} %get-tuple-element.13.sq0), channel_id=1, source_target_pairs={{0,3},{1,0},{2,1},{3,2},{4,7},{5,4},{6,5},{7,6},{8,11},{9,8},{10,9... | collective-permute-start | bytes 12296 | tf_op jit(solution)/shard_map/ppermute | solution.py:30
  181.0 4.0 %collective-permute-start.35 = (f32[8,128]{1,0:T(8,128)S(1)}, f32[8,128]{1,0:T(8,128)S(1)}, u32[]{:S(2)}, u32[]{:S(2)}) collective-permute-start(f32[8,128]{1,0:T(8,128)S(1)} %get-tuple-element.13.sq0), channel_id=1, source_target_pairs={{0,2},{1,3},{2,0},{3,1},{4,6},{5,7},{6,4},{7,5},{8,10},{9,11},{10,... | collective-permute-start | bytes 12296 | tf_op jit(solution)/shard_map/ppermute | solution.py:30
  189.9 10.4 %all-to-all-start = ((bf16[128,2,896]{2,1,0:T(2,128)(2,1)}), bf16[128,2,896]{2,1,0:T(2,128)(2,1)S(1)}, u32[]{:S(2)}, u32[]{:S(2)}) async-start(bf16[128,2,896]{2,1,0:T(2,128)(2,1)} %reshape.80), calls=%async_computation | async-start | bytes 917504 | tf_op jit(solution)/shard_map/all_to_all | solution.py:265
  200.4 3.4 %collective-permute-start.39 = (f32[8,128]{1,0:T(8,128)S(1)}, f32[8,128]{1,0:T(8,128)S(1)}, u32[]{:S(2)}, u32[]{:S(2)}) collective-permute-start(f32[8,128]{1,0:T(8,128)S(1)} %get-tuple-element.19), channel_id=1, source_target_pairs={{0,1},{1,2},{2,3},{3,0},{4,5},{5,6},{6,7},{7,4},{8,9},{9,10},{10,1... | collective-permute-start | bytes 12296 | tf_op jit(solution)/shard_map/ppermute | solution.py:30
  203.8 3.7 %collective-permute-start.40 = (f32[8,128]{1,0:T(8,128)S(1)}, f32[8,128]{1,0:T(8,128)S(1)}, u32[]{:S(2)}, u32[]{:S(2)}) collective-permute-start(f32[8,128]{1,0:T(8,128)S(1)} %get-tuple-element.19), channel_id=1, source_target_pairs={{0,3},{1,0},{2,1},{3,2},{4,7},{5,4},{6,5},{7,6},{8,11},{9,8},{10,9... | collective-permute-start | bytes 12296 | tf_op jit(solution)/shard_map/ppermute | solution.py:30
  207.5 4.0 %collective-permute-start.41 = (f32[8,128]{1,0:T(8,128)S(1)}, f32[8,128]{1,0:T(8,128)S(1)}, u32[]{:S(2)}, u32[]{:S(2)}) collective-permute-start(f32[8,128]{1,0:T(8,128)S(1)} %get-tuple-element.19), channel_id=1, source_target_pairs={{0,2},{1,3},{2,0},{3,1},{4,6},{5,7},{6,4},{7,5},{8,10},{9,11},{10,... | collective-permute-start | bytes 12296 | tf_op jit(solution)/shard_map/ppermute | solution.py:30
  214.5 4.1 %all-to-all-done = bf16[128,2,896]{2,1,0:T(2,128)(2,1)S(1)} async-done(((bf16[128,2,896]{2,1,0:T(2,128)(2,1)}), bf16[128,2,896]{2,1,0:T(2,128)(2,1)S(1)}, u32[]{:S(2)}, u32[]{:S(2)}) %all-to-all-start) | async-done | bytes 458784 | tf_op jit(solution)/shard_map/all_to_all | solution.py:265
  220.0 3.4 %collective-permute-start.36 = (bf16[256,128]{1,0:T(8,128)(2,1)S(1)}, bf16[256,128]{1,0:T(8,128)(2,1)S(1)}, u32[]{:S(2)}, u32[]{:S(2)}) collective-permute-start(bf16[256,128]{1,0:T(8,128)(2,1)S(1)} %get-tuple-element.16), channel_id=1, source_target_pairs={{0,1},{1,2},{2,3},{3,0},{4,5},{5,6},{6,7},{7,4},{8,9},{9,10},{10,1... | collective-permute-start | bytes 196616 | tf_op jit(solution)/shard_map/ppermute | solution.py:30
  223.4 5.7 %collective-permute-start.37 = (bf16[256,128]{1,0:T(8,128)(2,1)S(1)}, bf16[256,128]{1,0:T(8,128)(2,1)S(1)}, u32[]{:S(2)}, u32[]{:S(2)}) collective-permute-start(bf16[256,128]{1,0:T(8,128)(2,1)S(1)} %get-tuple-element.17), channel_id=1, source_target_pairs={{0,2},{1,3},{2,0},{3,1},{4,6},{5,7},{6,4},{7,5},{8,10},{9,11},{10,... | collective-permute-start | bytes 196616 | tf_op jit(solution)/shard_map/ppermute | solution.py:30
  231.7 3.6 %collective-permute-done.38 = bf16[256,128]{1,0:T(8,128)(2,1)S(1)} collective-permute-done((bf16[256,128]{1,0:T(8,128)(2,1)S(1)}, bf16[256,128]{1,0:T(8,128)(2,1)S(1)}, u32[]{:S(2)}, u32[]{:S(2)}) %collective-permute-start.38) | collective-permute-done | bytes 65568 | tf_op jit(solution)/shard_map/ppermute | solution.py:30
  236.0 9.6 %all-to-all-start.1 = ((bf16[128,2,128]{2,1,0:T(2,128)(2,1)}), bf16[128,2,128]{2,1,0:T(2,128)(2,1)S(1)}, u32[]{:S(2)}, u32[]{:S(2)}) async-start(bf16[128,2,128]{2,1,0:T(2,128)(2,1)} %bitcast.12), calls=%async_computation.1 | async-start | bytes 131072 | tf_op jit(solution)/shard_map/all_to_all | solution.py:286
  245.6 11.1 %all-to-all-done.1 = bf16[128,2,128]{2,1,0:T(2,128)(2,1)S(1)} async-done(((bf16[128,2,128]{2,1,0:T(2,128)(2,1)}), bf16[128,2,128]{2,1,0:T(2,128)(2,1)S(1)}, u32[]{:S(2)}, u32[]{:S(2)}) %all-to-all-start.1) | async-done | bytes 65568 | tf_op jit(solution)/shard_map/all_to_all | solution.py:286
  259.4 3.9 %collective-permute-start.43 = (f32[8,128]{1,0:T(8,128)S(1)}, f32[8,128]{1,0:T(8,128)S(1)}, u32[]{:S(2)}, u32[]{:S(2)}) collective-permute-start(f32[8,128]{1,0:T(8,128)S(1)} %get-tuple-element.21), channel_id=1, source_target_pairs={{0,3},{1,0},{2,1},{3,2},{4,7},{5,4},{6,5},{7,6},{8,11},{9,8},{10,9... | collective-permute-start | bytes 12296 | tf_op jit(solution)/shard_map/ppermute | solution.py:30
  266.5 3.8 %collective-permute-done.44 = f32[8,128]{1,0:T(8,128)S(1)} collective-permute-done((f32[8,128]{1,0:T(8,128)S(1)}, f32[8,128]{1,0:T(8,128)S(1)}, u32[]{:S(2)}, u32[]{:S(2)}) %collective-permute-start.44) | collective-permute-done | bytes 4128 | tf_op jit(solution)/shard_map/ppermute | solution.py:30
  (148 shorter events, 86.9 us)
Async XLA Ops:
  2.8 70.1 %collective-permute-start.30 = (f32[8,128]{1,0:T(8,128)S(1)}, f32[8,128]{1,0:T(8,128)S(1)}, u32[]{:S(2)}, u32[]{:S(2)}) collective-permute-start(f32[8,128]{1,0:T(8,128)S(1)} %select_maximum_fusion), channel_id=1, source_target_pairs={{0,1},{1,2},{2,3},{3,0},{4,5},{5,6},{6,7},{7,4},{8,9},{9,10},{10,1... | collective-permute-start | bytes 12296 | tf_op jit(solution)/shard_map/ppermute | solution.py:30
  6.2 69.7 %collective-permute-start.31 = (f32[8,128]{1,0:T(8,128)S(1)}, f32[8,128]{1,0:T(8,128)S(1)}, u32[]{:S(2)}, u32[]{:S(2)}) collective-permute-start(f32[8,128]{1,0:T(8,128)S(1)} %select_maximum_fusion), channel_id=1, source_target_pairs={{0,3},{1,0},{2,1},{3,2},{4,7},{5,4},{6,5},{7,6},{8,11},{9,8},{10,9... | collective-permute-start | bytes 12296 | tf_op jit(solution)/shard_map/ppermute | solution.py:30
  14.9 78.3 %collective-permute-start.4 = (bf16[128,896]{1,0:T(8,128)(2,1)}, bf16[128,896]{1,0:T(8,128)(2,1)}, u32[]{:S(2)}, u32[]{:S(2)}) collective-permute-start(bf16[128,896]{1,0:T(8,128)(2,1)} %get-tuple-element.25), channel_id=1, source_target_pairs={{0,1},{1,2},{2,3},{3,0},{4,5},{5,6},{6,7},{7,4},{8,9},{9,10},{10,1... | collective-permute-start | bytes 688136 | tf_op jit(solution)/shard_map/ppermute | solution.py:30
  37.2 18.0 %collective-permute-start.11 = (bf16[168,512]{1,0:T(8,128)(2,1)S(1)}, bf16[168,512]{1,0:T(8,128)(2,1)S(1)}, u32[]{:S(2)}, u32[]{:S(2)}) collective-permute-start(bf16[168,512]{1,0:T(8,128)(2,1)S(1)} %pad_maximum_fusion), channel_id=1, source_target_pairs={{0,24},{8,32},{16,40},{24,48},{32,56},{40,0},{48,8},{56,16},{1,25}... | collective-permute-start | bytes 516104 | tf_op jit(solution)/shard_map/ppermute | solution.py:30
  45.2 10.0 %collective-permute-start.12 = (bf16[112,512]{1,0:T(8,128)(2,1)S(1)}, bf16[112,512]{1,0:T(8,128)(2,1)S(1)}, u32[]{:S(2)}, u32[]{:S(2)}) collective-permute-start(bf16[112,512]{1,0:T(8,128)(2,1)S(1)} %pad_maximum_fusion.1), channel_id=1, source_target_pairs={{0,40},{8,48},{16,56},{24,0},{32,8},{40,16},{48,24},{56,32},{1,41}... | collective-permute-start | bytes 344072 | tf_op jit(solution)/shard_map/ppermute | solution.py:30
  55.7 24.6 %collective-permute-start.13 = (bf16[448,512]{1,0:T(8,128)(2,1)S(1)}, bf16[448,512]{1,0:T(8,128)(2,1)S(1)}, u32[]{:S(2)}, u32[]{:S(2)}) collective-permute-start(bf16[448,512]{1,0:T(8,128)(2,1)S(1)} %constant_dynamic-slice_fusion.refs_0_), channel_id=1, source_target_pairs={{0,64},{64,128},{128,192},{192,256},{256,320},{320,384},{384,448},... | collective-permute-start | bytes 1376264 | tf_op jit(solution)/shard_map/ppermute | solution.py:30
  60.9 21.6 %collective-permute-start.14 = (bf16[448,512]{1,0:T(8,128)(2,1)S(1)}, bf16[448,512]{1,0:T(8,128)(2,1)S(1)}, u32[]{:S(2)}, u32[]{:S(2)}) collective-permute-start(bf16[448,512]{1,0:T(8,128)(2,1)S(1)} %constant_dynamic-slice_fusion.refs_0_), channel_id=1, source_target_pairs={{0,448},{64,0},{128,64},{192,128},{256,192},{320,256},{384,320},{4... | collective-permute-start | bytes 1376264 | tf_op jit(solution)/shard_map/ppermute | solution.py:30
  72.9 15.4 %collective-permute-start.32 = (f32[8,128]{1,0:T(8,128)S(1)}, f32[8,128]{1,0:T(8,128)S(1)}, u32[]{:S(2)}, u32[]{:S(2)}) collective-permute-start(f32[8,128]{1,0:T(8,128)S(1)} %select_maximum_fusion), channel_id=1, source_target_pairs={{0,2},{1,3},{2,0},{3,1},{4,6},{5,7},{6,4},{7,5},{8,10},{9,11},{10,... | collective-permute-start | bytes 12296 | tf_op jit(solution)/shard_map/ppermute | solution.py:30
  75.9 20.1 %collective-permute-start.5 = (bf16[128,896]{1,0:T(8,128)(2,1)}, bf16[128,896]{1,0:T(8,128)(2,1)}, u32[]{:S(2)}, u32[]{:S(2)}) collective-permute-start(bf16[128,896]{1,0:T(8,128)(2,1)} %get-tuple-element.27), channel_id=1, source_target_pairs={{0,2},{1,3},{2,0},{3,1},{4,6},{5,7},{6,4},{7,5},{8,10},{9,11},{10,... | collective-permute-start | bytes 688136 | tf_op jit(solution)/shard_map/ppermute | solution.py:30
  80.3 38.3 %collective-permute-start.15 = (bf16[448,512]{1,0:T(8,128)(2,1)S(1)}, bf16[448,512]{1,0:T(8,128)(2,1)S(1)}, u32[]{:S(2)}, u32[]{:S(2)}) collective-permute-start(bf16[448,512]{1,0:T(8,128)(2,1)S(1)} %collective-permute-done.13.refs_1_), channel_id=1, source_target_pairs={{0,64},{64,128},{128,192},{192,256},{256,320},{320,384},{384,448},... | collective-permute-start | bytes 1376264 | tf_op jit(solution)/shard_map/ppermute | solution.py:30
  82.5 38.1 %collective-permute-start.16 = (bf16[448,512]{1,0:T(8,128)(2,1)S(1)}, bf16[448,512]{1,0:T(8,128)(2,1)S(1)}, u32[]{:S(2)}, u32[]{:S(2)}) collective-permute-start(bf16[448,512]{1,0:T(8,128)(2,1)S(1)} %collective-permute-done.14.refs_2_), channel_id=1, source_target_pairs={{0,448},{64,0},{128,64},{192,128},{256,192},{320,256},{384,320},{4... | collective-permute-start | bytes 1376264 | tf_op jit(solution)/shard_map/ppermute | solution.py:30
  88.4 39.4 %collective-permute-start = (bf16[512,896]{1,0:T(8,128)(2,1)}, bf16[512,896]{1,0:T(8,128)(2,1)}, u32[]{:S(2)}, u32[]{:S(2)}) collective-permute-start(bf16[512,896]{1,0:T(8,128)(2,1)} %param.9), channel_id=1, source_target_pairs={{0,1},{1,2},{2,3},{3,0},{4,5},{5,6},{6,7},{7,4},{8,9},{9,10},{10,1... | collective-permute-start | bytes 2752520 | tf_op jit(solution)/shard_map/ppermute | solution.py:30
  93.2 37.6 %collective-permute-start.1 = (bf16[512,896]{1,0:T(8,128)(2,1)}, bf16[512,896]{1,0:T(8,128)(2,1)}, u32[]{:S(2)}, u32[]{:S(2)}) collective-permute-start(bf16[512,896]{1,0:T(8,128)(2,1)} %param.9), channel_id=1, source_target_pairs={{0,3},{1,0},{2,1},{3,2},{4,7},{5,4},{6,5},{7,6},{8,11},{9,8},{10,9... | collective-permute-start | bytes 2752520 | tf_op jit(solution)/shard_map/ppermute | solution.py:30
  96.0 20.7 %collective-permute-start.6 = (bf16[128,896]{1,0:T(8,128)(2,1)S(1)}, bf16[128,896]{1,0:T(8,128)(2,1)S(1)}, u32[]{:S(2)}, u32[]{:S(2)}) collective-permute-start(bf16[128,896]{1,0:T(8,128)(2,1)S(1)} %get-tuple-element.24), channel_id=1, source_target_pairs={{0,3},{1,0},{2,1},{3,2},{4,7},{5,4},{6,5},{7,6},{8,11},{9,8},{10,9... | collective-permute-start | bytes 688136 | tf_op jit(solution)/shard_map/ppermute | solution.py:30
  116.7 17.6 %collective-permute-start.21 = (bf16[448,512]{1,0:T(8,128)(2,1)S(1)}, bf16[448,512]{1,0:T(8,128)(2,1)S(1)}, u32[]{:S(2)}, u32[]{:S(2)}) collective-permute-start(bf16[448,512]{1,0:T(8,128)(2,1)S(1)} %constant_dynamic-slice_fusion.refs_0_), channel_id=1, source_target_pairs={{0,4},{4,0},{1,5},{5,1},{2,6},{6,2},{3,7},{7,3},{8,12},{12,8},{9,1... | collective-permute-start | bytes 1376264 | tf_op jit(solution)/shard_map/ppermute | solution.py:30
  118.6 18.2 %collective-permute-start.17 = (bf16[448,512]{1,0:T(8,128)(2,1)S(1)}, bf16[448,512]{1,0:T(8,128)(2,1)S(1)}, u32[]{:S(2)}, u32[]{:S(2)}) collective-permute-start(bf16[448,512]{1,0:T(8,128)(2,1)S(1)} %collective-permute-done.15.refs_3_), channel_id=1, source_target_pairs={{0,64},{64,128},{128,192},{192,256},{256,320},{320,384},{384,448},... | collective-permute-start | bytes 1376264 | tf_op jit(solution)/shard_map/ppermute | solution.py:30
  120.6 19.6 %collective-permute-start.18 = (bf16[448,512]{1,0:T(8,128)(2,1)S(1)}, bf16[448,512]{1,0:T(8,128)(2,1)S(1)}, u32[]{:S(2)}, u32[]{:S(2)}) collective-permute-start(bf16[448,512]{1,0:T(8,128)(2,1)S(1)} %collective-permute-done.16.refs_4_), channel_id=1, source_target_pairs={{0,448},{64,0},{128,64},{192,128},{256,192},{320,256},{384,320},{4... | collective-permute-start | bytes 1376264 | tf_op jit(solution)/shard_map/ppermute | solution.py:30
  127.8 18.7 %collective-permute-start.22 = (bf16[448,512]{1,0:T(8,128)(2,1)S(1)}, bf16[448,512]{1,0:T(8,128)(2,1)S(1)}, u32[]{:S(2)}, u32[]{:S(2)}) collective-permute-start(bf16[448,512]{1,0:T(8,128)(2,1)S(1)} %collective-permute-done.13.refs_1_), channel_id=1, source_target_pairs={{0,4},{4,0},{1,5},{5,1},{2,6},{6,2},{3,7},{7,3},{8,12},{12,8},{9,1... | collective-permute-start | bytes 1376264 | tf_op jit(solution)/shard_map/ppermute | solution.py:30
  130.8 18.2 %collective-permute-start.23 = (bf16[448,512]{1,0:T(8,128)(2,1)S(1)}, bf16[448,512]{1,0:T(8,128)(2,1)S(1)}, u32[]{:S(2)}, u32[]{:S(2)}) collective-permute-start(bf16[448,512]{1,0:T(8,128)(2,1)S(1)} %collective-permute-done.14.refs_2_), channel_id=1, source_target_pairs={{0,4},{4,0},{1,5},{5,1},{2,6},{6,2},{3,7},{7,3},{8,12},{12,8},{9,1... | collective-permute-start | bytes 1376264 | tf_op jit(solution)/shard_map/ppermute | solution.py:30
  134.3 16.6 %collective-permute-start.2 = (bf16[256,896]{1,0:T(8,128)(2,1)S(1)}, bf16[256,896]{1,0:T(8,128)(2,1)S(1)}, u32[]{:S(2)}, u32[]{:S(2)}) collective-permute-start(bf16[256,896]{1,0:T(8,128)(2,1)S(1)} %slice.57), channel_id=1, source_target_pairs={{0,1},{1,2},{2,3},{3,0},{4,5},{5,6},{6,7},{7,4},{8,9},{9,10},{10,1... | collective-permute-start | bytes 1376264 | tf_op jit(solution)/shard_map/ppermute | solution.py:30
  136.8 19.3 %collective-permute-start.3 = (bf16[256,896]{1,0:T(8,128)(2,1)S(1)}, bf16[256,896]{1,0:T(8,128)(2,1)S(1)}, u32[]{:S(2)}, u32[]{:S(2)}) collective-permute-start(bf16[256,896]{1,0:T(8,128)(2,1)S(1)} %slice.58), channel_id=1, source_target_pairs={{0,3},{1,0},{2,1},{3,2},{4,7},{5,4},{6,5},{7,6},{8,11},{9,8},{10,9... | collective-permute-start | bytes 1376264 | tf_op jit(solution)/shard_map/ppermute | solution.py:30
  140.2 17.8 %collective-permute-start.24 = (bf16[448,512]{1,0:T(8,128)(2,1)S(1)}, bf16[448,512]{1,0:T(8,128)(2,1)S(1)}, u32[]{:S(2)}, u32[]{:S(2)}) collective-permute-start(bf16[448,512]{1,0:T(8,128)(2,1)S(1)} %collective-permute-done.15.refs_3_), channel_id=1, source_target_pairs={{0,4},{4,0},{1,5},{5,1},{2,6},{6,2},{3,7},{7,3},{8,12},{12,8},{9,1... | collective-permute-start | bytes 1376264 | tf_op jit(solution)/shard_map/ppermute | solution.py:30
  146.5 19.9 %collective-permute-start.25 = (bf16[448,512]{1,0:T(8,128)(2,1)S(1)}, bf16[448,512]{1,0:T(8,128)(2,1)S(1)}, u32[]{:S(2)}, u32[]{:S(2)}) collective-permute-start(bf16[448,512]{1,0:T(8,128)(2,1)S(1)} %collective-permute-done.16.refs_4_), channel_id=1, source_target_pairs={{0,4},{4,0},{1,5},{5,1},{2,6},{6,2},{3,7},{7,3},{8,12},{12,8},{9,1... | collective-permute-start | bytes 1376264 | tf_op jit(solution)/shard_map/ppermute | solution.py:30
  149.0 12.3 %collective-permute-start.19 = (bf16[224,512]{1,0:T(8,128)(2,1)S(1)}, bf16[224,512]{1,0:T(8,128)(2,1)S(1)}, u32[]{:S(2)}, u32[]{:S(2)}) collective-permute-start(bf16[224,512]{1,0:T(8,128)(2,1)S(1)} %slice.61), channel_id=1, source_target_pairs={{0,64},{64,128},{128,192},{192,256},{256,320},{320,384},{384,448},... | collective-permute-start | bytes 688136 | tf_op jit(solution)/shard_map/ppermute | solution.py:30
  150.9 12.3 %collective-permute-start.20 = (bf16[224,512]{1,0:T(8,128)(2,1)S(1)}, bf16[224,512]{1,0:T(8,128)(2,1)S(1)}, u32[]{:S(2)}, u32[]{:S(2)}) collective-permute-start(bf16[224,512]{1,0:T(8,128)(2,1)S(1)} %slice.62), channel_id=1, source_target_pairs={{0,448},{64,0},{128,64},{192,128},{256,192},{320,256},{384,320},{4... | collective-permute-start | bytes 688136 | tf_op jit(solution)/shard_map/ppermute | solution.py:30
  156.0 10.6 %collective-permute-start.26 = (bf16[448,512]{1,0:T(8,128)(2,1)S(1)}, bf16[448,512]{1,0:T(8,128)(2,1)S(1)}, u32[]{:S(2)}, u32[]{:S(2)}) collective-permute-start(bf16[448,512]{1,0:T(8,128)(2,1)S(1)} %collective-permute-done.17.refs_5_), channel_id=1, source_target_pairs={{0,4},{4,0},{1,5},{5,1},{2,6},{6,2},{3,7},{7,3},{8,12},{12,8},{9,1... | collective-permute-start | bytes 1376264 | tf_op jit(solution)/shard_map/ppermute | solution.py:30
  174.2 10.9 %collective-permute-start.33 = (f32[8,128]{1,0:T(8,128)S(1)}, f32[8,128]{1,0:T(8,128)S(1)}, u32[]{:S(2)}, u32[]{:S(2)}) collective-permute-start(f32[8,128]{1,0:T(8,128)S(1)} %get-tuple-element.13.sq0), channel_id=1, source_target_pairs={{0,1},{1,2},{2,3},{3,0},{4,5},{5,6},{6,7},{7,4},{8,9},{9,10},{10,1... | collective-permute-start | bytes 12296 | tf_op jit(solution)/shard_map/ppermute | solution.py:30
  189.9 28.7 %all-to-all-start = ((bf16[128,2,896]{2,1,0:T(2,128)(2,1)}), bf16[128,2,896]{2,1,0:T(2,128)(2,1)S(1)}, u32[]{:S(2)}, u32[]{:S(2)}) async-start(bf16[128,2,896]{2,1,0:T(2,128)(2,1)} %reshape.80), calls=%async_computation | async-start | bytes 917504 | tf_op jit(solution)/shard_map/all_to_all | solution.py:265
  200.4 11.7 %collective-permute-start.39 = (f32[8,128]{1,0:T(8,128)S(1)}, f32[8,128]{1,0:T(8,128)S(1)}, u32[]{:S(2)}, u32[]{:S(2)}) collective-permute-start(f32[8,128]{1,0:T(8,128)S(1)} %get-tuple-element.19), channel_id=1, source_target_pairs={{0,1},{1,2},{2,3},{3,0},{4,5},{5,6},{6,7},{7,4},{8,9},{9,10},{10,1... | collective-permute-start | bytes 12296 | tf_op jit(solution)/shard_map/ppermute | solution.py:30
  220.0 11.4 %collective-permute-start.36 = (bf16[256,128]{1,0:T(8,128)(2,1)S(1)}, bf16[256,128]{1,0:T(8,128)(2,1)S(1)}, u32[]{:S(2)}, u32[]{:S(2)}) collective-permute-start(bf16[256,128]{1,0:T(8,128)(2,1)S(1)} %get-tuple-element.16), channel_id=1, source_target_pairs={{0,1},{1,2},{2,3},{3,0},{4,5},{5,6},{6,7},{7,4},{8,9},{9,10},{10,1... | collective-permute-start | bytes 196616 | tf_op jit(solution)/shard_map/ppermute | solution.py:30
  236.0 20.7 %all-to-all-start.1 = ((bf16[128,2,128]{2,1,0:T(2,128)(2,1)}), bf16[128,2,128]{2,1,0:T(2,128)(2,1)S(1)}, u32[]{:S(2)}, u32[]{:S(2)}) async-start(bf16[128,2,128]{2,1,0:T(2,128)(2,1)} %bitcast.12), calls=%async_computation.1 | async-start | bytes 131072 | tf_op jit(solution)/shard_map/all_to_all | solution.py:286
  257.5 9.0 %collective-permute-start.42 = (f32[8,128]{1,0:T(8,128)S(1)}, f32[8,128]{1,0:T(8,128)S(1)}, u32[]{:S(2)}, u32[]{:S(2)}) collective-permute-start(f32[8,128]{1,0:T(8,128)S(1)} %get-tuple-element.21), channel_id=1, source_target_pairs={{0,1},{1,2},{2,3},{3,0},{4,5},{5,6},{6,7},{7,4},{8,9},{9,10},{10,1... | collective-permute-start | bytes 12296 | tf_op jit(solution)/shard_map/ppermute | solution.py:30
  (23 other events, 298.4 us)

commit v2 on v1

v2 whole, which is shorter than its diff:
```python
import jax
import jax.numpy as jnp
from jax import lax
from jax.experimental import pallas as pl
from jax.experimental.pallas import tpu as pltpu
from jax.sharding import Mesh, PartitionSpec as P

DP = ("z", "y", "core")
ALL = ("z", "y", "core", "tensor")
SIZES = {"z": 8, "y": 8, "core": 2, "tensor": 4}
BF = jnp.bfloat16
F32 = jnp.float32
NT = (((1,), (1,)), ((), ()))
VMEM = pl.BlockSpec(memory_space=pltpu.VMEM)
TOK, QUARTER, HALF = 512, 896, 448
DOCS, SLOTS, MEMBERS, SHARE = 128, 256, 512, 128


def params():
    return pltpu.CompilerParams(vmem_limit_bytes=40 * 1024 * 1024)


def cost(flops, nbytes):
    return pl.CostEstimate(flops=flops, bytes_accessed=nbytes, transcendentals=0)


def shift(value, axis, step):
    size = SIZES[axis]
    return lax.ppermute(value, axis, [(i, (i + step) % size) for i in range(size)])


def spread(flip):
    pairs = []
    for z in range(8):
        for y in range(8):
            for core in range(2):
                for x in range(4):
                    source = ((z * 8 + y) * 2 + core) * 4 + x
                    target = (((2 * x + z % 2) * 8 + y) * 2 + (core ^ flip)) * 4 + z // 2
                    pairs.append((source, target))
    return pairs


def project_kernel(ctx, weight, res, hidden, squares, total):
    step = pl.program_id(0)
    half = lax.rem(step, 2)
    product = lax.dot_general(ctx[0], weight[...], NT, preferred_element_type=F32)

    @pl.when(step < 2)
    def _():
        total[half] = product

    @pl.when(step >= 2)
    def _():
        total[half] += product

    @pl.when(step == 7)
    def _():
        for pack in range(4):
            rows = pl.ds(pack * 128, 128)
            value = jnp.concatenate([total[0, rows, :], total[1, rows, :]], axis=1)
            value = value + res[rows, :].astype(F32)
            hidden[rows, :] = value
            sq = value * value
            part = sq[:, 0:128]
            for tile in range(1, 7):
                part = part + sq[:, tile * 128 : tile * 128 + 128]
            squares[pl.ds(pack, 1), :] = jnp.sum(part.T, axis=0, keepdims=True)
        squares[pl.ds(4, 4), :] = jnp.zeros((4, 128), F32)


def pool_kernel(hidden, gain, pool, inverse, total, slots, squares):
    scale = lax.rsqrt(total[...] / 3584.0 + 1e-06)
    summed = None
    for pack in range(4):
        rows = pl.ds(pack * 128, 128)
        column = jnp.broadcast_to(scale[pack : pack + 1, :], (128, 128)).T
        column = jnp.concatenate([column] * 7, axis=1)
        normed = (hidden[rows, :] * column * gain[...]).astype(BF)
        term = jnp.dot(pool[:, pack * 128 : pack * 128 + 128], normed, preferred_element_type=F32)
        summed = term if summed is None else summed + term
    pooled = summed * jnp.concatenate([inverse[...]] * 7, axis=1)
    slots[...] = pooled.astype(BF)
    sq = pooled * pooled
    part = sq[:, 0:128]
    for tile in range(1, 7):
        part = part + sq[:, tile * 128 : tile * 128 + 128]
    squares[...] = jnp.zeros_like(squares)
    for block in range(2):
        squares[pl.ds(block, 1), :] = jnp.sum(
            part[block * 128 : block * 128 + 128, :].T, axis=0, keepdims=True
        )


def dots_kernel(arrived, members, factor, out):
    for part in range(4):
        rows = pl.ds(part * SHARE, SHARE)
        dots = lax.dot_general(arrived[...], members[rows, :], NT, preferred_element_type=F32)
        out[:, part * SHARE : part * SHARE + SHARE] = (dots * factor[pl.ds(part, 1), :]).astype(BF)


def home_kernel(returned, pick, scale, live, scores, best):
    rows = jnp.dot(pick[...], returned[...], preferred_element_type=F32) * scale[...]
    scores[...] = rows
    masked = jnp.where(live[...] > 0.0, rows, -1000000000.0)
    best[...] = jnp.broadcast_to(jnp.max(masked.T, axis=0, keepdims=True), (8, 128))


def body(
    context,
    residual,
    out_weight,
    norm_gain,
    members,
    doc_lengths,
    doc_cluster,
    owner_map,
    member_counts,
):
    z, y = lax.axis_index("z"), lax.axis_index("y")
    core, x = lax.axis_index("core"), lax.axis_index("tensor")

    weight = out_weight.T
    keep = lax.ppermute(weight, ALL, spread(0))
    cross = lax.ppermute(weight, ALL, spread(1))
    block = jnp.concatenate(
        [jnp.where(core == 0, keep, cross), jnp.where(core == 0, cross, keep)], axis=0
    )
    context, residual, doc_lengths, block = lax.optimization_barrier(
        (context, residual, doc_lengths, block)
    )
    plane = lax.all_gather(block, ("z", "y"), axis=0, tiled=True)

    ctx_down, ctx_up = shift(context, "tensor", 1), shift(context, "tensor", -1)

    res_parts = [
        lax.dynamic_slice(residual, (0, lax.rem(x + step, 4) * QUARTER), (128, QUARTER))
        for step in range(4)
    ]
    res_recv = [
        res_parts[0],
        shift(res_parts[1], "tensor", 1),
        shift(res_parts[2], "tensor", 2),
        shift(res_parts[3], "tensor", 3),
    ]
    res = jnp.zeros((TOK, QUARTER), BF)
    for step in range(4):
        res = lax.dynamic_update_slice(res, res_recv[step], (lax.rem(x - step + 4, 4) * 128, 0))

    resident = members[0]
    resident_f = resident.astype(F32)
    partial_sq = jnp.sum(resident_f * resident_f, axis=-1).reshape(4, 128)
    lens_rows = jnp.zeros((4, 128), F32)
    lens_rows = lax.dynamic_update_slice(lens_rows, doc_lengths.astype(F32), (x, 0))
    small = lax.psum(jnp.concatenate([partial_sq, lens_rows], axis=0), "tensor")
    small, res = lax.optimization_barrier((small, res))
    member_sq, lens = small[:4], small[4:, :32]

    far_a = shift(ctx_down[: TOK // 2], "tensor", 1)
    far_b = shift(ctx_up[TOK // 2 :], "tensor", -1)
    ctx = jnp.zeros((4, TOK, QUARTER), BF)
    ctx = lax.dynamic_update_slice(ctx, context[None], (x, 0, 0))
    ctx = lax.dynamic_update_slice(ctx, ctx_down[None], (lax.rem(x + 3, 4), 0, 0))
    ctx = lax.dynamic_update_slice(ctx, ctx_up[None], (lax.rem(x + 1, 4), 0, 0))
    ctx = lax.dynamic_update_slice(ctx, far_a[None], (lax.rem(x + 2, 4), 0, 0))
    ctx = lax.dynamic_update_slice(ctx, far_b[None], (lax.rem(x + 2, 4), TOK // 2, 0))

    cluster_ids = jnp.arange(owner_map.shape[0], dtype=jnp.int32)
    matches = doc_cluster[:, 0][:, None] == cluster_ids[None, :]
    doc_owner = jnp.sum(jnp.where(matches, owner_map[None, :], 0), axis=1)
    doc_members = jnp.sum(jnp.where(matches, member_counts[None, :], 0), axis=1)
    doc_order = jnp.arange(DOCS, dtype=jnp.int32)
    same_owner = (doc_owner[:, None] == doc_owner[None, :]) & (
        doc_order[:, None] > doc_order[None, :]
    )
    doc_slot = doc_owner * 2 + jnp.sum(same_owner.astype(jnp.int32), axis=1)
    slot_ids = jnp.arange(SLOTS, dtype=jnp.int32)
    select = slot_ids[:, None] == doc_slot[None, :]
    wide_ids = jnp.arange(4 * SLOTS, dtype=jnp.int32)
    wide_ids = lax.div(wide_ids, 8) * 2 + lax.rem(wide_ids, 2)
    pick = (doc_slot[:, None] == wide_ids[None, :]).astype(BF)
    lens_int = lens.astype(jnp.int32)
    ends = jnp.cumsum(lens_int, axis=1)
    offsets = 128 * jnp.arange(4, dtype=jnp.int32)[:, None]
    doc_begin = (ends - lens_int + offsets).reshape(DOCS)
    doc_end = (ends + offsets).reshape(DOCS)
    tokens = jnp.arange(TOK, dtype=jnp.int32)
    inside = (tokens[None, :] >= doc_begin[:, None]) & (tokens[None, :] < doc_end[:, None])
    pool = jnp.dot(select.astype(BF), inside.astype(BF), preferred_element_type=F32).astype(BF)
    slot_len = jnp.sum(jnp.where(select, lens.reshape(DOCS)[None, :], 0.0), axis=1)
    inverse = jnp.broadcast_to((1.0 / jnp.maximum(slot_len, 1.0))[:, None], (SLOTS, 128))
    columns = x * SHARE + jnp.arange(SHARE, dtype=jnp.int32)
    live = (columns[None, :] < doc_members[:, None]).astype(F32)

    own_dp = (z * 8 + y) * 2 + core
    own_count = jnp.sum(jnp.where(owner_map == own_dp, member_counts, 0))
    member_ids = jnp.arange(MEMBERS, dtype=jnp.int32).reshape(4, 128)
    factor = jnp.where(member_ids < own_count, lax.rsqrt(member_sq / 3584.0 + 1e-06), 0.0)

    hidden, squares = pl.pallas_call(
        project_kernel,
        out_shape=(
            jax.ShapeDtypeStruct((TOK, QUARTER), F32),
            jax.ShapeDtypeStruct((8, 128), F32),
        ),
        grid=(8,),
        in_specs=[
            pl.BlockSpec((1, TOK, QUARTER), lambda i: (lax.div(i, 2), 0, 0)),
            pl.BlockSpec((HALF, QUARTER), lambda i: (i, 0)),
            pl.BlockSpec((TOK, QUARTER), lambda i: (0, 0)),
        ],
        out_specs=(
            pl.BlockSpec((TOK, QUARTER), lambda i: (0, 0)),
            pl.BlockSpec((8, 128), lambda i: (0, 0)),
        ),
        scratch_shapes=[pltpu.VMEM((2, TOK, HALF), F32)],
        compiler_params=params(),
        cost_estimate=cost(2 * TOK * QUARTER * 3584, 13_000_000),
        name="project",
    )(ctx, plane, res)

    slots, doc_sq = pl.pallas_call(
        pool_kernel,
        out_shape=(
            jax.ShapeDtypeStruct((SLOTS, QUARTER), BF),
            jax.ShapeDtypeStruct((8, 128), F32),
        ),
        in_specs=[VMEM] * 5,
        out_specs=(VMEM, VMEM),
        compiler_params=params(),
        cost_estimate=cost(2 * SLOTS * TOK * QUARTER, 3_000_000),
        name="pool",
    )(hidden, gain_of(norm_gain, x), pool, inverse, lax.psum(squares, "tensor"))

    arrived = lax.all_to_all(
        slots.reshape(DOCS, 2, QUARTER), DP, split_axis=0, concat_axis=0, tiled=True
    ).reshape(SLOTS, QUARTER)

    slot_sq = lax.psum(doc_sq, "tensor")[:2].reshape(SLOTS)
    doc_total = jnp.sum(jnp.where(select, slot_sq[:, None], 0.0), axis=0)
    scale = jnp.broadcast_to(lax.rsqrt(doc_total + 1e-06)[:, None], (DOCS, SHARE))

    partial = pl.pallas_call(
        dots_kernel,
        out_shape=jax.ShapeDtypeStruct((SLOTS, MEMBERS), BF),
        in_specs=[VMEM] * 3,
        out_specs=VMEM,
        compiler_params=params(),
        cost_estimate=cost(2 * SLOTS * MEMBERS * QUARTER, 2_000_000),
        name="dots",
    )(arrived, resident, factor)

    partial = partial.reshape(DOCS, 2, 4, SHARE).transpose(0, 2, 1, 3).reshape(4 * DOCS, 2, SHARE)
    returned = lax.all_to_all(partial, ALL, split_axis=0, concat_axis=0, tiled=True)
    returned = returned.reshape(4 * SLOTS, SHARE)
    scores, best = pl.pallas_call(
        home_kernel,
        out_shape=(
            jax.ShapeDtypeStruct((DOCS, SHARE), F32),
            jax.ShapeDtypeStruct((8, 128), F32),
        ),
        in_specs=[VMEM] * 4,
        out_specs=(VMEM, VMEM),
        compiler_params=params(),
        cost_estimate=cost(2 * SLOTS * DOCS * SHARE, 400_000),
        name="home",
    )(returned, pick, scale, live)
    return scores, lax.pmax(best[0], "tensor")


def gain_of(norm_gain, x):
    return lax.dynamic_slice(norm_gain, (x * QUARTER,), (QUARTER,)).reshape(1, QUARTER)


def solution(mesh):
    split = Mesh(mesh.devices.reshape(8, 8, 2, 4), ALL)
    in_specs = (
        P(DP, "tensor"),
        P(ALL, None),
        P("tensor", DP),
        P(),
        P(DP, None, "tensor"),
        P(ALL, None),
        P(DP, None),
        P(),
        P(),
    )
    out_specs = (P(DP, "tensor"), P(DP))
    return jax.shard_map(body, mesh=split, in_specs=in_specs, out_specs=out_specs, check_vma=False)
```

time: 273 us -> 221 us (0.81)
  starting transfers between devices: 176 us -> 56.4 us
  blocking collectives: 0 us -> 48.8 us
  between operations: 1.58 us -> 14.5 us
  waiting for transfers between devices: 57.2 us -> 65.2 us
    ppermute x43 -> x7, starting transfers between devices: 150 us -> 27.9 us  [shift(): lax.ppermute(value, axis, [(i, (i + step) % size) for i in range(size)])]
    psum x0 -> x3, blocking collectives: none -> 38.1 us  [the longest x1 19.3 us: body(): small = lax.psum(jnp.concatenate([partial_sq, lens_rows], axis=0), 'tensor')]
    ppermute x43 -> x7, waiting for transfers between devices: 40 us -> 6.69 us  [shift(): lax.ppermute(value, axis, [(i, (i + step) % size) for i in range(size)])]
    all_gather x0 -> x1, waiting for transfers between devices: none -> 28 us  [body(): plane = lax.all_gather(block, ('z', 'y'), axis=0, tiled=True)]
    pmax x0 -> x1, blocking collectives: none -> 10.6 us  [body(): return (scores, lax.pmax(best[0], 'tensor'))]
    ppermute x2, waiting for transfers between devices: 2.04 us -> 8.37 us  [the longest x1 7.95 us: body(): cross = lax.ppermute(weight, ALL, spread(1))]
    all_to_all x1, waiting for transfers between devices: 11.1 us -> 15.5 us  [body(): lax.all_to_all(partial, ALL, split_axis=0, concat_axis=0, tiled=True)]
    unnamed x16 -> x12, local copies, waits for them, and re-layouts: 0.04 us -> 2.85 us
  transfers between devices with their start and end apart: 47 -> 12, of which waited for: 12 -> 7; matrix products, arithmetic and copies ran while one was open for 8% -> 8% of each run, Pallas kernels for 0% -> 0%
where the time goes in v2:
time: 221 us; the launch traced here: 220 us
  waiting for transfers between devices  65.2 us (30%)
  starting transfers between devices  56.4 us (26%)
  blocking collectives  48.8 us (22%)
  local copies, waits for them, and re-layouts  17.6 us (8%)
  between operations  14.5 us (7%)
  Pallas kernels  11.7 us (5%)
  other arithmetic  5.27 us (2%)
    all_gather x1, waiting for transfers between devices, body(): plane = lax.all_gather(block, ('z', 'y'), axis=0, tiled=True)  28 us
    ppermute x7, starting transfers between devices, shift(): lax.ppermute(value, axis, [(i, (i + step) % size) for i in range(size)])  27.9 us
    psum x1, blocking collectives, body(): small = lax.psum(jnp.concatenate([partial_sq, lens_rows], axis=0), 'tensor')  19.3 us
    all_to_all x1, waiting for transfers between devices, body(): lax.all_to_all(partial, ALL, split_axis=0, concat_axis=0, tiled=True)  15.5 us
    all_to_all x1, starting transfers between devices, body(): lax.all_to_all(partial, ALL, split_axis=0, concat_axis=0, tiled=True)  10.6 us
    pmax x1, blocking collectives, body(): return (scores, lax.pmax(best[0], 'tensor'))  10.6 us
    psum x1, blocking collectives, body(): slot_sq = lax.psum(doc_sq, 'tensor')[:2].reshape(SLOTS)  10.1 us
    all_to_all x1, starting transfers between devices, body(): lax.all_to_all(slots.reshape(DOCS, 2, QUARTER), DP, split_axis=0, concat_...  9.89 us
  transfers between devices with their start and end apart: 12, of which 7 were waited for; matrix products, arithmetic and copies ran while one was open for 8% of the time, Pallas kernels for 0%

profile of v2, /device:TPU:2, one launch (start us, length us, event | category | flops | bytes accessed | tf_op | source)
XLA Modules:
  0.0 219.7 jit_solution(4302111282947825824)
XLA Ops:
  7.2 6.1 %collective-permute-start = (bf16[28,896]{1,0:T(8,128)(2,1)}, bf16[28,896]{1,0:T(8,128)(2,1)S(1)}, u32[]{:S(2)}, u32[]{:S(2)}) collective-permute-start(bf16[28,896]{1,0:T(8,128)(2,1)} %bitcast.27), channel_id=1, source_target_pairs={{0,0},{1,128},{2,256},{3,384},{4,4},{5,132},{6,260},{7,388},{8,8},... | collective-permute-start | bytes 150536 | tf_op jit(solution)/shard_map/ppermute | solution.py:124
  13.3 1.9 collective-permute-start.1
  15.6 8.0 %collective-permute-done.1 = bf16[28,896]{1,0:T(8,128)(2,1)S(1)} collective-permute-done((bf16[28,896]{1,0:T(8,128)(2,1)}, bf16[28,896]{1,0:T(8,128)(2,1)S(1)}, u32[]{:S(2)}, u32[]{:S(2)}) %collective-permute-start.1) | collective-permute-done | bytes 50208 | tf_op jit(solution)/shard_map/ppermute | solution.py:125
  26.2 1.5 multiply_reduce_fusion
  27.7 10.3 %collective-permute-start.2 = (bf16[512,896]{1,0:T(8,128)(2,1)}, bf16[512,896]{1,0:T(8,128)(2,1)S(1)}, u32[]{:S(2)}, u32[]{:S(2)}) collective-permute-start(bf16[512,896]{1,0:T(8,128)(2,1)} %param.9), channel_id=1, source_target_pairs={{0,1},{1,2},{2,3},{3,0},{4,5},{5,6},{6,7},{7,4},{8,9},{9,10},{10,1... | collective-permute-start | bytes 2752520 | tf_op jit(solution)/shard_map/ppermute | solution.py:29
  38.0 1.9 collective-permute-start.3
  40.0 1.4 constant_dynamic-slice_fusion
  41.4 3.9 %collective-permute-start.6 = (bf16[128,896]{1,0:T(8,128)(2,1)S(1)}, bf16[128,896]{1,0:T(8,128)(2,1)}, u32[]{:S(2)}, u32[]{:S(2)}) collective-permute-start(bf16[128,896]{1,0:T(8,128)(2,1)S(1)} %get-tuple-element.30), channel_id=1, source_target_pairs={{0,1},{1,2},{2,3},{3,0},{4,5},{5,6},{6,7},{7,4},{8,9},{9,10},{10,1... | collective-permute-start | bytes 688136 | tf_op jit(solution)/shard_map/ppermute | solution.py:29
  45.3 1.9 collective-permute-start.7
  47.3 4.0 %collective-permute-start.8 = (bf16[128,896]{1,0:T(8,128)(2,1)S(1)}, bf16[128,896]{1,0:T(8,128)(2,1)}, u32[]{:S(2)}, u32[]{:S(2)}) collective-permute-start(bf16[128,896]{1,0:T(8,128)(2,1)S(1)} %get-tuple-element.28), channel_id=1, source_target_pairs={{0,3},{1,0},{2,1},{3,2},{4,7},{5,4},{6,5},{7,6},{8,11},{9,8},{10,9... | collective-permute-start | bytes 688136 | tf_op jit(solution)/shard_map/ppermute | solution.py:29
  51.2 2.1 broadcast_in_dim.102
  53.4 1.0 bitcast_dynamic-update-slice_fusion.2
  54.5 19.3 %psum.21 = f32[8,128]{1,0:T(8,128)S(1)} all-reduce(f32[8,128]{1,0:T(8,128)S(1)} %pad_maximum_fusion.1), channel_id=1, replica_groups=mesh['z'=8,'y'=8,'core'=2,'tensor'=4] {'tensor'}, use_global_device_ids=true, to_apply=%region_1.2 | all-reduce | flops 1024 | bytes 8192 | tf_op jit(solution)/shard_map/psum | solution.py:155
  73.8 1.0 constant_dynamic-update-slice_fusion.2
  74.8 1.0 constant_dynamic-update-slice_fusion.1
  75.8 1.0 constant_dynamic-update-slice_fusion.res
  77.8 3.6 %collective-permute-start.4 = (bf16[256,896]{1,0:T(8,128)(2,1)S(1)}, bf16[256,896]{1,0:T(8,128)(2,1)S(1)}, u32[]{:S(2)}, u32[]{:S(2)}) collective-permute-start(bf16[256,896]{1,0:T(8,128)(2,1)S(1)} %slice.24), channel_id=1, source_target_pairs={{0,1},{1,2},{2,3},{3,0},{4,5},{5,6},{6,7},{7,4},{8,9},{9,10},{10,1... | collective-permute-start | bytes 1376264 | tf_op jit(solution)/shard_map/ppermute | solution.py:29
  81.5 2.2 %collective-permute-start.5 = (bf16[256,896]{1,0:T(8,128)(2,1)S(1)}, bf16[256,896]{1,0:T(8,128)(2,1)S(1)}, u32[]{:S(2)}, u32[]{:S(2)}) collective-permute-start(bf16[256,896]{1,0:T(8,128)(2,1)S(1)} %slice.25), channel_id=1, source_target_pairs={{0,3},{1,0},{2,1},{3,2},{4,7},{5,4},{6,5},{7,6},{8,11},{9,8},{10,9... | collective-permute-start | bytes 1376264 | tf_op jit(solution)/shard_map/ppermute | solution.py:29
  83.8 1.0 bitcast_dynamic-update-slice_fusion.1
  84.8 1.1 bitcast_dynamic-update-slice_fusion
  85.9 4.5 %collective-permute-done.4 = bf16[256,896]{1,0:T(8,128)(2,1)S(1)} collective-permute-done((bf16[256,896]{1,0:T(8,128)(2,1)S(1)}, bf16[256,896]{1,0:T(8,128)(2,1)S(1)}, u32[]{:S(2)}, u32[]{:S(2)}) %collective-permute-start.4) | collective-permute-done | bytes 458784 | tf_op jit(solution)/shard_map/ppermute | solution.py:29
  91.2 2.2 collective-permute-done.5
  94.2 28.0 %all-gather.2.cloned.1.call-done.weight = bf16[3584,896]{1,0:T(8,128)(2,1)} async-done(((bf16[56,896]{1,0:T(8,128)(2,1)}), bf16[3584,896]{1,0:T(8,128)(2,1)}) %all-gather.2.cloned.1.call-update) | async-done | bytes 6422544 | tf_op jit(solution)/shard_map/all_gather | solution.py:132
  122.2 2.8 %copy-done.1 = bf16[3584,896]{1,0:T(8,128)(2,1)S(1)} copy-done((bf16[3584,896]{1,0:T(8,128)(2,1)S(1)}, bf16[3584,896]{1,0:T(8,128)(2,1)}, u32[]{:S(2)}) %copy-start.1) | copy-done | bytes 6422552
  125.0 9.4 %project.1 = (f32[512,896]{1,0:T(8,128)S(1)}, f32[8,128]{1,0:T(8,128)S(1)}) custom-call(bf16[4,512,896]{2,1,0:T(8,128)(2,1)} %bitcast_dynamic-update-slice_fusion.3.ctx, bf16[3584,896]{1,0:T(8,128)(2,1)S(1)} %copy-done.1, bf16[512,896]{1,0:T(8,128)(2,1)S(1)} %constant_dynamic-update-slice_fusion.res), custom_call_target="tpu_custom_call" | custom-call | flops 3288334336 | bytes 13000000 | tf_op jit(solution)/shard_map/project/pallas_call | solution.py:200
  134.5 8.7 %psum.22.total = f32[8,128]{1,0:T(8,128)S(1)} all-reduce(f32[8,128]{1,0:T(8,128)S(1)} %get-tuple-element.21), channel_id=1, replica_groups=mesh['z'=8,'y'=8,'core'=2,'tensor'=4] {'tensor'}, use_global_device_ids=true, to_apply=%region_6.7 | all-reduce | flops 1024 | bytes 8192 | tf_op jit(solution)/shard_map/psum | solution.py:233
  145.1 9.9 %all-to-all-start = ((bf16[128,2,896]{2,1,0:T(2,128)(2,1)}), bf16[128,2,896]{2,1,0:T(2,128)(2,1)S(1)}, u32[]{:S(2)}, u32[]{:S(2)}) async-start(bf16[128,2,896]{2,1,0:T(2,128)(2,1)} %reshape.91), calls=%async_computation | async-start | bytes 917504 | tf_op jit(solution)/shard_map/all_to_all | solution.py:235
  156.5 10.1 %psum.23 = f32[8,128]{1,0:T(8,128)S(1)} all-reduce(f32[8,128]{1,0:T(8,128)S(1)} %get-tuple-element.23), channel_id=1, replica_groups=mesh['z'=8,'y'=8,'core'=2,'tensor'=4] {'tensor'}, use_global_device_ids=true, to_apply=%region_8.9 | all-reduce | flops 1024 | bytes 8192 | tf_op jit(solution)/shard_map/psum | solution.py:239
  166.7 6.6 %all-to-all-done = bf16[128,2,896]{2,1,0:T(2,128)(2,1)S(1)} async-done(((bf16[128,2,896]{2,1,0:T(2,128)(2,1)}), bf16[128,2,896]{2,1,0:T(2,128)(2,1)S(1)}, u32[]{:S(2)}, u32[]{:S(2)}) %all-to-all-start) | async-done | bytes 458784 | tf_op jit(solution)/shard_map/all_to_all | solution.py:235
  175.1 10.6 %all-to-all-start.1 = ((bf16[512,2,128]{2,1,0:T(2,128)(2,1)}), bf16[512,2,128]{2,1,0:T(2,128)(2,1)S(1)}, u32[]{:S(2)}, u32[]{:S(2)}) async-start(bf16[512,2,128]{2,1,0:T(2,128)(2,1)} %bitcast.10), calls=%async_computation.1 | async-start | bytes 524288 | tf_op jit(solution)/shard_map/all_to_all | solution.py:254
  185.9 15.5 %all-to-all-done.1 = bf16[512,2,128]{2,1,0:T(2,128)(2,1)S(1)} async-done(((bf16[512,2,128]{2,1,0:T(2,128)(2,1)}), bf16[512,2,128]{2,1,0:T(2,128)(2,1)S(1)}, u32[]{:S(2)}, u32[]{:S(2)}) %all-to-all-start.1) | async-done | bytes 262176 | tf_op jit(solution)/shard_map/all_to_all | solution.py:254
  202.3 10.6 %pmax.7 = f32[128]{0:T(128)} all-reduce(f32[128]{0:T(128)S(1)} %slice_bitcast_fusion.1), channel_id=1, replica_groups=mesh['z'=8,'y'=8,'core'=2,'tensor'=4] {'tensor'}, use_global_device_ids=true, to_apply=%region_11.12 | all-reduce | flops 128 | bytes 1024 | tf_op jit(solution)/shard_map/pmax | solution.py:268
  (64 shorter events, 12.1 us)
Async XLA Ops:
  7.2 115.0 %all-gather.2.cloned.1.call-start = ((), (), s32[]{:S(2)}) async-start(), calls=%async_computation.2 | async-start | bytes 6522880 | tf_op jit(solution)/shard_map/all_gather | solution.py:132
  7.2 8.4 %collective-permute-start = (bf16[28,896]{1,0:T(8,128)(2,1)}, bf16[28,896]{1,0:T(8,128)(2,1)S(1)}, u32[]{:S(2)}, u32[]{:S(2)}) collective-permute-start(bf16[28,896]{1,0:T(8,128)(2,1)} %bitcast.27), channel_id=1, source_target_pairs={{0,0},{1,128},{2,256},{3,384},{4,4},{5,132},{6,260},{7,388},{8,8},... | collective-permute-start | bytes 150536 | tf_op jit(solution)/shard_map/ppermute | solution.py:124
  13.3 10.3 %collective-permute-start.1 = (bf16[28,896]{1,0:T(8,128)(2,1)}, bf16[28,896]{1,0:T(8,128)(2,1)S(1)}, u32[]{:S(2)}, u32[]{:S(2)}) collective-permute-start(bf16[28,896]{1,0:T(8,128)(2,1)} %bitcast.28), channel_id=1, source_target_pairs={{0,4},{1,132},{2,260},{3,388},{4,0},{5,128},{6,256},{7,384},{8,12}... | collective-permute-start | bytes 150536 | tf_op jit(solution)/shard_map/ppermute | solution.py:125
  26.2 27.2 %copy-start.2 = (bf16[512,896]{1,0:T(8,128)(2,1)S(1)}, bf16[512,896]{1,0:T(8,128)(2,1)}, u32[]{:S(2)}) copy-start(bf16[512,896]{1,0:T(8,128)(2,1)} %param.9) | copy-start | bytes 2752516
  27.7 50.1 %collective-permute-start.2 = (bf16[512,896]{1,0:T(8,128)(2,1)}, bf16[512,896]{1,0:T(8,128)(2,1)S(1)}, u32[]{:S(2)}, u32[]{:S(2)}) collective-permute-start(bf16[512,896]{1,0:T(8,128)(2,1)} %param.9), channel_id=1, source_target_pairs={{0,1},{1,2},{2,3},{3,0},{4,5},{5,6},{6,7},{7,4},{8,9},{9,10},{10,1... | collective-permute-start | bytes 2752520 | tf_op jit(solution)/shard_map/ppermute | solution.py:29
  38.0 43.5 %collective-permute-start.3 = (bf16[512,896]{1,0:T(8,128)(2,1)}, bf16[512,896]{1,0:T(8,128)(2,1)S(1)}, u32[]{:S(2)}, u32[]{:S(2)}) collective-permute-start(bf16[512,896]{1,0:T(8,128)(2,1)} %param.9), channel_id=1, source_target_pairs={{0,3},{1,0},{2,1},{3,2},{4,7},{5,4},{6,5},{7,6},{8,11},{9,8},{10,9... | collective-permute-start | bytes 2752520 | tf_op jit(solution)/shard_map/ppermute | solution.py:29
  40.0 14.4 %copy-start.5 = (s32[1,32]{1,0:T(1,128)S(1)}, s32[1,32]{1,0:T(1,128)}, u32[]{:S(2)}) copy-start(s32[1,32]{1,0:T(1,128)} %param.14) | copy-start | bytes 388
  41.4 32.4 %collective-permute-start.6 = (bf16[128,896]{1,0:T(8,128)(2,1)S(1)}, bf16[128,896]{1,0:T(8,128)(2,1)}, u32[]{:S(2)}, u32[]{:S(2)}) collective-permute-start(bf16[128,896]{1,0:T(8,128)(2,1)S(1)} %get-tuple-element.30), channel_id=1, source_target_pairs={{0,1},{1,2},{2,3},{3,0},{4,5},{5,6},{6,7},{7,4},{8,9},{9,10},{10,1... | collective-permute-start | bytes 688136 | tf_op jit(solution)/shard_map/ppermute | solution.py:29
  45.3 29.5 %collective-permute-start.7 = (bf16[128,896]{1,0:T(8,128)(2,1)S(1)}, bf16[128,896]{1,0:T(8,128)(2,1)}, u32[]{:S(2)}, u32[]{:S(2)}) collective-permute-start(bf16[128,896]{1,0:T(8,128)(2,1)S(1)} %get-tuple-element.29), channel_id=1, source_target_pairs={{0,2},{1,3},{2,0},{3,1},{4,6},{5,7},{6,4},{7,5},{8,10},{9,11},{10,... | collective-permute-start | bytes 688136 | tf_op jit(solution)/shard_map/ppermute | solution.py:29
  47.3 28.5 %collective-permute-start.8 = (bf16[128,896]{1,0:T(8,128)(2,1)S(1)}, bf16[128,896]{1,0:T(8,128)(2,1)}, u32[]{:S(2)}, u32[]{:S(2)}) collective-permute-start(bf16[128,896]{1,0:T(8,128)(2,1)S(1)} %get-tuple-element.28), channel_id=1, source_target_pairs={{0,3},{1,0},{2,1},{3,2},{4,7},{5,4},{6,5},{7,6},{8,11},{9,8},{10,9... | collective-permute-start | bytes 688136 | tf_op jit(solution)/shard_map/ppermute | solution.py:29
  77.8 12.5 %collective-permute-start.4 = (bf16[256,896]{1,0:T(8,128)(2,1)S(1)}, bf16[256,896]{1,0:T(8,128)(2,1)S(1)}, u32[]{:S(2)}, u32[]{:S(2)}) collective-permute-start(bf16[256,896]{1,0:T(8,128)(2,1)S(1)} %slice.24), channel_id=1, source_target_pairs={{0,1},{1,2},{2,3},{3,0},{4,5},{5,6},{6,7},{7,4},{8,9},{9,10},{10,1... | collective-permute-start | bytes 1376264 | tf_op jit(solution)/shard_map/ppermute | solution.py:29
  81.5 11.9 %collective-permute-start.5 = (bf16[256,896]{1,0:T(8,128)(2,1)S(1)}, bf16[256,896]{1,0:T(8,128)(2,1)S(1)}, u32[]{:S(2)}, u32[]{:S(2)}) collective-permute-start(bf16[256,896]{1,0:T(8,128)(2,1)S(1)} %slice.25), channel_id=1, source_target_pairs={{0,3},{1,0},{2,1},{3,2},{4,7},{5,4},{6,5},{7,6},{8,11},{9,8},{10,9... | collective-permute-start | bytes 1376264 | tf_op jit(solution)/shard_map/ppermute | solution.py:29
  122.2 2.8 %copy-start.1 = (bf16[3584,896]{1,0:T(8,128)(2,1)S(1)}, bf16[3584,896]{1,0:T(8,128)(2,1)}, u32[]{:S(2)}) copy-start(bf16[3584,896]{1,0:T(8,128)(2,1)} %all-gather.2.cloned.1.call-done.weight) | copy-start | bytes 19267588
  134.5 20.6 %copy-start.3 = (s32[128]{0:T(128)S(1)}, s32[128]{0:T(128)}, u32[]{:S(2)}) copy-start(s32[128]{0:T(128)} %param.17) | copy-start | bytes 1540
  134.5 20.6 %copy-start.4 = (s32[128]{0:T(128)S(1)}, s32[128]{0:T(128)}, u32[]{:S(2)}) copy-start(s32[128]{0:T(128)} %param.16) | copy-start | bytes 1540
  134.5 39.0 %copy-start = (bf16[1,512,896]{2,1,0:T(8,128)(2,1)S(1)}, bf16[1,512,896]{2,1,0:T(8,128)(2,1)}, u32[]{:S(2)}) copy-start(bf16[1,512,896]{2,1,0:T(8,128)(2,1)} %param.13) | copy-start | bytes 2752516
  145.1 28.2 %all-to-all-start = ((bf16[128,2,896]{2,1,0:T(2,128)(2,1)}), bf16[128,2,896]{2,1,0:T(2,128)(2,1)S(1)}, u32[]{:S(2)}, u32[]{:S(2)}) async-start(bf16[128,2,896]{2,1,0:T(2,128)(2,1)} %reshape.91), calls=%async_computation | async-start | bytes 917504 | tf_op jit(solution)/shard_map/all_to_all | solution.py:235
  175.1 26.2 %all-to-all-start.1 = ((bf16[512,2,128]{2,1,0:T(2,128)(2,1)}), bf16[512,2,128]{2,1,0:T(2,128)(2,1)S(1)}, u32[]{:S(2)}, u32[]{:S(2)}) async-start(bf16[512,2,128]{2,1,0:T(2,128)(2,1)} %bitcast.10), calls=%async_computation.1 | async-start | bytes 524288 | tf_op jit(solution)/shard_map/all_to_all | solution.py:254
Sparse Core Ops, SparseCore 0:
  24.4 97.7 all-gather.1

commit v3 on v2

--- a/solution.py
+++ b/solution.py
@@ -7,41 +7,102 @@
 
 DP = ("z", "y", "core")
 ALL = ("z", "y", "core", "tensor")
-SIZES = {"z": 8, "y": 8, "core": 2, "tensor": 4}
 BF = jnp.bfloat16
 F32 = jnp.float32
 NT = (((1,), (1,)), ((), ()))
+SMEM = pl.BlockSpec(memory_space=pltpu.SMEM)
 VMEM = pl.BlockSpec(memory_space=pltpu.VMEM)
-TOK, QUARTER, HALF = 512, 896, 448
+TOK, QUARTER, HALF, WINDOW, OFFSET = 512, 896, 448, 512, 384
 DOCS, SLOTS, MEMBERS, SHARE = 128, 256, 512, 128
 
 
 def params():
-    return pltpu.CompilerParams(vmem_limit_bytes=40 * 1024 * 1024)
+    return pltpu.CompilerParams(vmem_limit_bytes=20 * 1024 * 1024)
 
 
 def cost(flops, nbytes):
     return pl.CostEstimate(flops=flops, bytes_accessed=nbytes, transcendentals=0)
 
 
-def shift(value, axis, step):
-    size = SIZES[axis]
-    return lax.ppermute(value, axis, [(i, (i + step) % size) for i in range(size)])
+def device(z, y, core, x):
+    return ((z * 8 + y) * 2 + core) * 4 + x
+
+
+def placed(core, ring, line):
+    return (ring, line) if core == 0 else (line, ring)
+
+
+def grid():
+    return [(z, y, c, x) for z in range(8) for y in range(8) for c in range(2) for x in range(4)]
 
 
 def spread(flip):
     pairs = []
-    for z in range(8):
-        for y in range(8):
-            for core in range(2):
-                for x in range(4):
-                    source = ((z * 8 + y) * 2 + core) * 4 + x
-                    target = (((2 * x + z % 2) * 8 + y) * 2 + (core ^ flip)) * 4 + z // 2
-                    pairs.append((source, target))
+    for z, y, core, x in grid():
+        to = core ^ flip
+        to_z, to_y = placed(to, 2 * x + z % 2, y)
+        pairs.append((device(z, y, core, x), device(to_z, to_y, to, z // 2)))
     return pairs
 
 
-def project_kernel(ctx, weight, res, hidden, squares, total):
+def groups(along):
+    found = []
+    for core in range(2):
+        for x in range(4):
+            for other in range(8):
+                over_z = (along == "ring") == (core == 0)
+                found.append(
+                    [device(i, other, core, x) if over_z else device(other, i, core, x) for i in range(8)]
+                )
+    return found
+
+
+def pair(value, turn):
+    pairs = []
+    for z, y, core, x in grid():
+        pairs.append((device(z, y, core, x), device(z, y, core, x ^ (1 if core == turn else 3))))
+    return lax.ppermute(value, ALL, pairs)
+
+
+def core_swap(value):
+    return lax.ppermute(value, ALL, [(at, at ^ 4) for at in range(512)])
+
+
+def window(core):
+    return pl.ds(pl.multiple_of(core * OFFSET, 128), WINDOW)
+
+
+def pack_kernel(place, context, theirs, residual, small, near, side):
+    core = place[2]
+    for out in (near, side):
+        out[0:TOK, :] = context[:, window(core)]
+        out[TOK : 2 * TOK, :] = theirs[...]
+    for out, row, target in ((near, 1024, 3), (near, 1280, 5), (side, 1024, 4)):
+        start = place[target] * QUARTER
+        out[row : row + 128, :] = residual[:, pl.ds(pl.multiple_of(start, 128), WINDOW)]
+        out[row + 128 : row + 256, :] = residual[
+            :, pl.ds(pl.multiple_of(start + OFFSET, 128), WINDOW)
+        ]
+    near[1536:1552, :] = small[...]
+    side[1280:1296, :] = small[...]
+
+
+def gather_kernel(place, context, theirs, residual, near, side, far, ctx, res):
+    x = place[1]
+    ctx[x, 0:TOK, :] = context[:, window(place[2])]
+    ctx[x, TOK : 2 * TOK, :] = theirs[...]
+
+    def put(at, value):
+        res[pl.ds(pl.multiple_of(at * 128, 128), 128), :] = value
+
+    put(x, residual[:, pl.ds(pl.multiple_of(x * QUARTER, 128), QUARTER)])
+    for index, piece, row in ((3, near, 1024), (4, side, 1024), (5, far, 1280)):
+        ctx[place[index]] = piece[0 : 2 * TOK, :]
+        left, right = piece[row : row + 128, :], piece[row + 128 : row + 256, 128:512]
+        put(place[index], jnp.concatenate([left, right], axis=1))
+
+
+def sum_block(ctx, weight, total):
     step = pl.program_id(0)
     half = lax.rem(step, 2)
     product = lax.dot_general(ctx[0], weight[...], NT, preferred_element_type=F32)
@@ -54,29 +115,52 @@
     def _():
         total[half] += product
 
-    @pl.when(step == 7)
+
+def whole(total, pack):
+    rows = pl.ds(pack * 128, 128)
+    return jnp.concatenate([total[0, rows, :], total[1, rows, :]], axis=1)
+
+
+def other_kernel(ctx, weight, out, total):
+    sum_block(ctx, weight, total)
+
+    @pl.when(pl.program_id(0) == 7)
+    def _():
+        for pack in range(4):
+            out[pl.ds(pack * 128, 128), :] = whole(total, pack).astype(BF)
+
+
+def own_kernel(ctx, weight, res, out, total):
+    sum_block(ctx, weight, total)
+
+    @pl.when(pl.program_id(0) == 7)
     def _():
         for pack in range(4):
             rows = pl.ds(pack * 128, 128)
-            value = jnp.concatenate([total[0, rows, :], total[1, rows, :]], axis=1)
-            value = value + res[rows, :].astype(F32)
-            hidden[rows, :] = value
-            sq = value * value
-            part = sq[:, 0:128]
-            for tile in range(1, 7):
-                part = part + sq[:, tile * 128 : tile * 128 + 128]
-            squares[pl.ds(pack, 1), :] = jnp.sum(part.T, axis=0, keepdims=True)
-        squares[pl.ds(4, 4), :] = jnp.zeros((4, 128), F32)
-
-
-def pool_kernel(hidden, gain, pool, inverse, total, slots, squares):
+            out[rows, :] = whole(total, pack) + res[rows, :].astype(F32)
+
+
+def rms_kernel(own, swapped, squares):
+    squares[...] = jnp.zeros_like(squares)
+    for pack in range(4):
+        rows = pl.ds(pack * 128, 128)
+        value = own[rows, :] + swapped[rows, :].astype(F32)
+        sq = value * value
+        part = sq[:, 0:128]
+        for tile in range(1, 7):
+            part = part + sq[:, tile * 128 : tile * 128 + 128]
+        squares[pl.ds(pack, 1), :] = jnp.sum(part.T, axis=0, keepdims=True)
+
+
+def pool_kernel(own, swapped, gain, pool, inverse, total, slots, squares):
     scale = lax.rsqrt(total[...] / 3584.0 + 1e-06)
     summed = None
     for pack in range(4):
         rows = pl.ds(pack * 128, 128)
         column = jnp.broadcast_to(scale[pack : pack + 1, :], (128, 128)).T
         column = jnp.concatenate([column] * 7, axis=1)
-        normed = (hidden[rows, :] * column * gain[...]).astype(BF)
+        hidden = own[rows, :] + swapped[rows, :].astype(F32)
+        normed = (hidden * column * gain[...]).astype(BF)
         term = jnp.dot(pool[:, pack * 128 : pack * 128 + 128], normed, preferred_element_type=F32)
         summed = term if summed is None else summed + term
     pooled = summed * jnp.concatenate([inverse[...]] * 7, axis=1)
@@ -120,50 +204,59 @@
     z, y = lax.axis_index("z"), lax.axis_index("y")
     core, x = lax.axis_index("core"), lax.axis_index("tensor")
 
+    first = core == 0
+    ring, line = jnp.where(first, z, y), jnp.where(first, y, z)
+    near_x = jnp.where(first, x ^ 1, x ^ 3)
+    side_x = jnp.where(first, x ^ 3, x ^ 1)
+    far_x = x ^ 2
+    place = jnp.stack([ring, x, core, near_x, side_x, far_x]).astype(jnp.int32)
+
     weight = out_weight.T
-    keep = lax.ppermute(weight, ALL, spread(0))
-    cross = lax.ppermute(weight, ALL, spread(1))
+    lanes = lax.broadcasted_iota(jnp.int32, (28, WINDOW), 1)
+    low = weight[:, :WINDOW]
+    high = jnp.where(lanes < WINDOW - OFFSET, 0, weight[:, OFFSET:])
+    keep = lax.ppermute(jnp.where(first, low, high), ALL, spread(0))
+    cross = lax.ppermute(jnp.where(first, high, low), ALL, spread(1))
     block = jnp.concatenate(
-        [jnp.where(core == 0, keep, cross), jnp.where(core == 0, cross, keep)], axis=0
+        [jnp.where(first, keep, cross), jnp.where(first, cross, keep)], axis=0
     )
-    context, residual, doc_lengths, block = lax.optimization_barrier(
-        (context, residual, doc_lengths, block)
-    )
-    plane = lax.all_gather(block, ("z", "y"), axis=0, tiled=True)
-
-    ctx_down, ctx_up = shift(context, "tensor", 1), shift(context, "tensor", -1)
-
-    res_parts = [
-        lax.dynamic_slice(residual, (0, lax.rem(x + step, 4) * QUARTER), (128, QUARTER))
-        for step in range(4)
-    ]
-    res_recv = [
-        res_parts[0],
-        shift(res_parts[1], "tensor", 1),
-        shift(res_parts[2], "tensor", 2),
-        shift(res_parts[3], "tensor", 3),
-    ]
-    res = jnp.zeros((TOK, QUARTER), BF)
-    for step in range(4):
-        res = lax.dynamic_update_slice(res, res_recv[step], (lax.rem(x - step + 4, 4) * 128, 0))
-
+
+    late_context, _ = lax.optimization_barrier((context, keep))
+    theirs = core_swap(jnp.where(first, late_context[:, OFFSET:], late_context[:, :WINDOW]))
     resident = members[0]
     resident_f = resident.astype(F32)
-    partial_sq = jnp.sum(resident_f * resident_f, axis=-1).reshape(4, 128)
-    lens_rows = jnp.zeros((4, 128), F32)
-    lens_rows = lax.dynamic_update_slice(lens_rows, doc_lengths.astype(F32), (x, 0))
-    small = lax.psum(jnp.concatenate([partial_sq, lens_rows], axis=0), "tensor")
-    small, res = lax.optimization_barrier((small, res))
-    member_sq, lens = small[:4], small[4:, :32]
-
-    far_a = shift(ctx_down[: TOK // 2], "tensor", 1)
-    far_b = shift(ctx_up[TOK // 2 :], "tensor", -1)
-    ctx = jnp.zeros((4, TOK, QUARTER), BF)
-    ctx = lax.dynamic_update_slice(ctx, context[None], (x, 0, 0))
-    ctx = lax.dynamic_update_slice(ctx, ctx_down[None], (lax.rem(x + 3, 4), 0, 0))
-    ctx = lax.dynamic_update_slice(ctx, ctx_up[None], (lax.rem(x + 1, 4), 0, 0))
-    ctx = lax.dynamic_update_slice(ctx, far_a[None], (lax.rem(x + 2, 4), 0, 0))
-    ctx = lax.dynamic_update_slice(ctx, far_b[None], (lax.rem(x + 2, 4), TOK // 2, 0))
+    partial_sq = jnp.sum(resident_f * resident_f, axis=-1).astype(BF)
+    small = jnp.concatenate(
+        [partial_sq.reshape(4, 128), jnp.pad(doc_lengths.astype(BF), ((0, 0), (0, 96)))], axis=0
+    )
+    small = jnp.pad(small, ((0, 11), (0, WINDOW - 128)))
+    late_theirs, _ = lax.optimization_barrier((theirs, block))
+    to_near, to_side = pl.pallas_call(
+        pack_kernel,
+        out_shape=(
+            jax.ShapeDtypeStruct((1552, WINDOW), BF),
+            jax.ShapeDtypeStruct((1296, WINDOW), BF),
+        ),
+        in_specs=[SMEM] + [VMEM] * 4,
+        out_specs=(VMEM, VMEM),
+        compiler_params=params(),
+        cost_estimate=cost(0, 6_000_000),
+        name="pack",
+    )(place, context, late_theirs, residual, small)
+    block, to_near = lax.optimization_barrier((block, to_near))
+    near, side = pair(to_near, 0), pair(to_side, 1)
+    plane = lax.all_to_all(
+        jnp.broadcast_to(block[None], (8, 56, WINDOW)), ALL, 0, 0,
+        axis_index_groups=groups("line"), tiled=True,
+    ).reshape(HALF, WINDOW)
+    plane = lax.all_gather(plane, ALL, axis=0, axis_index_groups=groups("ring"), tiled=True)
+    far = pair(near, 1)
+
+    tails = [(x, small), (near_x, near[-16:]), (side_x, side[-16:]), (far_x, far[-16:])]
+    member_sq = sum((tail[:4, :128].astype(F32) for _, tail in tails[1:]), small[:4, :128].astype(F32))
+    lens = jnp.zeros((4, 32), F32)
+    for at, tail in tails:
+        lens = lax.dynamic_update_slice(lens, tail[4:5, :32].astype(F32), (at, 0))
 
     cluster_ids = jnp.arange(owner_map.shape[0], dtype=jnp.int32)
     matches = doc_cluster[:, 0][:, None] == cluster_ids[None, :]
@@ -197,27 +290,57 @@
     member_ids = jnp.arange(MEMBERS, dtype=jnp.int32).reshape(4, 128)
     factor = jnp.where(member_ids < own_count, lax.rsqrt(member_sq / 3584.0 + 1e-06), 0.0)
 
-    hidden, squares = pl.pallas_call(
-        project_kernel,
+    ctx, res = pl.pallas_call(
+        gather_kernel,
         out_shape=(
-            jax.ShapeDtypeStruct((TOK, QUARTER), F32),
-            jax.ShapeDtypeStruct((8, 128), F32),
+            jax.ShapeDtypeStruct((4, 2 * TOK, WINDOW), BF),
+            jax.ShapeDtypeStruct((TOK, QUARTER), BF),
         ),
+        in_specs=[SMEM] + [VMEM] * 6,
+        out_specs=(VMEM, VMEM),
+        compiler_params=params(),
+        cost_estimate=cost(0, 10_000_000),
+        name="gather",
+    )(place, context, theirs, residual, near, side, far)
+    weight_spec = pl.BlockSpec((HALF, WINDOW), lambda i: (i, 0))
+    out_spec = pl.BlockSpec((TOK, QUARTER), lambda i: (0, 0))
+    half_cost = cost(8 * 2 * TOK * WINDOW * HALF, 8_000_000)
+    other = pl.pallas_call(
+        other_kernel,
+        out_shape=jax.ShapeDtypeStruct((TOK, QUARTER), BF),
+        grid=(8,),
+        in_specs=[pl.BlockSpec((1, TOK, WINDOW), lambda i: (lax.div(i, 2), 1, 0)), weight_spec],
+        out_specs=out_spec,
+        scratch_shapes=[pltpu.VMEM((2, TOK, HALF), F32)],
+        compiler_params=params(),
+        cost_estimate=half_cost,
+        name="other",
+    )(ctx, plane)
+    swapped = core_swap(other)
+    own = pl.pallas_call(
+        own_kernel,
+        out_shape=jax.ShapeDtypeStruct((TOK, QUARTER), F32),
         grid=(8,),
         in_specs=[
-            pl.BlockSpec((1, TOK, QUARTER), lambda i: (lax.div(i, 2), 0, 0)),
-            pl.BlockSpec((HALF, QUARTER), lambda i: (i, 0)),
-            pl.BlockSpec((TOK, QUARTER), lambda i: (0, 0)),
+            pl.BlockSpec((1, TOK, WINDOW), lambda i: (lax.div(i, 2), 0, 0)),
+            weight_spec,
+            out_spec,
         ],
-        out_specs=(
-            pl.BlockSpec((TOK, QUARTER), lambda i: (0, 0)),
-            pl.BlockSpec((8, 128), lambda i: (0, 0)),
-        ),
+        out_specs=out_spec,
         scratch_shapes=[pltpu.VMEM((2, TOK, HALF), F32)],
         compiler_params=params(),
-        cost_estimate=cost(2 * TOK * QUARTER * 3584, 13_000_000),
-        name="project",
+        cost_estimate=half_cost,
+        name="own",
     )(ctx, plane, res)
+    squares = pl.pallas_call(
+        rms_kernel,
+        out_shape=jax.ShapeDtypeStruct((8, 128), F32),
+        in_specs=[VMEM] * 2,
+        out_specs=VMEM,
+        compiler_params=params(),
+        cost_estimate=cost(2 * TOK * QUARTER, 3_000_000),
+        name="rms",
+    )(own, swapped)
 
     slots, doc_sq = pl.pallas_call(
         pool_kernel,
@@ -225,12 +348,12 @@
             jax.ShapeDtypeStruct((SLOTS, QUARTER), BF),
             jax.ShapeDtypeStruct((8, 128), F32),
         ),
-        in_specs=[VMEM] * 5,
+        in_specs=[VMEM] * 6,
         out_specs=(VMEM, VMEM),
         compiler_params=params(),
         cost_estimate=cost(2 * SLOTS * TOK * QUARTER, 3_000_000),
         name="pool",
-    )(hidden, gain_of(norm_gain, x), pool, inverse, lax.psum(squares, "tensor"))
+    )(own, swapped, gain_of(norm_gain, x), pool, inverse, lax.psum(squares, "tensor"))
 
     arrived = lax.all_to_all(
         slots.reshape(DOCS, 2, QUARTER), DP, split_axis=0, concat_axis=0, tiled=True

time: 221 us -> 233 us (1.054)
  blocking collectives: 48.8 us -> 56.6 us
  Pallas kernels: 11.7 us -> 16.4 us
  other arithmetic: 5.27 us -> 9.33 us
  starting transfers between devices: 56.4 us -> 53.6 us
    all_gather x1, waiting for transfers between devices: 28 us -> 0.01 us  [body(): lax.all_gather(plane, ALL, axis=0, axis_index_groups=groups('ring'), tile...]
    ppermute x9 -> x7, waiting for transfers between devices: 15.1 us -> 42.3 us  [the longest x3 39.4 us: pair(): return lax.ppermute(value, ALL, pairs)]
    all_to_all x0 -> x1, blocking collectives: none -> 24.9 us  [body(): lax.all_to_all(jnp.broadcast_to(block[None], (8, 56, WINDOW)), ALL, 0, 0,...]
    psum x1 -> x0, blocking collectives: 19.3 us -> none  [body(): small = lax.psum(jnp.concatenate([partial_sq, lens_rows], axis=0), 'tensor')]
    unnamed x12 -> x30, local copies, waits for them, and re-layouts: 2.85 us -> 14.8 us
    dynamic_update_slice x9 -> x4, local copies, waits for them, and re-layouts: 7.77 us -> 0.14 us  [body(): lens = lax.dynamic_update_slice(lens, tail[4:5, :32].astype(F32), (at, 0))]
    pallas_call x1 -> x5, Pallas kernels: 9.42 us -> 14.1 us  [the longest x1 5.63 us: body(): pl.pallas_call(other_kernel, out_shape=jax.ShapeDtypeStruct((TOK, QUARTER...]
    convert_element_type x1 -> x5, other arithmetic: 0.01 us -> 2.63 us  [the longest x4 2.62 us: body(): lens = lax.dynamic_update_slice(lens, tail[4:5, :32].astype(F32), (at, 0))]
  transfers between devices with their start and end apart: 12 -> 10, of which waited for: 7 -> 5; matrix products, arithmetic and copies ran while one was open for 8% -> 4% of each run, Pallas kernels for 0% -> 3%
where the time goes in v3:
time: 233 us; the launch traced here: 232 us
  waiting for transfers between devices  62.9 us (27%)
  blocking collectives  56.6 us (24%)
  starting transfers between devices  53.6 us (23%)
  local copies, waits for them, and re-layouts  18.3 us (8%)
  Pallas kernels  16.4 us (7%)
  between operations  14.5 us (6%)
  other arithmetic  9.33 us (4%)
    ppermute x3, waiting for transfers between devices, pair(): return lax.ppermute(value, ALL, pairs)  39.4 us
    all_to_all x1, blocking collectives, body(): lax.all_to_all(jnp.broadcast_to(block[None], (8, 56, WINDOW)), ALL, 0, 0,...  24.9 us
    ppermute x3, starting transfers between devices, pair(): return lax.ppermute(value, ALL, pairs)  20.6 us
    all_to_all x1, waiting for transfers between devices, body(): lax.all_to_all(partial, ALL, split_axis=0, concat_axis=0, tiled=True)  15.4 us
    unnamed x30, local copies, waits for them, and re-layouts  14.8 us
    all_to_all x1, starting transfers between devices, body(): lax.all_to_all(partial, ALL, split_axis=0, concat_axis=0, tiled=True)  11.4 us
    psum x1, blocking collectives, body(): slot_sq = lax.psum(doc_sq, 'tensor')[:2].reshape(SLOTS)  11 us
    pmax x1, blocking collectives, body(): return (scores, lax.pmax(best[0], 'tensor'))  10.6 us
  transfers between devices with their start and end apart: 10, of which 5 were waited for; matrix products, arithmetic and copies ran while one was open for 4% of the time, Pallas kernels for 3%

profile of v3, /device:TPU:2, one launch (start us, length us, event | category | flops | bytes accessed | tf_op | source)
XLA Modules:
  0.0 231.9 jit_solution(10363917027582259820)
XLA Ops:
  8.2 3.9 %collective-permute-start.2 = (bf16[28,512]{1,0:T(8,128)(2,1)S(1)}, bf16[28,512]{1,0:T(8,128)(2,1)S(1)}, u32[]{:S(2)}, u32[]{:S(2)}) collective-permute-start(bf16[28,512]{1,0:T(8,128)(2,1)S(1)} %get-tuple-element.30), channel_id=1, source_target_pairs={{0,4},{1,20},{2,36},{3,52},{4,0},{5,128},{6,256},{7,384},{8,68},{9... | collective-permute-start | bytes 86024 | tf_op jit(solution)/shard_map/ppermute | solution.py:219
  12.1 4.1 %collective-permute-start = (bf16[28,512]{1,0:T(8,128)(2,1)S(1)}, bf16[28,512]{1,0:T(8,128)(2,1)S(1)}, u32[]{:S(2)}, u32[]{:S(2)}) collective-permute-start(bf16[28,512]{1,0:T(8,128)(2,1)S(1)} %get-tuple-element.31), channel_id=1, source_target_pairs={{0,0},{1,128},{2,256},{3,384},{4,4},{5,20},{6,36},{7,52},{8,8},{9,... | collective-permute-start | bytes 86024 | tf_op jit(solution)/shard_map/ppermute | solution.py:218
  16.8 2.9 %collective-permute-done = bf16[28,512]{1,0:T(8,128)(2,1)S(1)} collective-permute-done((bf16[28,512]{1,0:T(8,128)(2,1)S(1)}, bf16[28,512]{1,0:T(8,128)(2,1)S(1)}, u32[]{:S(2)}, u32[]{:S(2)}) %collective-permute-start) | collective-permute-done | bytes 28704 | tf_op jit(solution)/shard_map/ppermute | solution.py:218
  19.7 1.3 slice_select_fusion
  20.9 3.3 %collective-permute-start.1 = (bf16[512,512]{1,0:T(8,128)(2,1)S(1)}, bf16[512,512]{1,0:T(8,128)(2,1)S(1)}, u32[]{:S(2)}, u32[]{:S(2)}) collective-permute-start(bf16[512,512]{1,0:T(8,128)(2,1)S(1)} %slice_select_fusion), channel_id=1, source_target_pairs={{0,4},{1,5},{2,6},{3,7},{4,0},{5,1},{6,2},{7,3},{8,12},{9,13},{10,... | collective-permute-start | bytes 1572872 | tf_op jit(solution)/shard_map/ppermute | solution.py:68
  24.3 1.4 multiply_reduce_fusion
  26.7 1.1 copy-done.10
  27.9 1.1 copy-done.11
  29.0 24.9 %all_to_all.15 = bf16[8,56,512]{2,1,0:T(8,128)(2,1)} all-to-all(bf16[8,56,512]{2,1,0:T(8,128)(2,1)S(1)} %broadcast_in_dim.94), channel_id=1, replica_groups={{0,8,16,24,32,40,48,56},{64,72,80,88,96,104,112,120},{128,136,144,152,1..., dimensions={0} | all-to-all | bytes 917504 | tf_op jit(solution)/shard_map/all_to_all | solution.py:248
  53.9 1.9 collective-permute-start.3
  55.8 9.8 %collective-permute-start.4 = (bf16[1296,512]{1,0:T(8,128)(2,1)}, bf16[1296,512]{1,0:T(8,128)(2,1)}, u32[]{:S(2)}, u32[]{:S(2)}) collective-permute-start(bf16[1296,512]{1,0:T(8,128)(2,1)} %copy-done.11), channel_id=1, source_target_pairs={{0,3},{1,2},{2,1},{3,0},{4,5},{5,4},{6,7},{7,6},{8,11},{9,10},{10,... | collective-permute-start | bytes 3981320 | tf_op jit(solution)/shard_map/ppermute | solution.py:64
  65.7 23.1 %collective-permute-done.3.near = bf16[1552,512]{1,0:T(8,128)(2,1)} collective-permute-done((bf16[1552,512]{1,0:T(8,128)(2,1)}, bf16[1552,512]{1,0:T(8,128)(2,1)}, u32[]{:S(2)}, u32[]{:S(2)}) %collective-permute-start.3) | collective-permute-done | bytes 1589280 | tf_op jit(solution)/shard_map/ppermute | solution.py:64
  88.8 8.8 %collective-permute-start.5 = (bf16[1552,512]{1,0:T(8,128)(2,1)}, bf16[1552,512]{1,0:T(8,128)(2,1)}, u32[]{:S(2)}, u32[]{:S(2)}) collective-permute-start(bf16[1552,512]{1,0:T(8,128)(2,1)} %collective-permute-done.3.near), channel_id=1, source_target_pairs={{0,3},{1,2},{2,1},{3,0},{4,5},{5,4},{6,7},{7,6},{8,11},{9,10},{10,... | collective-permute-start | bytes 4767752 | tf_op jit(solution)/shard_map/ppermute | solution.py:64
  100.3 16.3 %collective-permute-done.5.far = bf16[1552,512]{1,0:T(8,128)(2,1)} collective-permute-done((bf16[1552,512]{1,0:T(8,128)(2,1)}, bf16[1552,512]{1,0:T(8,128)(2,1)}, u32[]{:S(2)}, u32[]{:S(2)}) %collective-permute-start.5) | collective-permute-done | bytes 1589280 | tf_op jit(solution)/shard_map/ppermute | solution.py:64
  117.5 2.6 %gather.1 = (bf16[4,1024,512]{2,1,0:T(8,128)(2,1)S(1)}, bf16[512,896]{1,0:T(8,128)(2,1)S(1)}) custom-call(s32[6]{0:T(128)S(1)} %stack.27.place, bf16[512,896]{1,0:T(8,128)(2,1)S(1)} %copy-done.5, bf16[512,512]{1,0:T(8,128)(2,1)S(1)} %collective-permute-done.1.theirs, bf16[128,3584]{1,0:T(8,128)(2,1)S(1)} %copy-done.7, ...), custom_call_target="tpu_custom_call" | custom-call | bytes 10000000 | tf_op jit(solution)/shard_map/gather/pallas_call | solution.py:293
  120.2 1.9 copy-done
  123.1 2.2 copy-done.1
  125.3 2.0 copy-done.3
  127.3 5.6 %other.1 = bf16[512,896]{1,0:T(8,128)(2,1)} custom-call(bf16[4,1024,512]{2,1,0:T(8,128)(2,1)S(1)} %copy-done.1, bf16[3584,512]{1,0:T(8,128)(2,1)S(1)} %copy-done.3), custom_call_target="tpu_custom_call" | custom-call | flops 1879048192 | bytes 8000000 | tf_op jit(solution)/shard_map/other/pallas_call | solution.py:308
  133.0 1.9 collective-permute-start.6
  135.6 2.2 copy-done.2
  137.8 2.0 copy-done.4
  139.8 1.2 copy-done.9
  141.0 4.8 %own.1 = f32[512,896]{1,0:T(8,128)S(1)} custom-call(bf16[4,1024,512]{2,1,0:T(8,128)(2,1)S(1)} %copy-done.2, bf16[3584,512]{1,0:T(8,128)(2,1)S(1)} %copy-done.4, bf16[512,896]{1,0:T(8,128)(2,1)S(1)} %copy-done.9), custom_call_target="tpu_custom_call" | custom-call | flops 1879048192 | bytes 8000000 | tf_op jit(solution)/shard_map/own/pallas_call | solution.py:320
  146.1 10.1 %psum.14.total = f32[8,128]{1,0:T(8,128)S(1)} all-reduce(f32[8,128]{1,0:T(8,128)S(1)} %rms.1), channel_id=1, replica_groups=mesh['z'=8,'y'=8,'core'=2,'tensor'=4] {'tensor'}, use_global_device_ids=true, to_apply=%region_5.6 | all-reduce | flops 1024 | bytes 8192 | tf_op jit(solution)/shard_map/psum | solution.py:356
  158.1 8.3 %all-to-all-start.1 = ((bf16[128,2,896]{2,1,0:T(2,128)(2,1)}), bf16[128,2,896]{2,1,0:T(2,128)(2,1)S(1)}, u32[]{:S(2)}, u32[]{:S(2)}) async-start(bf16[128,2,896]{2,1,0:T(2,128)(2,1)} %reshape.95), calls=%async_computation.1 | async-start | bytes 917504 | tf_op jit(solution)/shard_map/all_to_all | solution.py:358
  167.3 1.3 rsqrt_select_fusion.factor
  168.6 11.0 %psum.15 = f32[8,128]{1,0:T(8,128)S(1)} all-reduce(f32[8,128]{1,0:T(8,128)S(1)} %get-tuple-element.23), channel_id=1, replica_groups=mesh['z'=8,'y'=8,'core'=2,'tensor'=4] {'tensor'}, use_global_device_ids=true, to_apply=%region_7.8 | all-reduce | flops 1024 | bytes 8192 | tf_op jit(solution)/shard_map/psum | solution.py:362
  179.6 5.1 %all-to-all-done.1 = bf16[128,2,896]{2,1,0:T(2,128)(2,1)S(1)} async-done(((bf16[128,2,896]{2,1,0:T(2,128)(2,1)}), bf16[128,2,896]{2,1,0:T(2,128)(2,1)S(1)}, u32[]{:S(2)}, u32[]{:S(2)}) %all-to-all-start.1) | async-done | bytes 458784 | tf_op jit(solution)/shard_map/all_to_all | solution.py:358
  186.5 11.4 %all-to-all-start.2 = ((bf16[512,2,128]{2,1,0:T(2,128)(2,1)}), bf16[512,2,128]{2,1,0:T(2,128)(2,1)S(1)}, u32[]{:S(2)}, u32[]{:S(2)}) async-start(bf16[512,2,128]{2,1,0:T(2,128)(2,1)} %bitcast.12), calls=%async_computation.2 | async-start | bytes 524288 | tf_op jit(solution)/shard_map/all_to_all | solution.py:377
  198.1 15.4 %all-to-all-done.2 = bf16[512,2,128]{2,1,0:T(2,128)(2,1)S(1)} async-done(((bf16[512,2,128]{2,1,0:T(2,128)(2,1)}), bf16[512,2,128]{2,1,0:T(2,128)(2,1)S(1)}, u32[]{:S(2)}, u32[]{:S(2)}) %all-to-all-start.2) | async-done | bytes 262176 | tf_op jit(solution)/shard_map/all_to_all | solution.py:377
  214.5 10.6 %pmax.7 = f32[128]{0:T(128)} all-reduce(f32[128]{0:T(128)S(1)} %slice_bitcast_fusion.1), channel_id=1, replica_groups=mesh['z'=8,'y'=8,'core'=2,'tensor'=4] {'tensor'}, use_global_device_ids=true, to_apply=%region_10.11 | all-reduce | flops 128 | bytes 1024 | tf_op jit(solution)/shard_map/pmax | solution.py:391
  (81 shorter events, 13.6 us)
Async XLA Ops:
  7.2 18.8 %copy-start.5 = (bf16[512,896]{1,0:T(8,128)(2,1)S(1)}, bf16[512,896]{1,0:T(8,128)(2,1)}, u32[]{:S(2)}) copy-start(bf16[512,896]{1,0:T(8,128)(2,1)} %context.3) | copy-start | bytes 2752516
  7.2 18.8 %copy-start.7 = (bf16[128,3584]{1,0:T(8,128)(2,1)S(1)}, bf16[128,3584]{1,0:T(8,128)(2,1)}, u32[]{:S(2)}) copy-start(bf16[128,3584]{1,0:T(8,128)(2,1)} %residual.3) | copy-start | bytes 2752516
  7.2 115.9 %all-gather.2.cloned.1.call-start = ((), (), s32[]{:S(2)}) async-start(), calls=%async_computation.3 | async-start | bytes 4128768 | tf_op jit(solution)/shard_map/all_gather | solution.py:252
  8.2 17.7 %collective-permute-start.2 = (bf16[28,512]{1,0:T(8,128)(2,1)S(1)}, bf16[28,512]{1,0:T(8,128)(2,1)S(1)}, u32[]{:S(2)}, u32[]{:S(2)}) collective-permute-start(bf16[28,512]{1,0:T(8,128)(2,1)S(1)} %get-tuple-element.30), channel_id=1, source_target_pairs={{0,4},{1,20},{2,36},{3,52},{4,0},{5,128},{6,256},{7,384},{8,68},{9... | collective-permute-start | bytes 86024 | tf_op jit(solution)/shard_map/ppermute | solution.py:219
  12.1 7.6 %collective-permute-start = (bf16[28,512]{1,0:T(8,128)(2,1)S(1)}, bf16[28,512]{1,0:T(8,128)(2,1)S(1)}, u32[]{:S(2)}, u32[]{:S(2)}) collective-permute-start(bf16[28,512]{1,0:T(8,128)(2,1)S(1)} %get-tuple-element.31), channel_id=1, source_target_pairs={{0,0},{1,128},{2,256},{3,384},{4,4},{5,20},{6,36},{7,52},{8,8},{9,... | collective-permute-start | bytes 86024 | tf_op jit(solution)/shard_map/ppermute | solution.py:218
  20.9 5.0 %collective-permute-start.1 = (bf16[512,512]{1,0:T(8,128)(2,1)S(1)}, bf16[512,512]{1,0:T(8,128)(2,1)S(1)}, u32[]{:S(2)}, u32[]{:S(2)}) collective-permute-start(bf16[512,512]{1,0:T(8,128)(2,1)S(1)} %slice_select_fusion), channel_id=1, source_target_pairs={{0,4},{1,5},{2,6},{3,7},{4,0},{5,1},{6,2},{7,3},{8,12},{9,13},{10,... | collective-permute-start | bytes 1572872 | tf_op jit(solution)/shard_map/ppermute | solution.py:68
  25.9 72.6 %copy-start.12 = (s32[128]{0:T(128)S(1)}, s32[128]{0:T(128)}, u32[]{:S(2)}) copy-start(s32[128]{0:T(128)} %param.17) | copy-start | bytes 1540
  25.9 72.6 %copy-start.13 = (s32[128]{0:T(128)S(1)}, s32[128]{0:T(128)}, u32[]{:S(2)}) copy-start(s32[128]{0:T(128)} %param.16) | copy-start | bytes 1540
  25.9 72.6 %copy-start.14 = (s32[128,1]{0,1:T(1,128)S(1)}, s32[128,1]{0,1:T(1,128)}, u32[]{:S(2)}) copy-start(s32[128,1]{0,1:T(1,128)} %param.15) | copy-start | bytes 1540
  26.7 1.2 copy-start.10
  27.9 1.1 copy-start.11
  53.9 34.9 %collective-permute-start.3 = (bf16[1552,512]{1,0:T(8,128)(2,1)}, bf16[1552,512]{1,0:T(8,128)(2,1)}, u32[]{:S(2)}, u32[]{:S(2)}) collective-permute-start(bf16[1552,512]{1,0:T(8,128)(2,1)} %copy-done.10), channel_id=1, source_target_pairs={{0,1},{1,0},{2,3},{3,2},{4,7},{5,6},{6,5},{7,4},{8,9},{9,8},{10,11... | collective-permute-start | bytes 4767752 | tf_op jit(solution)/shard_map/ppermute | solution.py:64
  55.8 43.1 %collective-permute-start.4 = (bf16[1296,512]{1,0:T(8,128)(2,1)}, bf16[1296,512]{1,0:T(8,128)(2,1)}, u32[]{:S(2)}, u32[]{:S(2)}) collective-permute-start(bf16[1296,512]{1,0:T(8,128)(2,1)} %copy-done.11), channel_id=1, source_target_pairs={{0,3},{1,2},{2,1},{3,0},{4,5},{5,4},{6,7},{7,6},{8,11},{9,10},{10,... | collective-permute-start | bytes 3981320 | tf_op jit(solution)/shard_map/ppermute | solution.py:64
  88.8 27.7 %collective-permute-start.5 = (bf16[1552,512]{1,0:T(8,128)(2,1)}, bf16[1552,512]{1,0:T(8,128)(2,1)}, u32[]{:S(2)}, u32[]{:S(2)}) collective-permute-start(bf16[1552,512]{1,0:T(8,128)(2,1)} %collective-permute-done.3.near), channel_id=1, source_target_pairs={{0,3},{1,2},{2,1},{3,0},{4,5},{5,4},{6,7},{7,6},{8,11},{9,10},{10,... | collective-permute-start | bytes 4767752 | tf_op jit(solution)/shard_map/ppermute | solution.py:64
  120.2 1.9 copy-start
  122.1 1.0 copy-start.8
  123.1 2.2 copy-start.1
  125.3 2.0 copy-start.3
  133.0 12.9 %collective-permute-start.6 = (bf16[512,896]{1,0:T(8,128)(2,1)}, bf16[512,896]{1,0:T(8,128)(2,1)S(1)}, u32[]{:S(2)}, u32[]{:S(2)}) collective-permute-start(bf16[512,896]{1,0:T(8,128)(2,1)} %other.1), channel_id=1, source_target_pairs={{0,4},{1,5},{2,6},{3,7},{4,0},{5,1},{6,2},{7,3},{8,12},{9,13},{10,... | collective-permute-start | bytes 2752520 | tf_op jit(solution)/shard_map/ppermute | solution.py:68
  135.6 2.2 copy-start.2
  137.8 2.0 copy-start.4
  139.8 1.2 copy-start.9
  157.1 27.8 %copy-start.6 = (bf16[1,512,896]{2,1,0:T(8,128)(2,1)S(1)}, bf16[1,512,896]{2,1,0:T(8,128)(2,1)}, u32[]{:S(2)}) copy-start(bf16[1,512,896]{2,1,0:T(8,128)(2,1)} %param.13) | copy-start | bytes 2752516
  158.1 26.7 %all-to-all-start.1 = ((bf16[128,2,896]{2,1,0:T(2,128)(2,1)}), bf16[128,2,896]{2,1,0:T(2,128)(2,1)S(1)}, u32[]{:S(2)}, u32[]{:S(2)}) async-start(bf16[128,2,896]{2,1,0:T(2,128)(2,1)} %reshape.95), calls=%async_computation.1 | async-start | bytes 917504 | tf_op jit(solution)/shard_map/all_to_all | solution.py:358
  186.5 27.0 %all-to-all-start.2 = ((bf16[512,2,128]{2,1,0:T(2,128)(2,1)}), bf16[512,2,128]{2,1,0:T(2,128)(2,1)S(1)}, u32[]{:S(2)}, u32[]{:S(2)}) async-start(bf16[512,2,128]{2,1,0:T(2,128)(2,1)} %bitcast.12), calls=%async_computation.2 | async-start | bytes 524288 | tf_op jit(solution)/shard_map/all_to_all | solution.py:377
Sparse Core Ops, SparseCore 0:
  54.0 43.8 all-gather.1

commit v4 on v3

--- a/solution.py
+++ b/solution.py
@@ -16,8 +16,8 @@
 DOCS, SLOTS, MEMBERS, SHARE = 128, 256, 512, 128
 
 
-def params():
-    return pltpu.CompilerParams(vmem_limit_bytes=20 * 1024 * 1024)
+def params(mib=20):
+    return pltpu.CompilerParams(vmem_limit_bytes=mib * 1024 * 1024)
 
 
 def cost(flops, nbytes):
@@ -237,20 +237,21 @@
             jax.ShapeDtypeStruct((1552, WINDOW), BF),
             jax.ShapeDtypeStruct((1296, WINDOW), BF),
         ),
-        in_specs=[SMEM] + [VMEM] * 4,
-        out_specs=(VMEM, VMEM),
-        compiler_params=params(),
+        in_specs=[SMEM] + [pl.BlockSpec()] * 4,
+        out_specs=(pl.BlockSpec(), pl.BlockSpec()),
+        compiler_params=params(56),
         cost_estimate=cost(0, 6_000_000),
         name="pack",
     )(place, context, late_theirs, residual, small)
     block, to_near = lax.optimization_barrier((block, to_near))
-    near, side = pair(to_near, 0), pair(to_side, 1)
+    near = pair(to_near, 0)
     plane = lax.all_to_all(
         jnp.broadcast_to(block[None], (8, 56, WINDOW)), ALL, 0, 0,
         axis_index_groups=groups("line"), tiled=True,
     ).reshape(HALF, WINDOW)
+    plane, near, to_side = lax.optimization_barrier((plane, near, to_side))
     plane = lax.all_gather(plane, ALL, axis=0, axis_index_groups=groups("ring"), tiled=True)
-    far = pair(near, 1)
+    far, side = pair(near, 1), pair(to_side, 1)
 
     tails = [(x, small), (near_x, near[-16:]), (side_x, side[-16:]), (far_x, far[-16:])]
     member_sq = sum((tail[:4, :128].astype(F32) for _, tail in tails[1:]), small[:4, :128].astype(F32))
@@ -296,9 +297,9 @@
             jax.ShapeDtypeStruct((4, 2 * TOK, WINDOW), BF),
             jax.ShapeDtypeStruct((TOK, QUARTER), BF),
         ),
-        in_specs=[SMEM] + [VMEM] * 6,
-        out_specs=(VMEM, VMEM),
-        compiler_params=params(),
+        in_specs=[SMEM] + [pl.BlockSpec()] * 6,
+        out_specs=(pl.BlockSpec(), pl.BlockSpec()),
+        compiler_params=params(56),
         cost_estimate=cost(0, 10_000_000),
         name="gather",
     )(place, context, theirs, residual, near, side, far)
@@ -312,7 +313,7 @@
         in_specs=[pl.BlockSpec((1, TOK, WINDOW), lambda i: (lax.div(i, 2), 1, 0)), weight_spec],
         out_specs=out_spec,
         scratch_shapes=[pltpu.VMEM((2, TOK, HALF), F32)],
-        compiler_params=params(),
+        compiler_params=params(56),
         cost_estimate=half_cost,
         name="other",
     )(ctx, plane)
@@ -328,7 +329,7 @@
         ],
         out_specs=out_spec,
         scratch_shapes=[pltpu.VMEM((2, TOK, HALF), F32)],
-        compiler_params=params(),
+        compiler_params=params(56),
         cost_estimate=half_cost,
         name="own",
     )(ctx, plane, res)

time: 233 us -> 224 us (0.961)
  Pallas kernels: 16.4 us -> 30 us
  waiting for transfers between devices: 62.9 us -> 52.7 us
  local copies, waits for them, and re-layouts: 18.3 us -> 10.3 us
  starting transfers between devices: 53.6 us -> 50.9 us
    ppermute x3, waiting for transfers between devices: 39.4 us -> 29.2 us  [pair(): return lax.ppermute(value, ALL, pairs)]
    unnamed x30 -> x20, local copies, waits for them, and re-layouts: 14.8 us -> 5.6 us
    ppermute x3, starting transfers between devices: 20.6 us -> 14.3 us  [pair(): return lax.ppermute(value, ALL, pairs)]
    pallas_call x1, Pallas kernels: 4.81 us -> 9.53 us  [body(): pl.pallas_call(own_kernel, out_shape=jax.ShapeDtypeStruct((TOK, QUARTER),...]
    all_to_all x1, starting transfers between devices: 8.33 us -> 11.9 us  [body(): lax.all_to_all(slots.reshape(DOCS, 2, QUARTER), DP, split_axis=0, concat_...]
    pallas_call x1, Pallas kernels: 5.63 us -> 8.69 us  [body(): pl.pallas_call(other_kernel, out_shape=jax.ShapeDtypeStruct((TOK, QUARTER...]
    pallas_call x1, Pallas kernels: 2.64 us -> 5.69 us  [body(): pl.pallas_call(gather_kernel, out_shape=(jax.ShapeDtypeStruct((4, 2 * TOK...]
    pallas_call x1, Pallas kernels: 0.73 us -> 3.45 us  [body(): pl.pallas_call(pack_kernel, out_shape=(jax.ShapeDtypeStruct((1552, WINDOW...]
  transfers between devices with their start and end apart: 10 -> 10, of which waited for: 5 -> 4; matrix products, arithmetic and copies ran while one was open for 4% -> 5% of each run, Pallas kernels for 3% -> 7%
where the time goes in v4:
time: 224 us; the launch traced here: 223 us
  blocking collectives  55.9 us (25%)
  waiting for transfers between devices  52.7 us (24%)
  starting transfers between devices  50.9 us (23%)
  Pallas kernels  30 us (13%)
  between operations  14.4 us (6%)
  local copies, waits for them, and re-layouts  10.3 us (5%)
  other arithmetic  8.18 us (4%)
    ppermute x3, waiting for transfers between devices, pair(): return lax.ppermute(value, ALL, pairs)  29.2 us
    all_to_all x1, blocking collectives, body(): lax.all_to_all(jnp.broadcast_to(block[None], (8, 56, WINDOW)), ALL, 0, 0,...  25 us
    all_to_all x1, waiting for transfers between devices, body(): lax.all_to_all(partial, ALL, split_axis=0, concat_axis=0, tiled=True)  15.5 us
    ppermute x3, starting transfers between devices, pair(): return lax.ppermute(value, ALL, pairs)  14.3 us
    all_to_all x1, starting transfers between devices, body(): lax.all_to_all(slots.reshape(DOCS, 2, QUARTER), DP, split_axis=0, concat_...  11.9 us
    all_to_all x1, starting transfers between devices, body(): lax.all_to_all(partial, ALL, split_axis=0, concat_axis=0, tiled=True)  11.4 us
    psum x1, blocking collectives, body(): slot_sq = lax.psum(doc_sq, 'tensor')[:2].reshape(SLOTS)  11 us
    pmax x1, blocking collectives, body(): return (scores, lax.pmax(best[0], 'tensor'))  10.5 us
  transfers between devices with their start and end apart: 10, of which 4 were waited for; matrix products, arithmetic and copies ran while one was open for 5% of the time, Pallas kernels for 7%

profile of v4, /device:TPU:2, one launch (start us, length us, event | category | flops | bytes accessed | tf_op | source)
XLA Modules:
  0.0 222.7 jit_solution(2565646699152630479)
XLA Ops:
  7.2 0.9 broadcast_select_fusion.2
  8.1 3.9 %collective-permute-start.2 = (bf16[28,512]{1,0:T(8,128)(2,1)S(1)}, bf16[28,512]{1,0:T(8,128)(2,1)S(1)}, u32[]{:S(2)}, u32[]{:S(2)}) collective-permute-start(bf16[28,512]{1,0:T(8,128)(2,1)S(1)} %get-tuple-element.36), channel_id=1, source_target_pairs={{0,4},{1,20},{2,36},{3,52},{4,0},{5,128},{6,256},{7,384},{8,68},{9... | collective-permute-start | bytes 86024 | tf_op jit(solution)/shard_map/ppermute | solution.py:219
  12.0 4.1 %collective-permute-start = (bf16[28,512]{1,0:T(8,128)(2,1)S(1)}, bf16[28,512]{1,0:T(8,128)(2,1)S(1)}, u32[]{:S(2)}, u32[]{:S(2)}) collective-permute-start(bf16[28,512]{1,0:T(8,128)(2,1)S(1)} %get-tuple-element.37), channel_id=1, source_target_pairs={{0,0},{1,128},{2,256},{3,384},{4,4},{5,20},{6,36},{7,52},{8,8},{9,... | collective-permute-start | bytes 86024 | tf_op jit(solution)/shard_map/ppermute | solution.py:218
  16.8 2.9 %collective-permute-done = bf16[28,512]{1,0:T(8,128)(2,1)S(1)} collective-permute-done((bf16[28,512]{1,0:T(8,128)(2,1)S(1)}, bf16[28,512]{1,0:T(8,128)(2,1)S(1)}, u32[]{:S(2)}, u32[]{:S(2)}) %collective-permute-start) | collective-permute-done | bytes 28704 | tf_op jit(solution)/shard_map/ppermute | solution.py:218
  19.6 1.3 slice_select_fusion
  20.9 3.3 %collective-permute-start.1 = (bf16[512,512]{1,0:T(8,128)(2,1)S(1)}, bf16[512,512]{1,0:T(8,128)(2,1)S(1)}, u32[]{:S(2)}, u32[]{:S(2)}) collective-permute-start(bf16[512,512]{1,0:T(8,128)(2,1)S(1)} %slice_select_fusion), channel_id=1, source_target_pairs={{0,4},{1,5},{2,6},{3,7},{4,0},{5,1},{6,2},{7,3},{8,12},{9,13},{10,... | collective-permute-start | bytes 1572872 | tf_op jit(solution)/shard_map/ppermute | solution.py:68
  26.7 3.5 %pack.1 = (bf16[1552,512]{1,0:T(8,128)(2,1)}, bf16[1296,512]{1,0:T(8,128)(2,1)}) custom-call(s32[6]{0:T(128)} %stack.27.place, bf16[512,896]{1,0:T(8,128)(2,1)} %context.3, bf16[512,512]{1,0:T(8,128)(2,1)} %copy-done.6, bf16[128,3584]{1,0:T(8,128)(2,1)} %residual.3, bf16[16,512]{1,0:T(8,128)(2,1)} %pad.9.small), custom_call_target="tpu_custom_call" | custom-call | bytes 6000000 | tf_op jit(solution)/shard_map/pack/pallas_call | solution.py:234
  30.1 1.9 collective-permute-start.3
  32.1 25.0 %all_to_all.15 = bf16[8,56,512]{2,1,0:T(8,128)(2,1)} all-to-all(bf16[8,56,512]{2,1,0:T(8,128)(2,1)S(1)} %broadcast_in_dim.94), channel_id=1, replica_groups={{0,8,16,24,32,40,48,56},{64,72,80,88,96,104,112,120},{128,136,144,152,1..., dimensions={0} | all-to-all | bytes 917504 | tf_op jit(solution)/shard_map/all_to_all | solution.py:248
  57.1 10.5 %collective-permute-start.5 = (bf16[1552,512]{1,0:T(8,128)(2,1)}, bf16[1552,512]{1,0:T(8,128)(2,1)}, u32[]{:S(2)}, u32[]{:S(2)}) collective-permute-start(bf16[1552,512]{1,0:T(8,128)(2,1)} %collective-permute-done.3.near), channel_id=1, source_target_pairs={{0,3},{1,2},{2,1},{3,0},{4,5},{5,4},{6,7},{7,6},{8,11},{9,10},{10,... | collective-permute-start | bytes 4767752 | tf_op jit(solution)/shard_map/ppermute | solution.py:64
  67.6 1.9 collective-permute-start.4
  71.5 29.2 %collective-permute-done.4.side = bf16[1296,512]{1,0:T(8,128)(2,1)} collective-permute-done((bf16[1296,512]{1,0:T(8,128)(2,1)}, bf16[1296,512]{1,0:T(8,128)(2,1)}, u32[]{:S(2)}, u32[]{:S(2)}) %collective-permute-start.4) | collective-permute-done | bytes 1327136 | tf_op jit(solution)/shard_map/ppermute | solution.py:64
  102.4 5.7 %gather.1 = (bf16[4,1024,512]{2,1,0:T(8,128)(2,1)}, bf16[512,896]{1,0:T(8,128)(2,1)}) custom-call(s32[6]{0:T(128)} %stack.27.place, bf16[512,896]{1,0:T(8,128)(2,1)} %context.3, bf16[512,512]{1,0:T(8,128)(2,1)} %copy-done.6, bf16[128,3584]{1,0:T(8,128)(2,1)} %residual.3, bf16[1552,512]{1,0:T(8,128)(2,1)} %collective-permute-done.3.near, ...), custom_call_target="tpu_custom_call" | custom-call | bytes 10000000 | tf_op jit(solution)/shard_map/gather/pallas_call | solution.py:294
  108.1 8.7 %other.1 = bf16[512,896]{1,0:T(8,128)(2,1)} custom-call(bf16[4,1024,512]{2,1,0:T(8,128)(2,1)} %get-tuple-element.25.ctx, bf16[3584,512]{1,0:T(8,128)(2,1)} %all-gather.2.cloned.1.call-done.weight), custom_call_target="tpu_custom_call" | custom-call | flops 1879048192 | bytes 8000000 | tf_op jit(solution)/shard_map/other/pallas_call | solution.py:309
  116.7 1.9 collective-permute-start.6
  119.4 9.5 %own.1 = f32[512,896]{1,0:T(8,128)} custom-call(bf16[4,1024,512]{2,1,0:T(8,128)(2,1)} %get-tuple-element.25.ctx, bf16[3584,512]{1,0:T(8,128)(2,1)} %all-gather.2.cloned.1.call-done.weight, bf16[512,896]{1,0:T(8,128)(2,1)} %get-tuple-element.27.res), custom_call_target="tpu_custom_call" | custom-call | flops 1879048192 | bytes 8000000 | tf_op jit(solution)/shard_map/own/pallas_call | solution.py:321
  128.9 0.9 copy-done.3
  129.8 1.5 copy-done
  131.3 1.2 copy-done.4
  132.8 9.5 %psum.14.total = f32[8,128]{1,0:T(8,128)S(1)} all-reduce(f32[8,128]{1,0:T(8,128)S(1)} %rms.1), channel_id=1, replica_groups=mesh['z'=8,'y'=8,'core'=2,'tensor'=4] {'tensor'}, use_global_device_ids=true, to_apply=%region_5.6 | all-reduce | flops 1024 | bytes 8192 | tf_op jit(solution)/shard_map/psum | solution.py:357
  142.4 1.2 copy-done.5
  143.6 0.8 pool.1
  144.4 0.9 reshape.95
  145.4 11.9 %all-to-all-start.1 = ((bf16[128,2,896]{2,1,0:T(2,128)(2,1)}), bf16[128,2,896]{2,1,0:T(2,128)(2,1)S(1)}, u32[]{:S(2)}, u32[]{:S(2)}) async-start(bf16[128,2,896]{2,1,0:T(2,128)(2,1)} %reshape.95), calls=%async_computation.1 | async-start | bytes 917504 | tf_op jit(solution)/shard_map/all_to_all | solution.py:359
  158.1 1.4 rsqrt_select_fusion.factor
  159.5 11.0 %psum.15 = f32[8,128]{1,0:T(8,128)S(1)} all-reduce(f32[8,128]{1,0:T(8,128)S(1)} %get-tuple-element.29), channel_id=1, replica_groups=mesh['z'=8,'y'=8,'core'=2,'tensor'=4] {'tensor'}, use_global_device_ids=true, to_apply=%region_7.8 | all-reduce | flops 1024 | bytes 8192 | tf_op jit(solution)/shard_map/psum | solution.py:363
  170.5 5.1 %all-to-all-done.1 = bf16[128,2,896]{2,1,0:T(2,128)(2,1)S(1)} async-done(((bf16[128,2,896]{2,1,0:T(2,128)(2,1)}), bf16[128,2,896]{2,1,0:T(2,128)(2,1)S(1)}, u32[]{:S(2)}, u32[]{:S(2)}) %all-to-all-start.1) | async-done | bytes 458784 | tf_op jit(solution)/shard_map/all_to_all | solution.py:359
  176.5 0.9 copy.12
  177.4 11.4 %all-to-all-start.2 = ((bf16[512,2,128]{2,1,0:T(2,128)(2,1)}), bf16[512,2,128]{2,1,0:T(2,128)(2,1)S(1)}, u32[]{:S(2)}, u32[]{:S(2)}) async-start(bf16[512,2,128]{2,1,0:T(2,128)(2,1)} %bitcast.12), calls=%async_computation.2 | async-start | bytes 524288 | tf_op jit(solution)/shard_map/all_to_all | solution.py:378
  188.9 15.5 %all-to-all-done.2 = bf16[512,2,128]{2,1,0:T(2,128)(2,1)S(1)} async-done(((bf16[512,2,128]{2,1,0:T(2,128)(2,1)}), bf16[512,2,128]{2,1,0:T(2,128)(2,1)S(1)}, u32[]{:S(2)}, u32[]{:S(2)}) %all-to-all-start.2) | async-done | bytes 262176 | tf_op jit(solution)/shard_map/all_to_all | solution.py:378
  204.5 0.9 home.1
  205.3 10.5 %pmax.7 = f32[128]{0:T(128)} all-reduce(f32[128]{0:T(128)S(1)} %slice_bitcast_fusion.1), channel_id=1, replica_groups=mesh['z'=8,'y'=8,'core'=2,'tensor'=4] {'tensor'}, use_global_device_ids=true, to_apply=%region_10.11 | all-reduce | flops 128 | bytes 1024 | tf_op jit(solution)/shard_map/pmax | solution.py:392
  (71 shorter events, 9.7 us)
Async XLA Ops:
  7.2 17.1 %copy-start.2 = (bf16[1,512,896]{2,1,0:T(8,128)(2,1)S(1)}, bf16[1,512,896]{2,1,0:T(8,128)(2,1)}, u32[]{:S(2)}) copy-start(bf16[1,512,896]{2,1,0:T(8,128)(2,1)} %param.13) | copy-start | bytes 2752516
  7.2 100.9 %all-gather.2.cloned.1.call-start = ((), (), s32[]{:S(2)}) async-start(), calls=%async_computation.3 | async-start | bytes 4128768 | tf_op jit(solution)/shard_map/all_gather | solution.py:253
  8.1 17.7 %collective-permute-start.2 = (bf16[28,512]{1,0:T(8,128)(2,1)S(1)}, bf16[28,512]{1,0:T(8,128)(2,1)S(1)}, u32[]{:S(2)}, u32[]{:S(2)}) collective-permute-start(bf16[28,512]{1,0:T(8,128)(2,1)S(1)} %get-tuple-element.36), channel_id=1, source_target_pairs={{0,4},{1,20},{2,36},{3,52},{4,0},{5,128},{6,256},{7,384},{8,68},{9... | collective-permute-start | bytes 86024 | tf_op jit(solution)/shard_map/ppermute | solution.py:219
  12.0 7.6 %collective-permute-start = (bf16[28,512]{1,0:T(8,128)(2,1)S(1)}, bf16[28,512]{1,0:T(8,128)(2,1)S(1)}, u32[]{:S(2)}, u32[]{:S(2)}) collective-permute-start(bf16[28,512]{1,0:T(8,128)(2,1)S(1)} %get-tuple-element.37), channel_id=1, source_target_pairs={{0,0},{1,128},{2,256},{3,384},{4,4},{5,20},{6,36},{7,52},{8,8},{9,... | collective-permute-start | bytes 86024 | tf_op jit(solution)/shard_map/ppermute | solution.py:218
  20.9 5.0 %collective-permute-start.1 = (bf16[512,512]{1,0:T(8,128)(2,1)S(1)}, bf16[512,512]{1,0:T(8,128)(2,1)S(1)}, u32[]{:S(2)}, u32[]{:S(2)}) collective-permute-start(bf16[512,512]{1,0:T(8,128)(2,1)S(1)} %slice_select_fusion), channel_id=1, source_target_pairs={{0,4},{1,5},{2,6},{3,7},{4,0},{5,1},{6,2},{7,3},{8,12},{9,13},{10,... | collective-permute-start | bytes 1572872 | tf_op jit(solution)/shard_map/ppermute | solution.py:68
  25.8 44.5 %copy-start.7 = (s32[128]{0:T(128)S(1)}, s32[128]{0:T(128)}, u32[]{:S(2)}) copy-start(s32[128]{0:T(128)} %param.17) | copy-start | bytes 1540
  25.8 44.5 %copy-start.8 = (s32[128]{0:T(128)S(1)}, s32[128]{0:T(128)}, u32[]{:S(2)}) copy-start(s32[128]{0:T(128)} %param.16) | copy-start | bytes 1540
  25.8 44.5 %copy-start.9 = (s32[128,1]{0,1:T(1,128)S(1)}, s32[128,1]{0,1:T(1,128)}, u32[]{:S(2)}) copy-start(s32[128,1]{0,1:T(1,128)} %param.15) | copy-start | bytes 1540
  25.9 0.8 copy-start.6
  30.1 26.9 %collective-permute-start.3 = (bf16[1552,512]{1,0:T(8,128)(2,1)}, bf16[1552,512]{1,0:T(8,128)(2,1)}, u32[]{:S(2)}, u32[]{:S(2)}) collective-permute-start(bf16[1552,512]{1,0:T(8,128)(2,1)} %get-tuple-element.21), channel_id=1, source_target_pairs={{0,1},{1,0},{2,3},{3,2},{4,7},{5,6},{6,5},{7,4},{8,9},{9,8},{10,11... | collective-permute-start | bytes 4767752 | tf_op jit(solution)/shard_map/ppermute | solution.py:64
  57.1 44.3 %collective-permute-start.5 = (bf16[1552,512]{1,0:T(8,128)(2,1)}, bf16[1552,512]{1,0:T(8,128)(2,1)}, u32[]{:S(2)}, u32[]{:S(2)}) collective-permute-start(bf16[1552,512]{1,0:T(8,128)(2,1)} %collective-permute-done.3.near), channel_id=1, source_target_pairs={{0,3},{1,2},{2,1},{3,0},{4,5},{5,4},{6,7},{7,6},{8,11},{9,10},{10,... | collective-permute-start | bytes 4767752 | tf_op jit(solution)/shard_map/ppermute | solution.py:64
  67.6 33.1 %collective-permute-start.4 = (bf16[1296,512]{1,0:T(8,128)(2,1)}, bf16[1296,512]{1,0:T(8,128)(2,1)}, u32[]{:S(2)}, u32[]{:S(2)}) collective-permute-start(bf16[1296,512]{1,0:T(8,128)(2,1)} %get-tuple-element.24), channel_id=1, source_target_pairs={{0,3},{1,2},{2,1},{3,0},{4,5},{5,4},{6,7},{7,6},{8,11},{9,10},{10,... | collective-permute-start | bytes 3981320 | tf_op jit(solution)/shard_map/ppermute | solution.py:64
  116.7 12.2 %collective-permute-start.6 = (bf16[512,896]{1,0:T(8,128)(2,1)}, bf16[512,896]{1,0:T(8,128)(2,1)S(1)}, u32[]{:S(2)}, u32[]{:S(2)}) collective-permute-start(bf16[512,896]{1,0:T(8,128)(2,1)} %other.1), channel_id=1, source_target_pairs={{0,4},{1,5},{2,6},{3,7},{4,0},{5,1},{6,2},{7,3},{8,12},{9,13},{10,... | collective-permute-start | bytes 2752520 | tf_op jit(solution)/shard_map/ppermute | solution.py:68
  128.9 0.9 copy-start.3
  129.8 1.5 copy-start
  131.3 1.2 copy-start.4
  132.5 9.9 %copy-start.1 = (f32[512,896]{1,0:T(8,128)S(1)}, f32[512,896]{1,0:T(8,128)}, u32[]{:S(2)}) copy-start(f32[512,896]{1,0:T(8,128)} %own.1) | copy-start | bytes 5505028
  142.4 1.2 copy-start.5
  145.4 30.2 %all-to-all-start.1 = ((bf16[128,2,896]{2,1,0:T(2,128)(2,1)}), bf16[128,2,896]{2,1,0:T(2,128)(2,1)S(1)}, u32[]{:S(2)}, u32[]{:S(2)}) async-start(bf16[128,2,896]{2,1,0:T(2,128)(2,1)} %reshape.95), calls=%async_computation.1 | async-start | bytes 917504 | tf_op jit(solution)/shard_map/all_to_all | solution.py:359
  177.4 27.0 %all-to-all-start.2 = ((bf16[512,2,128]{2,1,0:T(2,128)(2,1)}), bf16[512,2,128]{2,1,0:T(2,128)(2,1)S(1)}, u32[]{:S(2)}, u32[]{:S(2)}) async-start(bf16[512,2,128]{2,1,0:T(2,128)(2,1)} %bitcast.12), calls=%async_computation.2 | async-start | bytes 524288 | tf_op jit(solution)/shard_map/all_to_all | solution.py:378
Sparse Core Ops, SparseCore 0:
  57.2 50.2 all-gather.1

commit v5 on v2

--- a/solution.py
+++ b/solution.py
@@ -7,66 +7,103 @@
 
 DP = ("z", "y", "core")
 ALL = ("z", "y", "core", "tensor")
-SIZES = {"z": 8, "y": 8, "core": 2, "tensor": 4}
 BF = jnp.bfloat16
 F32 = jnp.float32
 NT = (((1,), (1,)), ((), ()))
+SMEM = pl.BlockSpec(memory_space=pltpu.SMEM)
 VMEM = pl.BlockSpec(memory_space=pltpu.VMEM)
 TOK, QUARTER, HALF = 512, 896, 448
 DOCS, SLOTS, MEMBERS, SHARE = 128, 256, 512, 128
 
 
-def params():
-    return pltpu.CompilerParams(vmem_limit_bytes=40 * 1024 * 1024)
+def params(mib=20):
+    return pltpu.CompilerParams(vmem_limit_bytes=mib * 1024 * 1024)
 
 
 def cost(flops, nbytes):
     return pl.CostEstimate(flops=flops, bytes_accessed=nbytes, transcendentals=0)
 
 
-def shift(value, axis, step):
-    size = SIZES[axis]
-    return lax.ppermute(value, axis, [(i, (i + step) % size) for i in range(size)])
+def device(z, y, core, x):
+    return ((z * 8 + y) * 2 + core) * 4 + x
+
+
+def placed(core, ring, line):
+    return (ring, line) if core == 0 else (line, ring)
+
+
+def grid():
+    return [(z, y, c, x) for z in range(8) for y in range(8) for c in range(2) for x in range(4)]
 
 
 def spread(flip):
     pairs = []
-    for z in range(8):
-        for y in range(8):
-            for core in range(2):
-                for x in range(4):
-                    source = ((z * 8 + y) * 2 + core) * 4 + x
-                    target = (((2 * x + z % 2) * 8 + y) * 2 + (core ^ flip)) * 4 + z // 2
-                    pairs.append((source, target))
+    for z, y, core, x in grid():
+        to = core ^ flip
+        to_z, to_y = placed(to, 2 * x + z % 2, y)
+        pairs.append((device(z, y, core, x), device(to_z, to_y, to, z // 2)))
     return pairs
 
 
-def project_kernel(ctx, weight, res, hidden, squares, total):
+def groups(along):
+    found = []
+    for core in range(2):
+        for x in range(4):
+            for other in range(8):
+                over_z = (along == "ring") == (core == 0)
+                found.append(
+                    [device(i, other, core, x) if over_z else device(other, i, core, x) for i in range(8)]
+                )
+    return found
+
+
+def pair(value, turn):
+    pairs = []
+    for z, y, core, x in grid():
+        pairs.append((device(z, y, core, x), device(z, y, core, x ^ (1 if core == turn else 3))))
+    return lax.ppermute(value, ALL, pairs)
+
+
+def core_swap(value):
+    return lax.ppermute(value, ALL, [(at, at ^ 4) for at in range(512)])
+
+
+def pack_kernel(place, context, residual, small, near, side):
+    near[0:TOK, :] = context[...]
+    side[0:TOK, :] = context[...]
+    for out, row, target in ((near, 512, 1), (near, 640, 3), (side, 512, 2)):
+        start = pl.multiple_of(place[target] * QUARTER, 128)
+        out[row : row + 128, :] = residual[:, pl.ds(start, QUARTER)]
+    near[768:784, :] = small[...]
+    side[640:656, :] = small[...]
+
+
+def project_kernel(place, context, near, side, far, weight, res, hidden, squares):
     step = pl.program_id(0)
-    half = lax.rem(step, 2)
-    product = lax.dot_general(ctx[0], weight[...], NT, preferred_element_type=F32)
-
-    @pl.when(step < 2)
+    for index, piece in enumerate((context, near, side, far)):
+
+        @pl.when(step == index)
+        def _(index=index, piece=piece):
+            product = lax.dot_general(piece[0:TOK, :], weight[...], NT, preferred_element_type=F32)
+            if index == 0:
+                hidden[...] = product
+            else:
+                hidden[...] += product
+
+    @pl.when(step == 3)
     def _():
-        total[half] = product
-
-    @pl.when(step >= 2)
-    def _():
-        total[half] += product
-
-    @pl.when(step == 7)
-    def _():
+        tails = (res[...], near[512:640, :], side[512:640, :], far[640:768, :])
+        for index, tail in enumerate(tails):
+            rows = pl.ds(pl.multiple_of(place[index] * 128, 128), 128)
+            hidden[rows, :] += tail.astype(F32)
+        squares[...] = jnp.zeros_like(squares)
         for pack in range(4):
-            rows = pl.ds(pack * 128, 128)
-            value = jnp.concatenate([total[0, rows, :], total[1, rows, :]], axis=1)
-            value = value + res[rows, :].astype(F32)
-            hidden[rows, :] = value
+            value = hidden[pl.ds(pack * 128, 128), :]
             sq = value * value
             part = sq[:, 0:128]
             for tile in range(1, 7):
                 part = part + sq[:, tile * 128 : tile * 128 + 128]
             squares[pl.ds(pack, 1), :] = jnp.sum(part.T, axis=0, keepdims=True)
-        squares[pl.ds(4, 4), :] = jnp.zeros((4, 128), F32)
 
 
 def pool_kernel(hidden, gain, pool, inverse, total, slots, squares):
@@ -120,50 +157,54 @@
     z, y = lax.axis_index("z"), lax.axis_index("y")
     core, x = lax.axis_index("core"), lax.axis_index("tensor")
 
+    first = core == 0
+    near_x = jnp.where(first, x ^ 1, x ^ 3)
+    side_x = jnp.where(first, x ^ 3, x ^ 1)
+    far_x = x ^ 2
+    place = jnp.stack([x, near_x, side_x, far_x]).astype(jnp.int32)
+
     weight = out_weight.T
     keep = lax.ppermute(weight, ALL, spread(0))
     cross = lax.ppermute(weight, ALL, spread(1))
     block = jnp.concatenate(
-        [jnp.where(core == 0, keep, cross), jnp.where(core == 0, cross, keep)], axis=0
+        [jnp.where(first, keep, cross), jnp.where(first, cross, keep)], axis=0
     )
-    context, residual, doc_lengths, block = lax.optimization_barrier(
-        (context, residual, doc_lengths, block)
-    )
-    plane = lax.all_gather(block, ("z", "y"), axis=0, tiled=True)
-
-    ctx_down, ctx_up = shift(context, "tensor", 1), shift(context, "tensor", -1)
-
-    res_parts = [
-        lax.dynamic_slice(residual, (0, lax.rem(x + step, 4) * QUARTER), (128, QUARTER))
-        for step in range(4)
-    ]
-    res_recv = [
-        res_parts[0],
-        shift(res_parts[1], "tensor", 1),
-        shift(res_parts[2], "tensor", 2),
-        shift(res_parts[3], "tensor", 3),
-    ]
-    res = jnp.zeros((TOK, QUARTER), BF)
-    for step in range(4):
-        res = lax.dynamic_update_slice(res, res_recv[step], (lax.rem(x - step + 4, 4) * 128, 0))
 
     resident = members[0]
     resident_f = resident.astype(F32)
-    partial_sq = jnp.sum(resident_f * resident_f, axis=-1).reshape(4, 128)
-    lens_rows = jnp.zeros((4, 128), F32)
-    lens_rows = lax.dynamic_update_slice(lens_rows, doc_lengths.astype(F32), (x, 0))
-    small = lax.psum(jnp.concatenate([partial_sq, lens_rows], axis=0), "tensor")
-    small, res = lax.optimization_barrier((small, res))
-    member_sq, lens = small[:4], small[4:, :32]
-
-    far_a = shift(ctx_down[: TOK // 2], "tensor", 1)
-    far_b = shift(ctx_up[TOK // 2 :], "tensor", -1)
-    ctx = jnp.zeros((4, TOK, QUARTER), BF)
-    ctx = lax.dynamic_update_slice(ctx, context[None], (x, 0, 0))
-    ctx = lax.dynamic_update_slice(ctx, ctx_down[None], (lax.rem(x + 3, 4), 0, 0))
-    ctx = lax.dynamic_update_slice(ctx, ctx_up[None], (lax.rem(x + 1, 4), 0, 0))
-    ctx = lax.dynamic_update_slice(ctx, far_a[None], (lax.rem(x + 2, 4), 0, 0))
-    ctx = lax.dynamic_update_slice(ctx, far_b[None], (lax.rem(x + 2, 4), TOK // 2, 0))
+    partial_sq = jnp.sum(resident_f * resident_f, axis=-1).astype(BF)
+    small = jnp.concatenate(
+        [partial_sq.reshape(4, 128), jnp.pad(doc_lengths.astype(BF), ((0, 0), (0, 96)))], axis=0
+    )
+    small = jnp.pad(small, ((0, 11), (0, QUARTER - 128)))
+    to_near, to_side = pl.pallas_call(
+        pack_kernel,
+        out_shape=(
+            jax.ShapeDtypeStruct((784, QUARTER), BF),
+            jax.ShapeDtypeStruct((656, QUARTER), BF),
+        ),
+        in_specs=[SMEM] + [pl.BlockSpec()] * 3,
+        out_specs=(pl.BlockSpec(), pl.BlockSpec()),
+        compiler_params=params(56),
+        cost_estimate=cost(0, 6_000_000),
+        name="pack",
+    )(place, context, residual, small)
+
+    block, to_near = lax.optimization_barrier((block, to_near))
+    near = pair(to_near, 0)
+    plane = lax.all_to_all(
+        jnp.broadcast_to(block[None], (8, 56, QUARTER)), ALL, 0, 0,
+        axis_index_groups=groups("line"), tiled=True,
+    ).reshape(HALF, QUARTER)
+    plane, near, to_side = lax.optimization_barrier((plane, near, to_side))
+    plane = lax.all_gather(plane, ALL, axis=0, axis_index_groups=groups("ring"), tiled=True)
+    far, side = pair(near, 1), pair(to_side, 1)
+
+    tails = [(x, small), (near_x, near[-16:]), (side_x, side[-16:]), (far_x, far[-16:])]
+    member_sq = sum((tail[:4, :128].astype(F32) for _, tail in tails[1:]), small[:4, :128].astype(F32))
+    lens = jnp.zeros((4, 32), F32)
+    for at, tail in tails:
+        lens = lax.dynamic_update_slice(lens, tail[4:5, :32].astype(F32), (at, 0))
 
     cluster_ids = jnp.arange(owner_map.shape[0], dtype=jnp.int32)
     matches = doc_cluster[:, 0][:, None] == cluster_ids[None, :]
@@ -197,27 +238,33 @@
     member_ids = jnp.arange(MEMBERS, dtype=jnp.int32).reshape(4, 128)
     factor = jnp.where(member_ids < own_count, lax.rsqrt(member_sq / 3584.0 + 1e-06), 0.0)
 
+    res = lax.dynamic_slice(residual, (0, x * QUARTER), (128, QUARTER))
     hidden, squares = pl.pallas_call(
         project_kernel,
         out_shape=(
             jax.ShapeDtypeStruct((TOK, QUARTER), F32),
             jax.ShapeDtypeStruct((8, 128), F32),
         ),
-        grid=(8,),
-        in_specs=[
-            pl.BlockSpec((1, TOK, QUARTER), lambda i: (lax.div(i, 2), 0, 0)),
-            pl.BlockSpec((HALF, QUARTER), lambda i: (i, 0)),
-            pl.BlockSpec((TOK, QUARTER), lambda i: (0, 0)),
-        ],
-        out_specs=(
-            pl.BlockSpec((TOK, QUARTER), lambda i: (0, 0)),
-            pl.BlockSpec((8, 128), lambda i: (0, 0)),
-        ),
-        scratch_shapes=[pltpu.VMEM((2, TOK, HALF), F32)],
-        compiler_params=params(),
+        grid_spec=pltpu.PrefetchScalarGridSpec(
+            num_scalar_prefetch=1,
+            grid=(4,),
+            in_specs=[
+                pl.BlockSpec((TOK, QUARTER), lambda i, place: (0, 0)),
+                pl.BlockSpec((784, QUARTER), lambda i, place: (0, 0)),
+                pl.BlockSpec((656, QUARTER), lambda i, place: (0, 0)),
+                pl.BlockSpec((784, QUARTER), lambda i, place: (0, 0)),
+                pl.BlockSpec((QUARTER, QUARTER), lambda i, place: (place[i], 0)),
+                pl.BlockSpec((128, QUARTER), lambda i, place: (0, 0)),
+            ],
+            out_specs=(
+                pl.BlockSpec((TOK, QUARTER), lambda i, place: (0, 0)),
+                pl.BlockSpec((8, 128), lambda i, place: (0, 0)),
+            ),
+        ),
+        compiler_params=params(56),
         cost_estimate=cost(2 * TOK * QUARTER * 3584, 13_000_000),
         name="project",
-    )(ctx, plane, res)
+    )(place, context, near, side, far, plane, res)
 
     slots, doc_sq = pl.pallas_call(
         pool_kernel,

time: 221 us -> 208 us (0.941)
  blocking collectives: 48.8 us -> 29.4 us
  waiting for transfers between devices: 65.2 us -> 77.7 us
  local copies, waits for them, and re-layouts: 17.6 us -> 8.2 us
  Pallas kernels: 11.7 us -> 15.9 us
  starting transfers between devices: 56.4 us -> 53.4 us
  other arithmetic: 5.27 us -> 7.89 us
    ppermute x7 -> x3, waiting for transfers between devices: 6.69 us -> 28.3 us  [pair(): return lax.ppermute(value, ALL, pairs)]
    psum x1 -> x0, blocking collectives: 19.3 us -> none  [body(): small = lax.psum(jnp.concatenate([partial_sq, lens_rows], axis=0), 'tensor')]
    ppermute x7 -> x3, starting transfers between devices: 27.9 us -> 11 us  [pair(): return lax.ppermute(value, ALL, pairs)]
    all_gather x1, waiting for transfers between devices: 28 us -> 13.6 us  [body(): lax.all_gather(plane, ALL, axis=0, axis_index_groups=groups('ring'), tile...]
    all_to_all x0 -> x1, waiting for transfers between devices: none -> 14.3 us  [body(): lax.all_to_all(jnp.broadcast_to(block[None], (8, 56, QUARTER)), ALL, 0, 0...]
    all_to_all x0 -> x1, starting transfers between devices: none -> 10.6 us  [body(): lax.all_to_all(jnp.broadcast_to(block[None], (8, 56, QUARTER)), ALL, 0, 0...]
    ppermute x1, waiting for transfers between devices: 7.95 us -> 0.01 us  [body(): cross = lax.ppermute(weight, ALL, spread(1))]
    dynamic_update_slice x9 -> x4, local copies, waits for them, and re-layouts: 7.77 us -> 0.13 us  [body(): lens = lax.dynamic_update_slice(lens, tail[4:5, :32].astype(F32), (at, 0))]
  transfers between devices with their start and end apart: 12 -> 9, of which waited for: 7 -> 6; matrix products, arithmetic and copies ran while one was open for 8% -> 6% of each run, Pallas kernels for 0% -> 2%
where the time goes in v5:
time: 208 us; the launch traced here: 207 us
  waiting for transfers between devices  77.7 us (37%)
  starting transfers between devices  53.4 us (26%)
  blocking collectives  29.4 us (14%)
  Pallas kernels  15.9 us (8%)
  between operations  14.3 us (7%)
  local copies, waits for them, and re-layouts  8.2 us (4%)
  other arithmetic  7.89 us (4%)
    ppermute x3, waiting for transfers between devices, pair(): return lax.ppermute(value, ALL, pairs)  28.3 us
    all_to_all x1, waiting for transfers between devices, body(): lax.all_to_all(partial, ALL, split_axis=0, concat_axis=0, tiled=True)  15.5 us
    all_to_all x1, waiting for transfers between devices, body(): lax.all_to_all(jnp.broadcast_to(block[None], (8, 56, QUARTER)), ALL, 0, 0...  14.3 us
    all_gather x1, waiting for transfers between devices, body(): lax.all_gather(plane, ALL, axis=0, axis_index_groups=groups('ring'), tile...  13.6 us
    all_to_all x1, starting transfers between devices, body(): lax.all_to_all(slots.reshape(DOCS, 2, QUARTER), DP, split_axis=0, concat_...  11.4 us
    ppermute x3, starting transfers between devices, pair(): return lax.ppermute(value, ALL, pairs)  11 us
    all_to_all x1, starting transfers between devices, body(): lax.all_to_all(partial, ALL, split_axis=0, concat_axis=0, tiled=True)  10.8 us
    pmax x1, blocking collectives, body(): return (scores, lax.pmax(best[0], 'tensor'))  10.6 us
  transfers between devices with their start and end apart: 9, of which 6 were waited for; matrix products, arithmetic and copies ran while one was open for 6% of the time, Pallas kernels for 2%

profile of v5, /device:TPU:2, one launch (start us, length us, event | category | flops | bytes accessed | tf_op | source)
XLA Modules:
  0.0 207.1 jit_solution(9051779419274956560)
XLA Ops:
  7.2 6.1 %collective-permute-start = (bf16[28,896]{1,0:T(8,128)(2,1)}, bf16[28,896]{1,0:T(8,128)(2,1)S(1)}, u32[]{:S(2)}, u32[]{:S(2)}) collective-permute-start(bf16[28,896]{1,0:T(8,128)(2,1)} %bitcast.26), channel_id=1, source_target_pairs={{0,0},{1,128},{2,256},{3,384},{4,4},{5,20},{6,36},{7,52},{8,8},{9,... | collective-permute-start | bytes 150536 | tf_op jit(solution)/shard_map/ppermute | solution.py:167
  13.2 3.4 %collective-permute-start.1 = (bf16[28,896]{1,0:T(8,128)(2,1)}, bf16[28,896]{1,0:T(8,128)(2,1)S(1)}, u32[]{:S(2)}, u32[]{:S(2)}) collective-permute-start(bf16[28,896]{1,0:T(8,128)(2,1)} %bitcast.27), channel_id=1, source_target_pairs={{0,4},{1,20},{2,36},{3,52},{4,0},{5,128},{6,256},{7,384},{8,68},{9... | collective-permute-start | bytes 150536 | tf_op jit(solution)/shard_map/ppermute | solution.py:168
  17.3 1.4 multiply_reduce_fusion
  20.0 3.2 %pack.1 = (bf16[784,896]{1,0:T(8,128)(2,1)}, bf16[656,896]{1,0:T(8,128)(2,1)}) custom-call(s32[4]{0:T(128)} %pad_add_fusion.place, bf16[512,896]{1,0:T(8,128)(2,1)} %context.3, bf16[128,3584]{1,0:T(8,128)(2,1)} %residual.1, bf16[16,896]{1,0:T(8,128)(2,1)} %pad.9.small), custom_call_target="tpu_custom_call" | custom-call | bytes 6000000 | tf_op jit(solution)/shard_map/pack/pallas_call | solution.py:180
  23.2 1.0 broadcast_in_dim.89
  24.2 10.6 %all-to-all-start = ((bf16[8,56,896]{2,1,0:T(8,128)(2,1)}), bf16[8,56,896]{2,1,0:T(8,128)(2,1)S(1)}, u32[]{:S(2)}, u32[]{:S(2)}) async-start(bf16[8,56,896]{2,1,0:T(8,128)(2,1)} %broadcast_in_dim.89), calls=%async_computation | async-start | bytes 1605632 | tf_op jit(solution)/shard_map/all_to_all | solution.py:195
  34.9 1.9 collective-permute-start.2
  36.8 14.3 %all-to-all-done = bf16[8,56,896]{2,1,0:T(8,128)(2,1)S(1)} async-done(((bf16[8,56,896]{2,1,0:T(8,128)(2,1)}), bf16[8,56,896]{2,1,0:T(8,128)(2,1)S(1)}, u32[]{:S(2)}, u32[]{:S(2)}) %all-to-all-start) | async-done | bytes 802848 | tf_op jit(solution)/shard_map/all_to_all | solution.py:195
  51.1 4.3 %collective-permute-done.2.near = bf16[784,896]{1,0:T(8,128)(2,1)} collective-permute-done((bf16[784,896]{1,0:T(8,128)(2,1)S(1)}, bf16[784,896]{1,0:T(8,128)(2,1)}, u32[]{:S(2)}, u32[]{:S(2)}) %collective-permute-start.2) | collective-permute-done | bytes 1404960 | tf_op jit(solution)/shard_map/ppermute | solution.py:64
  55.5 7.2 %collective-permute-start.4 = (bf16[784,896]{1,0:T(8,128)(2,1)}, bf16[784,896]{1,0:T(8,128)(2,1)}, u32[]{:S(2)}, u32[]{:S(2)}) collective-permute-start(bf16[784,896]{1,0:T(8,128)(2,1)} %collective-permute-done.2.near), channel_id=1, source_target_pairs={{0,3},{1,2},{2,1},{3,0},{4,5},{5,4},{6,7},{7,6},{8,11},{9,10},{10,... | collective-permute-start | bytes 4214792 | tf_op jit(solution)/shard_map/ppermute | solution.py:64
  62.7 1.9 collective-permute-start.3
  64.7 0.8 dynamic_slice.7
  65.9 1.7 constant_dynamic-slice_fusion.res
  67.5 0.7 slice_convert_fusion.2
  68.2 23.9 %collective-permute-done.3.side = bf16[656,896]{1,0:T(8,128)(2,1)} collective-permute-done((bf16[656,896]{1,0:T(8,128)(2,1)S(1)}, bf16[656,896]{1,0:T(8,128)(2,1)}, u32[]{:S(2)}, u32[]{:S(2)}) %collective-permute-start.3) | collective-permute-done | bytes 1175584 | tf_op jit(solution)/shard_map/ppermute | solution.py:64
  92.2 0.7 slice_convert_fusion.1
  92.9 0.7 slice_convert_fusion
  94.6 13.6 %all-gather.2.cloned.1.call-done.weight = bf16[3584,896]{1,0:T(8,128)(2,1)} async-done(((bf16[448,896]{1,0:T(8,128)(2,1)}), bf16[3584,896]{1,0:T(8,128)(2,1)}) %all-gather.2.cloned.1.call-update) | async-done | bytes 6422544 | tf_op jit(solution)/shard_map/all_gather | solution.py:200
  108.2 10.4 %project.1 = (f32[512,896]{1,0:T(8,128)}, f32[8,128]{1,0:T(8,128)}) custom-call(s32[4]{0:T(128)} %pad_add_fusion.place, bf16[512,896]{1,0:T(8,128)(2,1)} %context.3, bf16[784,896]{1,0:T(8,128)(2,1)} %collective-permute-done.2.near, bf16[656,896]{1,0:T(8,128)(2,1)} %collective-permute-done.3.side, bf16[784,896]{1,0:T(8,128)(2,1)} %collective-permute-done.4.far, ...), custom_call_target="tpu_custom_call" | custom-call | flops 3288334336 | bytes 13000000 | tf_op jit(solution)/shard_map/project/pallas_call | solution.py:242
  118.6 8.7 %psum.14.total = f32[8,128]{1,0:T(8,128)S(1)} all-reduce(f32[8,128]{1,0:T(8,128)} %get-tuple-element.23), channel_id=1, replica_groups=mesh['z'=8,'y'=8,'core'=2,'tensor'=4] {'tensor'}, use_global_device_ids=true, to_apply=%region_5.6 | all-reduce | flops 1024 | bytes 8192 | tf_op jit(solution)/shard_map/psum | solution.py:280
  127.4 1.5 copy-done.1
  128.9 0.8 pool.1
  129.7 0.9 reshape.95
  130.7 11.4 %all-to-all-start.1 = ((bf16[128,2,896]{2,1,0:T(2,128)(2,1)}), bf16[128,2,896]{2,1,0:T(2,128)(2,1)S(1)}, u32[]{:S(2)}, u32[]{:S(2)}) async-start(bf16[128,2,896]{2,1,0:T(2,128)(2,1)} %reshape.95), calls=%async_computation.1 | async-start | bytes 917504 | tf_op jit(solution)/shard_map/all_to_all | solution.py:282
  143.0 1.4 rsqrt_select_fusion.factor
  144.4 10.1 %psum.15 = f32[8,128]{1,0:T(8,128)S(1)} all-reduce(f32[8,128]{1,0:T(8,128)S(1)} %get-tuple-element.25), channel_id=1, replica_groups=mesh['z'=8,'y'=8,'core'=2,'tensor'=4] {'tensor'}, use_global_device_ids=true, to_apply=%region_7.8 | all-reduce | flops 1024 | bytes 8192 | tf_op jit(solution)/shard_map/psum | solution.py:286
  154.5 6.0 %all-to-all-done.1 = bf16[128,2,896]{2,1,0:T(2,128)(2,1)S(1)} async-done(((bf16[128,2,896]{2,1,0:T(2,128)(2,1)}), bf16[128,2,896]{2,1,0:T(2,128)(2,1)S(1)}, u32[]{:S(2)}, u32[]{:S(2)}) %all-to-all-start.1) | async-done | bytes 458784 | tf_op jit(solution)/shard_map/all_to_all | solution.py:282
  161.4 0.9 copy.12
  162.3 10.8 %all-to-all-start.2 = ((bf16[512,2,128]{2,1,0:T(2,128)(2,1)}), bf16[512,2,128]{2,1,0:T(2,128)(2,1)S(1)}, u32[]{:S(2)}, u32[]{:S(2)}) async-start(bf16[512,2,128]{2,1,0:T(2,128)(2,1)} %bitcast.10), calls=%async_computation.2 | async-start | bytes 524288 | tf_op jit(solution)/shard_map/all_to_all | solution.py:301
  173.2 15.5 %all-to-all-done.2 = bf16[512,2,128]{2,1,0:T(2,128)(2,1)S(1)} async-done(((bf16[512,2,128]{2,1,0:T(2,128)(2,1)}), bf16[512,2,128]{2,1,0:T(2,128)(2,1)S(1)}, u32[]{:S(2)}, u32[]{:S(2)}) %all-to-all-start.2) | async-done | bytes 262176 | tf_op jit(solution)/shard_map/all_to_all | solution.py:301
  188.8 0.9 home.1
  189.6 10.6 %pmax.7 = f32[128]{0:T(128)} all-reduce(f32[128]{0:T(128)S(1)} %slice_bitcast_fusion.1), channel_id=1, replica_groups=mesh['z'=8,'y'=8,'core'=2,'tensor'=4] {'tensor'}, use_global_device_ids=true, to_apply=%region_10.11 | all-reduce | flops 128 | bytes 1024 | tf_op jit(solution)/shard_map/pmax | solution.py:315
  (59 shorter events, 5.5 us)
Async XLA Ops:
  7.2 16.0 %collective-permute-start = (bf16[28,896]{1,0:T(8,128)(2,1)}, bf16[28,896]{1,0:T(8,128)(2,1)S(1)}, u32[]{:S(2)}, u32[]{:S(2)}) collective-permute-start(bf16[28,896]{1,0:T(8,128)(2,1)} %bitcast.26), channel_id=1, source_target_pairs={{0,0},{1,128},{2,256},{3,384},{4,4},{5,20},{6,36},{7,52},{8,8},{9,... | collective-permute-start | bytes 150536 | tf_op jit(solution)/shard_map/ppermute | solution.py:167
  13.2 9.9 %collective-permute-start.1 = (bf16[28,896]{1,0:T(8,128)(2,1)}, bf16[28,896]{1,0:T(8,128)(2,1)S(1)}, u32[]{:S(2)}, u32[]{:S(2)}) collective-permute-start(bf16[28,896]{1,0:T(8,128)(2,1)} %bitcast.27), channel_id=1, source_target_pairs={{0,4},{1,20},{2,36},{3,52},{4,0},{5,128},{6,256},{7,384},{8,68},{9... | collective-permute-start | bytes 150536 | tf_op jit(solution)/shard_map/ppermute | solution.py:168
  23.2 11.7 %copy-start.6 = (bf16[784,896]{1,0:T(8,128)(2,1)S(1)}, bf16[784,896]{1,0:T(8,128)(2,1)}, u32[]{:S(2)}) copy-start(bf16[784,896]{1,0:T(8,128)(2,1)} %get-tuple-element.17) | copy-start | bytes 4214788
  24.2 38.5 %copy-start.7 = (bf16[656,896]{1,0:T(8,128)(2,1)S(1)}, bf16[656,896]{1,0:T(8,128)(2,1)}, u32[]{:S(2)}) copy-start(bf16[656,896]{1,0:T(8,128)(2,1)} %get-tuple-element.20) | copy-start | bytes 3526660
  24.2 41.3 %copy-start.3 = (s32[128]{0:T(128)S(1)}, s32[128]{0:T(128)}, u32[]{:S(2)}) copy-start(s32[128]{0:T(128)} %param.17) | copy-start | bytes 1540
  24.2 41.3 %copy-start.4 = (s32[128]{0:T(128)S(1)}, s32[128]{0:T(128)}, u32[]{:S(2)}) copy-start(s32[128]{0:T(128)} %param.16) | copy-start | bytes 1540
  24.2 41.3 %copy-start.5 = (s32[128,1]{0,1:T(1,128)S(1)}, s32[128,1]{0,1:T(1,128)}, u32[]{:S(2)}) copy-start(s32[128,1]{0,1:T(1,128)} %param.15) | copy-start | bytes 1540
  24.2 26.9 %all-to-all-start = ((bf16[8,56,896]{2,1,0:T(8,128)(2,1)}), bf16[8,56,896]{2,1,0:T(8,128)(2,1)S(1)}, u32[]{:S(2)}, u32[]{:S(2)}) async-start(bf16[8,56,896]{2,1,0:T(8,128)(2,1)} %broadcast_in_dim.89), calls=%async_computation | async-start | bytes 1605632 | tf_op jit(solution)/shard_map/all_to_all | solution.py:195
  34.8 73.4 %all-gather.2.cloned.1.call-start = ((), (), s32[]{:S(2)}) async-start(), calls=%async_computation.3 | async-start | bytes 7225344 | tf_op jit(solution)/shard_map/all_gather | solution.py:200
  34.9 20.6 %collective-permute-start.2 = (bf16[784,896]{1,0:T(8,128)(2,1)S(1)}, bf16[784,896]{1,0:T(8,128)(2,1)}, u32[]{:S(2)}, u32[]{:S(2)}) collective-permute-start(bf16[784,896]{1,0:T(8,128)(2,1)S(1)} %copy-done.6), channel_id=1, source_target_pairs={{0,1},{1,0},{2,3},{3,2},{4,7},{5,6},{6,5},{7,4},{8,9},{9,8},{10,11... | collective-permute-start | bytes 4214792 | tf_op jit(solution)/shard_map/ppermute | solution.py:64
  51.1 4.4 %copy-start.2 = (bf16[8,56,896]{2,1,0:T(8,128)(2,1)}, bf16[8,56,896]{2,1,0:T(8,128)(2,1)S(1)}, u32[]{:S(2)}) copy-start(bf16[8,56,896]{2,1,0:T(8,128)(2,1)S(1)} %all-to-all-done) | copy-start | bytes 2408452
  55.5 37.4 %collective-permute-start.4 = (bf16[784,896]{1,0:T(8,128)(2,1)}, bf16[784,896]{1,0:T(8,128)(2,1)}, u32[]{:S(2)}, u32[]{:S(2)}) collective-permute-start(bf16[784,896]{1,0:T(8,128)(2,1)} %collective-permute-done.2.near), channel_id=1, source_target_pairs={{0,3},{1,2},{2,1},{3,0},{4,5},{5,4},{6,7},{7,6},{8,11},{9,10},{10,... | collective-permute-start | bytes 4214792 | tf_op jit(solution)/shard_map/ppermute | solution.py:64
  62.7 29.5 %collective-permute-start.3 = (bf16[656,896]{1,0:T(8,128)(2,1)S(1)}, bf16[656,896]{1,0:T(8,128)(2,1)}, u32[]{:S(2)}, u32[]{:S(2)}) collective-permute-start(bf16[656,896]{1,0:T(8,128)(2,1)S(1)} %copy-done.7), channel_id=1, source_target_pairs={{0,3},{1,2},{2,1},{3,0},{4,5},{5,4},{6,7},{7,6},{8,11},{9,10},{10,... | collective-permute-start | bytes 3526664 | tf_op jit(solution)/shard_map/ppermute | solution.py:64
  127.4 1.5 copy-start.1
  129.7 30.9 %copy-start = (bf16[1,512,896]{2,1,0:T(8,128)(2,1)S(1)}, bf16[1,512,896]{2,1,0:T(8,128)(2,1)}, u32[]{:S(2)}) copy-start(bf16[1,512,896]{2,1,0:T(8,128)(2,1)} %param.13) | copy-start | bytes 2752516
  130.7 29.8 %all-to-all-start.1 = ((bf16[128,2,896]{2,1,0:T(2,128)(2,1)}), bf16[128,2,896]{2,1,0:T(2,128)(2,1)S(1)}, u32[]{:S(2)}, u32[]{:S(2)}) async-start(bf16[128,2,896]{2,1,0:T(2,128)(2,1)} %reshape.95), calls=%async_computation.1 | async-start | bytes 917504 | tf_op jit(solution)/shard_map/all_to_all | solution.py:282
  162.3 26.4 %all-to-all-start.2 = ((bf16[512,2,128]{2,1,0:T(2,128)(2,1)}), bf16[512,2,128]{2,1,0:T(2,128)(2,1)S(1)}, u32[]{:S(2)}, u32[]{:S(2)}) async-start(bf16[512,2,128]{2,1,0:T(2,128)(2,1)} %bitcast.10), calls=%async_computation.2 | async-start | bytes 524288 | tf_op jit(solution)/shard_map/all_to_all | solution.py:301
Sparse Core Ops, SparseCore 0:
  55.6 52.5 all-gather.1

commit v6 on v5

--- a/solution.py
+++ b/solution.py
@@ -78,32 +78,51 @@
     side[640:656, :] = small[...]
 
 
-def project_kernel(place, context, near, side, far, weight, res, hidden, squares):
-    step = pl.program_id(0)
+def project_kernel(
+    place, context, near, side, far, weight, res, hidden, squares, ctx, tails, blocks, sems
+):
+    def fetch(source, target, at):
+        return pltpu.make_async_copy(source, target, sems.at[at])
+
+    copies = []
     for index, piece in enumerate((context, near, side, far)):
-
-        @pl.when(step == index)
-        def _(index=index, piece=piece):
-            product = lax.dot_general(piece[0:TOK, :], weight[...], NT, preferred_element_type=F32)
-            if index == 0:
-                hidden[...] = product
-            else:
-                hidden[...] += product
-
-    @pl.when(step == 3)
-    def _():
-        tails = (res[...], near[512:640, :], side[512:640, :], far[640:768, :])
-        for index, tail in enumerate(tails):
-            rows = pl.ds(pl.multiple_of(place[index] * 128, 128), 128)
-            hidden[rows, :] += tail.astype(F32)
-        squares[...] = jnp.zeros_like(squares)
-        for pack in range(4):
-            value = hidden[pl.ds(pack * 128, 128), :]
-            sq = value * value
-            part = sq[:, 0:128]
-            for tile in range(1, 7):
-                part = part + sq[:, tile * 128 : tile * 128 + 128]
-            squares[pl.ds(pack, 1), :] = jnp.sum(part.T, axis=0, keepdims=True)
+        start = pl.multiple_of(place[index] * QUARTER, QUARTER)
+        copies.append(
+            (
+                fetch(piece.at[pl.ds(0, TOK), :], ctx.at[index], 2 * index),
+                fetch(weight.at[pl.ds(start, QUARTER), :], blocks.at[index], 2 * index + 1),
+            )
+        )
+    ends = [
+        fetch(piece.at[pl.ds(row, 128), :], tails.at[index], 8 + index)
+        for index, (piece, row) in enumerate(((res, 0), (near, 512), (side, 512), (far, 640)))
+    ]
+    for pair_of in copies:
+        for copy in pair_of:
+            copy.start()
+    for copy in ends:
+        copy.start()
+    for index in range(4):
+        for copy in copies[index]:
+            copy.wait()
+        product = lax.dot_general(ctx[index], blocks[index], NT, preferred_element_type=F32)
+        if index == 0:
+            hidden[...] = product
+        else:
+            hidden[...] += product
+    for copy in ends:
+        copy.wait()
+    squares[...] = jnp.zeros_like(squares)
+    for index in range(4):
+        at = place[index]
+        rows = pl.ds(pl.multiple_of(at * 128, 128), 128)
+        value = hidden[rows, :] + tails[index].astype(F32)
+        hidden[rows, :] = value
+        sq = value * value
+        part = sq[:, 0:128]
+        for tile in range(1, 7):
+            part = part + sq[:, tile * 128 : tile * 128 + 128]
+        squares[pl.ds(at, 1), :] = jnp.sum(part.T, axis=0, keepdims=True)
 
 
 def pool_kernel(hidden, gain, pool, inverse, total, slots, squares):
@@ -183,22 +202,21 @@
             jax.ShapeDtypeStruct((784, QUARTER), BF),
             jax.ShapeDtypeStruct((656, QUARTER), BF),
         ),
-        in_specs=[SMEM] + [pl.BlockSpec()] * 3,
+        in_specs=[SMEM] + [VMEM] * 3,
         out_specs=(pl.BlockSpec(), pl.BlockSpec()),
-        compiler_params=params(56),
+        compiler_params=params(),
         cost_estimate=cost(0, 6_000_000),
         name="pack",
     )(place, context, residual, small)
 
-    block, to_near = lax.optimization_barrier((block, to_near))
-    near = pair(to_near, 0)
+    near, side = pair(to_near, 0), pair(to_side, 1)
     plane = lax.all_to_all(
         jnp.broadcast_to(block[None], (8, 56, QUARTER)), ALL, 0, 0,
         axis_index_groups=groups("line"), tiled=True,
     ).reshape(HALF, QUARTER)
-    plane, near, to_side = lax.optimization_barrier((plane, near, to_side))
+    plane, _, _ = lax.optimization_barrier((plane, to_near, to_side))
     plane = lax.all_gather(plane, ALL, axis=0, axis_index_groups=groups("ring"), tiled=True)
-    far, side = pair(near, 1), pair(to_side, 1)
+    far = pair(near, 1)
 
     tails = [(x, small), (near_x, near[-16:]), (side_x, side[-16:]), (far_x, far[-16:])]
     member_sq = sum((tail[:4, :128].astype(F32) for _, tail in tails[1:]), small[:4, :128].astype(F32))
@@ -245,23 +263,15 @@
             jax.ShapeDtypeStruct((TOK, QUARTER), F32),
             jax.ShapeDtypeStruct((8, 128), F32),
         ),
-        grid_spec=pltpu.PrefetchScalarGridSpec(
-            num_scalar_prefetch=1,
-            grid=(4,),
-            in_specs=[
-                pl.BlockSpec((TOK, QUARTER), lambda i, place: (0, 0)),
-                pl.BlockSpec((784, QUARTER), lambda i, place: (0, 0)),
-                pl.BlockSpec((656, QUARTER), lambda i, place: (0, 0)),
-                pl.BlockSpec((784, QUARTER), lambda i, place: (0, 0)),
-                pl.BlockSpec((QUARTER, QUARTER), lambda i, place: (place[i], 0)),
-                pl.BlockSpec((128, QUARTER), lambda i, place: (0, 0)),
-            ],
-            out_specs=(
-                pl.BlockSpec((TOK, QUARTER), lambda i, place: (0, 0)),
-                pl.BlockSpec((8, 128), lambda i, place: (0, 0)),
-            ),
-        ),
-        compiler_params=params(56),
+        in_specs=[SMEM] + [pl.BlockSpec(memory_space=pl.ANY)] * 6,
+        out_specs=(VMEM, VMEM),
+        scratch_shapes=[
+            pltpu.VMEM((4, TOK, QUARTER), BF),
+            pltpu.VMEM((4, 128, QUARTER), BF),
+            pltpu.VMEM((4, QUARTER, QUARTER), BF),
+            pltpu.SemaphoreType.DMA((12,)),
+        ],
+        compiler_params=params(54),
         cost_estimate=cost(2 * TOK * QUARTER * 3584, 13_000_000),
         name="project",
     )(place, context, near, side, far, plane, res)
@@ -274,7 +284,7 @@
         ),
         in_specs=[VMEM] * 5,
         out_specs=(VMEM, VMEM),
-        compiler_params=params(),
+        compiler_params=params(54),
         cost_estimate=cost(2 * SLOTS * TOK * QUARTER, 3_000_000),
         name="pool",
     )(hidden, gain_of(norm_gain, x), pool, inverse, lax.psum(squares, "tensor"))

time: 208 us -> 211 us (1.014)
  starting transfers between devices: 53.4 us -> 61.5 us
  waiting for transfers between devices: 77.7 us -> 71 us
  blocking collectives: 29.4 us -> 32.5 us
  other arithmetic: 7.89 us -> 5.47 us
    ppermute x3, starting transfers between devices: 11 us -> 27.2 us  [pair(): return lax.ppermute(value, ALL, pairs)]
    all_gather x1, waiting for transfers between devices: 13.6 us -> 0.01 us  [body(): lax.all_gather(plane, ALL, axis=0, axis_index_groups=groups('ring'), tile...]
    ppermute x1, waiting for transfers between devices: 0.01 us -> 6.34 us  [body(): cross = lax.ppermute(weight, ALL, spread(1))]
    all_to_all x1, starting transfers between devices: 11.4 us -> 6.17 us  [body(): lax.all_to_all(slots.reshape(DOCS, 2, QUARTER), DP, split_axis=0, concat_...]
    all_to_all x1, starting transfers between devices: 10.6 us -> 7.05 us  [body(): lax.all_to_all(jnp.broadcast_to(block[None], (8, 56, QUARTER)), ALL, 0, 0...]
    ppermute x3, waiting for transfers between devices: 28.3 us -> 30.9 us  [pair(): return lax.ppermute(value, ALL, pairs)]
    pallas_call x1, Pallas kernels: 3.15 us -> 0.73 us  [body(): pl.pallas_call(pack_kernel, out_shape=(jax.ShapeDtypeStruct((784, QUARTER...]
    psum x1, blocking collectives: 8.71 us -> 11.1 us  [body(): lax.psum(squares, 'tensor')]
  transfers between devices with their start and end apart: 9 -> 9, of which waited for: 6 -> 6; matrix products, arithmetic and copies ran while one was open for 6% -> 4% of each run, Pallas kernels for 2% -> 0%
where the time goes in v6:
time: 211 us; the launch traced here: 210 us
  waiting for transfers between devices  71 us (34%)
  starting transfers between devices  61.5 us (29%)
  blocking collectives  32.5 us (15%)
  Pallas kernels  14.5 us (7%)
  between operations  14.4 us (7%)
  local copies, waits for them, and re-layouts  9.5 us (5%)
  other arithmetic  5.47 us (3%)
    ppermute x3, waiting for transfers between devices, pair(): return lax.ppermute(value, ALL, pairs)  30.9 us
    ppermute x3, starting transfers between devices, pair(): return lax.ppermute(value, ALL, pairs)  27.2 us
    all_to_all x1, waiting for transfers between devices, body(): lax.all_to_all(partial, ALL, split_axis=0, concat_axis=0, tiled=True)  15.5 us
    all_to_all x1, waiting for transfers between devices, body(): lax.all_to_all(jnp.broadcast_to(block[None], (8, 56, QUARTER)), ALL, 0, 0...  13.1 us
    all_to_all x1, starting transfers between devices, body(): lax.all_to_all(partial, ALL, split_axis=0, concat_axis=0, tiled=True)  11.6 us
    psum x1, blocking collectives, body(): lax.psum(squares, 'tensor')  11.1 us
    psum x1, blocking collectives, body(): slot_sq = lax.psum(doc_sq, 'tensor')[:2].reshape(SLOTS)  11 us
    pmax x1, blocking collectives, body(): return (scores, lax.pmax(best[0], 'tensor'))  10.5 us
  transfers between devices with their start and end apart: 9, of which 6 were waited for; matrix products, arithmetic and copies ran while one was open for 4% of the time, Pallas kernels for 0%

profile of v6, /device:TPU:2, one launch (start us, length us, event | category | flops | bytes accessed | tf_op | source)
XLA Modules:
  0.0 209.8 jit_solution(15439741976326727340)
XLA Ops:
  7.2 6.1 %collective-permute-start.3 = (bf16[28,896]{1,0:T(8,128)(2,1)}, bf16[28,896]{1,0:T(8,128)(2,1)S(1)}, u32[]{:S(2)}, u32[]{:S(2)}) collective-permute-start(bf16[28,896]{1,0:T(8,128)(2,1)} %bitcast.25), channel_id=1, source_target_pairs={{0,0},{1,128},{2,256},{3,384},{4,4},{5,20},{6,36},{7,52},{8,8},{9,... | collective-permute-start | bytes 150536 | tf_op jit(solution)/shard_map/ppermute | solution.py:186
  13.2 3.4 %collective-permute-start.4 = (bf16[28,896]{1,0:T(8,128)(2,1)}, bf16[28,896]{1,0:T(8,128)(2,1)S(1)}, u32[]{:S(2)}, u32[]{:S(2)}) collective-permute-start(bf16[28,896]{1,0:T(8,128)(2,1)} %bitcast.26), channel_id=1, source_target_pairs={{0,4},{1,20},{2,36},{3,52},{4,0},{5,128},{6,256},{7,384},{8,68},{9... | collective-permute-start | bytes 150536 | tf_op jit(solution)/shard_map/ppermute | solution.py:187
  16.7 6.3 %collective-permute-done.4 = bf16[28,896]{1,0:T(8,128)(2,1)S(1)} collective-permute-done((bf16[28,896]{1,0:T(8,128)(2,1)}, bf16[28,896]{1,0:T(8,128)(2,1)S(1)}, u32[]{:S(2)}, u32[]{:S(2)}) %collective-permute-start.4) | collective-permute-done | bytes 50208 | tf_op jit(solution)/shard_map/ppermute | solution.py:187
  23.1 0.9 broadcast_in_dim.89
  24.0 7.0 %all-to-all-start = ((bf16[8,56,896]{2,1,0:T(8,128)(2,1)}), bf16[8,56,896]{2,1,0:T(8,128)(2,1)}, u32[]{:S(2)}, u32[]{:S(2)}) async-start(bf16[8,56,896]{2,1,0:T(8,128)(2,1)} %broadcast_in_dim.89), calls=%async_computation | async-start | bytes 1605632 | tf_op jit(solution)/shard_map/all_to_all | solution.py:213
  31.6 0.7 pack.1
  32.3 1.1 copy-done.4
  33.4 1.0 copy-done.5
  34.4 13.1 %all-to-all-done = bf16[8,56,896]{2,1,0:T(8,128)(2,1)} async-done(((bf16[8,56,896]{2,1,0:T(8,128)(2,1)}), bf16[8,56,896]{2,1,0:T(8,128)(2,1)}, u32[]{:S(2)}, u32[]{:S(2)}) %all-to-all-start) | async-done | bytes 802848 | tf_op jit(solution)/shard_map/all_to_all | solution.py:213
  47.5 1.9 collective-permute-start
  49.5 11.4 %collective-permute-start.1 = (bf16[656,896]{1,0:T(8,128)(2,1)}, bf16[656,896]{1,0:T(8,128)(2,1)}, u32[]{:S(2)}, u32[]{:S(2)}) collective-permute-start(bf16[656,896]{1,0:T(8,128)(2,1)} %copy-done.5), channel_id=1, source_target_pairs={{0,3},{1,2},{2,1},{3,0},{4,5},{5,4},{6,7},{7,6},{8,11},{9,10},{10,... | collective-permute-start | bytes 3526664 | tf_op jit(solution)/shard_map/ppermute | solution.py:64
  60.9 18.0 %collective-permute-done.near = bf16[784,896]{1,0:T(8,128)(2,1)} collective-permute-done((bf16[784,896]{1,0:T(8,128)(2,1)}, bf16[784,896]{1,0:T(8,128)(2,1)}, u32[]{:S(2)}, u32[]{:S(2)}) %collective-permute-start) | collective-permute-done | bytes 1404960 | tf_op jit(solution)/shard_map/ppermute | solution.py:64
  78.8 13.8 %collective-permute-start.2 = (bf16[784,896]{1,0:T(8,128)(2,1)}, bf16[784,896]{1,0:T(8,128)(2,1)}, u32[]{:S(2)}, u32[]{:S(2)}) collective-permute-start(bf16[784,896]{1,0:T(8,128)(2,1)} %collective-permute-done.near), channel_id=1, source_target_pairs={{0,3},{1,2},{2,1},{3,0},{4,5},{5,4},{6,7},{7,6},{8,11},{9,10},{10,... | collective-permute-start | bytes 4214792 | tf_op jit(solution)/shard_map/ppermute | solution.py:64
  92.7 0.8 dynamic_slice.7
  94.5 0.7 constant_dynamic-slice_fusion.res
  96.7 12.9 %collective-permute-done.2.far = bf16[784,896]{1,0:T(8,128)(2,1)} collective-permute-done((bf16[784,896]{1,0:T(8,128)(2,1)}, bf16[784,896]{1,0:T(8,128)(2,1)}, u32[]{:S(2)}, u32[]{:S(2)}) %collective-permute-start.2) | collective-permute-done | bytes 1404960 | tf_op jit(solution)/shard_map/ppermute | solution.py:64
  109.6 0.7 slice_convert_fusion
  111.0 1.0 convolution_convert_fusion.pool
  112.0 9.1 %project.1 = (f32[512,896]{1,0:T(8,128)}, f32[8,128]{1,0:T(8,128)}) custom-call(s32[4]{0:T(128)} %copy-done.3, bf16[512,896]{1,0:T(8,128)(2,1)} %context.3, bf16[784,896]{1,0:T(8,128)(2,1)} %collective-permute-done.near, bf16[656,896]{1,0:T(8,128)(2,1)} %collective-permute-done.1.side, bf16[784,896]{1,0:T(8,128)(2,1)} %collective-permute-done.2.far, ...), custom_call_target="tpu_custom_call" | custom-call | flops 3288334336 | bytes 13000000 | tf_op jit(solution)/shard_map/project/pallas_call | solution.py:260
  121.1 11.1 %psum.14.total = f32[8,128]{1,0:T(8,128)} all-reduce(f32[8,128]{1,0:T(8,128)} %get-tuple-element.15), channel_id=1, replica_groups=mesh['z'=8,'y'=8,'core'=2,'tensor'=4] {'tensor'}, use_global_device_ids=true, to_apply=%region_5.6 | all-reduce | flops 1024 | bytes 8192 | tf_op jit(solution)/shard_map/psum | solution.py:290
  132.2 0.7 broadcast_in_dim.96.inverse
  133.0 3.1 %pool.1 = (bf16[256,896]{1,0:T(8,128)(2,1)}, f32[8,128]{1,0:T(8,128)}) custom-call(f32[512,896]{1,0:T(8,128)} %get-tuple-element.14.hidden, f32[1,896]{1,0:T(1,128)} %reshape.94.gain, bf16[256,512]{1,0:T(8,128)(2,1)} %convolution_convert_fusion.pool, f32[256,128]{1,0:T(8,128)} %broadcast_in_dim.96.inverse, f32[8,128]{1,0:T(8,128)} %psum.14.total), custom_call_target="tpu_custom_call" | custom-call | flops 234881024 | bytes 3000000 | tf_op jit(solution)/shard_map/pool/pallas_call | solution.py:279
  136.1 2.0 reshape.95
  138.0 6.2 %all-to-all-start.1 = ((bf16[128,2,896]{2,1,0:T(2,128)(2,1)}), bf16[128,2,896]{2,1,0:T(2,128)(2,1)S(1)}, u32[]{:S(2)}, u32[]{:S(2)}) async-start(bf16[128,2,896]{2,1,0:T(2,128)(2,1)} %reshape.95), calls=%async_computation.1 | async-start | bytes 917504 | tf_op jit(solution)/shard_map/all_to_all | solution.py:292
  145.1 1.3 rsqrt_select_fusion.factor
  146.4 11.0 %psum.15 = f32[8,128]{1,0:T(8,128)S(1)} all-reduce(f32[8,128]{1,0:T(8,128)S(1)} %copy-done.6), channel_id=1, replica_groups=mesh['z'=8,'y'=8,'core'=2,'tensor'=4] {'tensor'}, use_global_device_ids=true, to_apply=%region_7.8 | all-reduce | flops 1024 | bytes 8192 | tf_op jit(solution)/shard_map/psum | solution.py:296
  157.4 5.1 %all-to-all-done.1 = bf16[128,2,896]{2,1,0:T(2,128)(2,1)S(1)} async-done(((bf16[128,2,896]{2,1,0:T(2,128)(2,1)}), bf16[128,2,896]{2,1,0:T(2,128)(2,1)S(1)}, u32[]{:S(2)}, u32[]{:S(2)}) %all-to-all-start.1) | async-done | bytes 458784 | tf_op jit(solution)/shard_map/all_to_all | solution.py:292
  163.4 0.9 copy.12
  164.3 11.6 %all-to-all-start.2 = ((bf16[512,2,128]{2,1,0:T(2,128)(2,1)}), bf16[512,2,128]{2,1,0:T(2,128)(2,1)S(1)}, u32[]{:S(2)}, u32[]{:S(2)}) async-start(bf16[512,2,128]{2,1,0:T(2,128)(2,1)} %bitcast.10), calls=%async_computation.2 | async-start | bytes 524288 | tf_op jit(solution)/shard_map/all_to_all | solution.py:311
  176.0 15.5 %all-to-all-done.2 = bf16[512,2,128]{2,1,0:T(2,128)(2,1)S(1)} async-done(((bf16[512,2,128]{2,1,0:T(2,128)(2,1)}), bf16[512,2,128]{2,1,0:T(2,128)(2,1)S(1)}, u32[]{:S(2)}, u32[]{:S(2)}) %all-to-all-start.2) | async-done | bytes 262176 | tf_op jit(solution)/shard_map/all_to_all | solution.py:311
  191.6 0.9 home.1
  192.5 10.5 %pmax.7 = f32[128]{0:T(128)} all-reduce(f32[128]{0:T(128)S(1)} %slice_bitcast_fusion.1), channel_id=1, replica_groups=mesh['z'=8,'y'=8,'core'=2,'tensor'=4] {'tensor'}, use_global_device_ids=true, to_apply=%region_10.11 | all-reduce | flops 128 | bytes 1024 | tf_op jit(solution)/shard_map/pmax | solution.py:325
  (65 shorter events, 5.5 us)
Async XLA Ops:
  7.2 9.5 %collective-permute-start.3 = (bf16[28,896]{1,0:T(8,128)(2,1)}, bf16[28,896]{1,0:T(8,128)(2,1)S(1)}, u32[]{:S(2)}, u32[]{:S(2)}) collective-permute-start(bf16[28,896]{1,0:T(8,128)(2,1)} %bitcast.25), channel_id=1, source_target_pairs={{0,0},{1,128},{2,256},{3,384},{4,4},{5,20},{6,36},{7,52},{8,8},{9,... | collective-permute-start | bytes 150536 | tf_op jit(solution)/shard_map/ppermute | solution.py:186
  13.2 9.8 %collective-permute-start.4 = (bf16[28,896]{1,0:T(8,128)(2,1)}, bf16[28,896]{1,0:T(8,128)(2,1)S(1)}, u32[]{:S(2)}, u32[]{:S(2)}) collective-permute-start(bf16[28,896]{1,0:T(8,128)(2,1)} %bitcast.26), channel_id=1, source_target_pairs={{0,4},{1,20},{2,36},{3,52},{4,0},{5,128},{6,256},{7,384},{8,68},{9... | collective-permute-start | bytes 150536 | tf_op jit(solution)/shard_map/ppermute | solution.py:187
  23.0 8.1 %copy-start = (bf16[1,512,896]{2,1,0:T(8,128)(2,1)S(1)}, bf16[1,512,896]{2,1,0:T(8,128)(2,1)}, u32[]{:S(2)}) copy-start(bf16[1,512,896]{2,1,0:T(8,128)(2,1)} %param.13) | copy-start | bytes 2752516
  24.0 7.4 %copy-start.10 = (s32[1,32]{1,0:T(1,128)S(1)}, s32[1,32]{1,0:T(1,128)}, u32[]{:S(2)}) copy-start(s32[1,32]{1,0:T(1,128)} %param.14) | copy-start | bytes 388
  24.0 7.5 %copy-start.1 = (bf16[128,3584]{1,0:T(8,128)(2,1)S(1)}, bf16[128,3584]{1,0:T(8,128)(2,1)}, u32[]{:S(2)}) copy-start(bf16[128,3584]{1,0:T(8,128)(2,1)} %residual.1) | copy-start | bytes 2752516
  24.0 7.5 %copy-start.2 = (bf16[512,896]{1,0:T(8,128)(2,1)S(1)}, bf16[512,896]{1,0:T(8,128)(2,1)}, u32[]{:S(2)}) copy-start(bf16[512,896]{1,0:T(8,128)(2,1)} %context.3) | copy-start | bytes 2752516
  24.0 23.5 %all-to-all-start = ((bf16[8,56,896]{2,1,0:T(8,128)(2,1)}), bf16[8,56,896]{2,1,0:T(8,128)(2,1)}, u32[]{:S(2)}, u32[]{:S(2)}) async-start(bf16[8,56,896]{2,1,0:T(8,128)(2,1)} %broadcast_in_dim.89), calls=%async_computation | async-start | bytes 1605632 | tf_op jit(solution)/shard_map/all_to_all | solution.py:213
  31.1 80.9 %all-gather.2.cloned.1.call-start = ((), (), s32[]{:S(2)}) async-start(), calls=%async_computation.3 | async-start | bytes 7225344 | tf_op jit(solution)/shard_map/all_gather | solution.py:218
  31.4 62.7 %copy-start.7 = (s32[128]{0:T(128)S(1)}, s32[128]{0:T(128)}, u32[]{:S(2)}) copy-start(s32[128]{0:T(128)} %param.17) | copy-start | bytes 1540
  31.4 62.7 %copy-start.8 = (s32[128]{0:T(128)S(1)}, s32[128]{0:T(128)}, u32[]{:S(2)}) copy-start(s32[128]{0:T(128)} %param.16) | copy-start | bytes 1540
  31.4 62.7 %copy-start.9 = (s32[128,1]{0,1:T(1,128)S(1)}, s32[128,1]{0,1:T(1,128)}, u32[]{:S(2)}) copy-start(s32[128,1]{0,1:T(1,128)} %param.15) | copy-start | bytes 1540
  31.6 63.7 %copy-start.3 = (s32[4]{0:T(128)}, s32[4]{0:T(128)S(1)}, u32[]{:S(2)}) copy-start(s32[4]{0:T(128)S(1)} %pad_add_fusion.place) | copy-start | bytes 52
  32.3 1.1 copy-start.4
  33.4 1.0 copy-start.5
  47.5 31.3 %collective-permute-start = (bf16[784,896]{1,0:T(8,128)(2,1)}, bf16[784,896]{1,0:T(8,128)(2,1)}, u32[]{:S(2)}, u32[]{:S(2)}) collective-permute-start(bf16[784,896]{1,0:T(8,128)(2,1)} %copy-done.4), channel_id=1, source_target_pairs={{0,1},{1,0},{2,3},{3,2},{4,7},{5,6},{6,5},{7,4},{8,9},{9,8},{10,11... | collective-permute-start | bytes 4214792 | tf_op jit(solution)/shard_map/ppermute | solution.py:64
  49.5 45.8 %collective-permute-start.1 = (bf16[656,896]{1,0:T(8,128)(2,1)}, bf16[656,896]{1,0:T(8,128)(2,1)}, u32[]{:S(2)}, u32[]{:S(2)}) collective-permute-start(bf16[656,896]{1,0:T(8,128)(2,1)} %copy-done.5), channel_id=1, source_target_pairs={{0,3},{1,2},{2,1},{3,0},{4,5},{5,4},{6,7},{7,6},{8,11},{9,10},{10,... | collective-permute-start | bytes 3526664 | tf_op jit(solution)/shard_map/ppermute | solution.py:64
  78.8 30.8 %collective-permute-start.2 = (bf16[784,896]{1,0:T(8,128)(2,1)}, bf16[784,896]{1,0:T(8,128)(2,1)}, u32[]{:S(2)}, u32[]{:S(2)}) collective-permute-start(bf16[784,896]{1,0:T(8,128)(2,1)} %collective-permute-done.near), channel_id=1, source_target_pairs={{0,3},{1,2},{2,1},{3,0},{4,5},{5,4},{6,7},{7,6},{8,11},{9,10},{10,... | collective-permute-start | bytes 4214792 | tf_op jit(solution)/shard_map/ppermute | solution.py:64
  136.1 10.4 %copy-start.6 = (f32[8,128]{1,0:T(8,128)S(1)}, f32[8,128]{1,0:T(8,128)}, u32[]{:S(2)}) copy-start(f32[8,128]{1,0:T(8,128)} %get-tuple-element.17) | copy-start | bytes 12292
  138.0 24.5 %all-to-all-start.1 = ((bf16[128,2,896]{2,1,0:T(2,128)(2,1)}), bf16[128,2,896]{2,1,0:T(2,128)(2,1)S(1)}, u32[]{:S(2)}, u32[]{:S(2)}) async-start(bf16[128,2,896]{2,1,0:T(2,128)(2,1)} %reshape.95), calls=%async_computation.1 | async-start | bytes 917504 | tf_op jit(solution)/shard_map/all_to_all | solution.py:292
  164.3 27.2 %all-to-all-start.2 = ((bf16[512,2,128]{2,1,0:T(2,128)(2,1)}), bf16[512,2,128]{2,1,0:T(2,128)(2,1)S(1)}, u32[]{:S(2)}, u32[]{:S(2)}) async-start(bf16[512,2,128]{2,1,0:T(2,128)(2,1)} %bitcast.10), calls=%async_computation.2 | async-start | bytes 524288 | tf_op jit(solution)/shard_map/all_to_all | solution.py:311
Sparse Core Ops, SparseCore 0:
  47.7 50.8 all-gather.1

commit v7 on v6

--- a/solution.py
+++ b/solution.py
@@ -209,14 +209,15 @@
         name="pack",
     )(place, context, residual, small)
 
-    near, side = pair(to_near, 0), pair(to_side, 1)
+    near = pair(to_near, 0)
     plane = lax.all_to_all(
         jnp.broadcast_to(block[None], (8, 56, QUARTER)), ALL, 0, 0,
         axis_index_groups=groups("line"), tiled=True,
     ).reshape(HALF, QUARTER)
     plane, _, _ = lax.optimization_barrier((plane, to_near, to_side))
     plane = lax.all_gather(plane, ALL, axis=0, axis_index_groups=groups("ring"), tiled=True)
-    far = pair(near, 1)
+    near, late_side = lax.optimization_barrier((near, to_side))
+    far, side = pair(near, 1), pair(late_side, 1)
 
     tails = [(x, small), (near_x, near[-16:]), (side_x, side[-16:]), (far_x, far[-16:])]
     member_sq = sum((tail[:4, :128].astype(F32) for _, tail in tails[1:]), small[:4, :128].astype(F32))
@@ -284,7 +285,7 @@
         ),
         in_specs=[VMEM] * 5,
         out_specs=(VMEM, VMEM),
-        compiler_params=params(54),
+        compiler_params=params(),
         cost_estimate=cost(2 * SLOTS * TOK * QUARTER, 3_000_000),
         name="pool",
     )(hidden, gain_of(norm_gain, x), pool, inverse, lax.psum(squares, "tensor"))

time: 211 us -> 212 us (level)
  waiting for transfers between devices: 71 us -> 83.8 us
  starting transfers between devices: 61.5 us -> 55.7 us
  Pallas kernels: 14.5 us -> 12.2 us
    ppermute x3, waiting for transfers between devices: 30.9 us -> 43.8 us  [pair(): return lax.ppermute(value, ALL, pairs)]
    ppermute x3, starting transfers between devices: 27.2 us -> 16.6 us  [pair(): return lax.ppermute(value, ALL, pairs)]
    all_to_all x1, starting transfers between devices: 6.17 us -> 11 us  [body(): lax.all_to_all(slots.reshape(DOCS, 2, QUARTER), DP, split_axis=0, concat_...]
    pallas_call x1, Pallas kernels: 3.09 us -> 0.84 us  [body(): pl.pallas_call(pool_kernel, out_shape=(jax.ShapeDtypeStruct((SLOTS, QUART...]
where the time goes in v7:
time: 212 us; the launch traced here: 211 us
  waiting for transfers between devices  83.8 us (40%)
  starting transfers between devices  55.7 us (26%)
  blocking collectives  30.7 us (14%)
  between operations  14.4 us (7%)
  Pallas kernels  12.2 us (6%)
  local copies, waits for them, and re-layouts  8.84 us (4%)
  other arithmetic  5.51 us (3%)
    ppermute x3, waiting for transfers between devices, pair(): return lax.ppermute(value, ALL, pairs)  43.8 us
    ppermute x3, starting transfers between devices, pair(): return lax.ppermute(value, ALL, pairs)  16.6 us
    all_to_all x1, waiting for transfers between devices, body(): lax.all_to_all(partial, ALL, split_axis=0, concat_axis=0, tiled=True)  15.5 us
    all_to_all x1, waiting for transfers between devices, body(): lax.all_to_all(jnp.broadcast_to(block[None], (8, 56, QUARTER)), ALL, 0, 0...  13 us
    all_to_all x1, starting transfers between devices, body(): lax.all_to_all(partial, ALL, split_axis=0, concat_axis=0, tiled=True)  11.6 us
    all_to_all x1, starting transfers between devices, body(): lax.all_to_all(slots.reshape(DOCS, 2, QUARTER), DP, split_axis=0, concat_...  11 us
    psum x1, blocking collectives, body(): slot_sq = lax.psum(doc_sq, 'tensor')[:2].reshape(SLOTS)  11 us
    pmax x1, blocking collectives, body(): return (scores, lax.pmax(best[0], 'tensor'))  10.5 us
  transfers between devices with their start and end apart: 9, of which 6 were waited for; matrix products, arithmetic and copies ran while one was open for 4% of the time, Pallas kernels for 0%

profile of v7, /device:TPU:2, one launch (start us, length us, event | category | flops | bytes accessed | tf_op | source)
XLA Modules:
  0.0 211.5 jit_solution(10375077493723152560)
XLA Ops:
  7.2 6.1 %collective-permute-start.3 = (bf16[28,896]{1,0:T(8,128)(2,1)}, bf16[28,896]{1,0:T(8,128)(2,1)S(1)}, u32[]{:S(2)}, u32[]{:S(2)}) collective-permute-start(bf16[28,896]{1,0:T(8,128)(2,1)} %bitcast.25), channel_id=1, source_target_pairs={{0,0},{1,128},{2,256},{3,384},{4,4},{5,20},{6,36},{7,52},{8,8},{9,... | collective-permute-start | bytes 150536 | tf_op jit(solution)/shard_map/ppermute | solution.py:186
  13.2 3.4 %collective-permute-start.4 = (bf16[28,896]{1,0:T(8,128)(2,1)}, bf16[28,896]{1,0:T(8,128)(2,1)S(1)}, u32[]{:S(2)}, u32[]{:S(2)}) collective-permute-start(bf16[28,896]{1,0:T(8,128)(2,1)} %bitcast.26), channel_id=1, source_target_pairs={{0,4},{1,20},{2,36},{3,52},{4,0},{5,128},{6,256},{7,384},{8,68},{9... | collective-permute-start | bytes 150536 | tf_op jit(solution)/shard_map/ppermute | solution.py:187
  16.7 6.3 %collective-permute-done.4 = bf16[28,896]{1,0:T(8,128)(2,1)S(1)} collective-permute-done((bf16[28,896]{1,0:T(8,128)(2,1)}, bf16[28,896]{1,0:T(8,128)(2,1)S(1)}, u32[]{:S(2)}, u32[]{:S(2)}) %collective-permute-start.4) | collective-permute-done | bytes 50208 | tf_op jit(solution)/shard_map/ppermute | solution.py:187
  23.1 1.0 broadcast_in_dim.89
  24.1 7.0 %all-to-all-start = ((bf16[8,56,896]{2,1,0:T(8,128)(2,1)}), bf16[8,56,896]{2,1,0:T(8,128)(2,1)}, u32[]{:S(2)}, u32[]{:S(2)}) async-start(bf16[8,56,896]{2,1,0:T(8,128)(2,1)} %broadcast_in_dim.89), calls=%async_computation | async-start | bytes 1605632 | tf_op jit(solution)/shard_map/all_to_all | solution.py:213
  31.6 0.7 pack.1
  32.4 1.1 copy-done.5
  33.5 1.1 copy-done.6
  34.6 13.0 %all-to-all-done = bf16[8,56,896]{2,1,0:T(8,128)(2,1)} async-done(((bf16[8,56,896]{2,1,0:T(8,128)(2,1)}), bf16[8,56,896]{2,1,0:T(8,128)(2,1)}, u32[]{:S(2)}, u32[]{:S(2)}) %all-to-all-start) | async-done | bytes 802848 | tf_op jit(solution)/shard_map/all_to_all | solution.py:213
  47.6 1.9 collective-permute-start
  49.5 18.9 %collective-permute-done.near = bf16[784,896]{1,0:T(8,128)(2,1)} collective-permute-done((bf16[784,896]{1,0:T(8,128)(2,1)}, bf16[784,896]{1,0:T(8,128)(2,1)}, u32[]{:S(2)}, u32[]{:S(2)}) %collective-permute-start) | collective-permute-done | bytes 1404960 | tf_op jit(solution)/shard_map/ppermute | solution.py:64
  68.4 12.7 %collective-permute-start.2 = (bf16[784,896]{1,0:T(8,128)(2,1)}, bf16[784,896]{1,0:T(8,128)(2,1)}, u32[]{:S(2)}, u32[]{:S(2)}) collective-permute-start(bf16[784,896]{1,0:T(8,128)(2,1)} %collective-permute-done.near), channel_id=1, source_target_pairs={{0,3},{1,2},{2,1},{3,0},{4,5},{5,4},{6,7},{7,6},{8,11},{9,10},{10,... | collective-permute-start | bytes 4214792 | tf_op jit(solution)/shard_map/ppermute | solution.py:64
  81.2 1.9 collective-permute-start.1
  83.1 0.8 dynamic_slice.7
  84.3 0.7 constant_dynamic-slice_fusion.res
  85.1 0.7 slice_convert_fusion.2
  85.8 24.9 %collective-permute-done.1.side = bf16[656,896]{1,0:T(8,128)(2,1)} collective-permute-done((bf16[656,896]{1,0:T(8,128)(2,1)}, bf16[656,896]{1,0:T(8,128)(2,1)}, u32[]{:S(2)}, u32[]{:S(2)}) %collective-permute-start.1) | collective-permute-done | bytes 1175584 | tf_op jit(solution)/shard_map/ppermute | solution.py:64
  110.7 0.7 slice_convert_fusion.1
  113.1 9.1 %project.1 = (f32[512,896]{1,0:T(8,128)}, f32[8,128]{1,0:T(8,128)}) custom-call(s32[4]{0:T(128)} %copy-done.4, bf16[512,896]{1,0:T(8,128)(2,1)} %context.3, bf16[784,896]{1,0:T(8,128)(2,1)} %collective-permute-done.near, bf16[656,896]{1,0:T(8,128)(2,1)} %collective-permute-done.1.side, bf16[784,896]{1,0:T(8,128)(2,1)} %collective-permute-done.2.far, ...), custom_call_target="tpu_custom_call" | custom-call | flops 3288334336 | bytes 13000000 | tf_op jit(solution)/shard_map/project/pallas_call | solution.py:261
  122.2 9.3 %psum.14.total = f32[8,128]{1,0:T(8,128)S(1)} all-reduce(f32[8,128]{1,0:T(8,128)} %get-tuple-element.19), channel_id=1, replica_groups=mesh['z'=8,'y'=8,'core'=2,'tensor'=4] {'tensor'}, use_global_device_ids=true, to_apply=%region_5.6 | all-reduce | flops 1024 | bytes 8192 | tf_op jit(solution)/shard_map/psum | solution.py:291
  131.6 1.5 copy-done.1
  133.1 0.8 pool.1
  133.9 0.9 reshape.95
  134.9 11.0 %all-to-all-start.1 = ((bf16[128,2,896]{2,1,0:T(2,128)(2,1)}), bf16[128,2,896]{2,1,0:T(2,128)(2,1)S(1)}, u32[]{:S(2)}, u32[]{:S(2)}) async-start(bf16[128,2,896]{2,1,0:T(2,128)(2,1)} %reshape.95), calls=%async_computation.1 | async-start | bytes 917504 | tf_op jit(solution)/shard_map/all_to_all | solution.py:293
  146.8 1.3 rsqrt_select_fusion.factor
  148.1 11.0 %psum.15 = f32[8,128]{1,0:T(8,128)S(1)} all-reduce(f32[8,128]{1,0:T(8,128)S(1)} %get-tuple-element.21), channel_id=1, replica_groups=mesh['z'=8,'y'=8,'core'=2,'tensor'=4] {'tensor'}, use_global_device_ids=true, to_apply=%region_7.8 | all-reduce | flops 1024 | bytes 8192 | tf_op jit(solution)/shard_map/psum | solution.py:297
  159.1 5.1 %all-to-all-done.1 = bf16[128,2,896]{2,1,0:T(2,128)(2,1)S(1)} async-done(((bf16[128,2,896]{2,1,0:T(2,128)(2,1)}), bf16[128,2,896]{2,1,0:T(2,128)(2,1)S(1)}, u32[]{:S(2)}, u32[]{:S(2)}) %all-to-all-start.1) | async-done | bytes 458784 | tf_op jit(solution)/shard_map/all_to_all | solution.py:293
  165.1 0.9 copy.12
  166.0 11.6 %all-to-all-start.2 = ((bf16[512,2,128]{2,1,0:T(2,128)(2,1)}), bf16[512,2,128]{2,1,0:T(2,128)(2,1)S(1)}, u32[]{:S(2)}, u32[]{:S(2)}) async-start(bf16[512,2,128]{2,1,0:T(2,128)(2,1)} %bitcast.10), calls=%async_computation.2 | async-start | bytes 524288 | tf_op jit(solution)/shard_map/all_to_all | solution.py:312
  177.7 15.5 %all-to-all-done.2 = bf16[512,2,128]{2,1,0:T(2,128)(2,1)S(1)} async-done(((bf16[512,2,128]{2,1,0:T(2,128)(2,1)}), bf16[512,2,128]{2,1,0:T(2,128)(2,1)S(1)}, u32[]{:S(2)}, u32[]{:S(2)}) %all-to-all-start.2) | async-done | bytes 262176 | tf_op jit(solution)/shard_map/all_to_all | solution.py:312
  193.3 0.9 home.1
  194.1 10.5 %pmax.7 = f32[128]{0:T(128)} all-reduce(f32[128]{0:T(128)S(1)} %slice_bitcast_fusion.1), channel_id=1, replica_groups=mesh['z'=8,'y'=8,'core'=2,'tensor'=4] {'tensor'}, use_global_device_ids=true, to_apply=%region_10.11 | all-reduce | flops 128 | bytes 1024 | tf_op jit(solution)/shard_map/pmax | solution.py:326
  (65 shorter events, 4.7 us)
Async XLA Ops:
  7.2 9.5 %collective-permute-start.3 = (bf16[28,896]{1,0:T(8,128)(2,1)}, bf16[28,896]{1,0:T(8,128)(2,1)S(1)}, u32[]{:S(2)}, u32[]{:S(2)}) collective-permute-start(bf16[28,896]{1,0:T(8,128)(2,1)} %bitcast.25), channel_id=1, source_target_pairs={{0,0},{1,128},{2,256},{3,384},{4,4},{5,20},{6,36},{7,52},{8,8},{9,... | collective-permute-start | bytes 150536 | tf_op jit(solution)/shard_map/ppermute | solution.py:186
  13.2 9.8 %collective-permute-start.4 = (bf16[28,896]{1,0:T(8,128)(2,1)}, bf16[28,896]{1,0:T(8,128)(2,1)S(1)}, u32[]{:S(2)}, u32[]{:S(2)}) collective-permute-start(bf16[28,896]{1,0:T(8,128)(2,1)} %bitcast.26), channel_id=1, source_target_pairs={{0,4},{1,20},{2,36},{3,52},{4,0},{5,128},{6,256},{7,384},{8,68},{9... | collective-permute-start | bytes 150536 | tf_op jit(solution)/shard_map/ppermute | solution.py:187
  23.0 8.2 %copy-start = (bf16[1,512,896]{2,1,0:T(8,128)(2,1)S(1)}, bf16[1,512,896]{2,1,0:T(8,128)(2,1)}, u32[]{:S(2)}) copy-start(bf16[1,512,896]{2,1,0:T(8,128)(2,1)} %param.13) | copy-start | bytes 2752516
  24.1 7.4 %copy-start.10 = (s32[1,32]{1,0:T(1,128)S(1)}, s32[1,32]{1,0:T(1,128)}, u32[]{:S(2)}) copy-start(s32[1,32]{1,0:T(1,128)} %param.14) | copy-start | bytes 388
  24.1 7.5 %copy-start.2 = (bf16[128,3584]{1,0:T(8,128)(2,1)S(1)}, bf16[128,3584]{1,0:T(8,128)(2,1)}, u32[]{:S(2)}) copy-start(bf16[128,3584]{1,0:T(8,128)(2,1)} %residual.1) | copy-start | bytes 2752516
  24.1 7.5 %copy-start.3 = (bf16[512,896]{1,0:T(8,128)(2,1)S(1)}, bf16[512,896]{1,0:T(8,128)(2,1)}, u32[]{:S(2)}) copy-start(bf16[512,896]{1,0:T(8,128)(2,1)} %context.3) | copy-start | bytes 2752516
  24.1 23.5 %all-to-all-start = ((bf16[8,56,896]{2,1,0:T(8,128)(2,1)}), bf16[8,56,896]{2,1,0:T(8,128)(2,1)}, u32[]{:S(2)}, u32[]{:S(2)}) async-start(bf16[8,56,896]{2,1,0:T(8,128)(2,1)} %broadcast_in_dim.89), calls=%async_computation | async-start | bytes 1605632 | tf_op jit(solution)/shard_map/all_to_all | solution.py:213
  31.1 82.0 %all-gather.2.cloned.1.call-start = ((), (), s32[]{:S(2)}) async-start(), calls=%async_computation.3 | async-start | bytes 7225344 | tf_op jit(solution)/shard_map/all_gather | solution.py:218
  31.5 52.5 %copy-start.7 = (s32[128]{0:T(128)S(1)}, s32[128]{0:T(128)}, u32[]{:S(2)}) copy-start(s32[128]{0:T(128)} %param.17) | copy-start | bytes 1540
  31.5 52.5 %copy-start.8 = (s32[128]{0:T(128)S(1)}, s32[128]{0:T(128)}, u32[]{:S(2)}) copy-start(s32[128]{0:T(128)} %param.16) | copy-start | bytes 1540
  31.5 52.5 %copy-start.9 = (s32[128,1]{0,1:T(1,128)S(1)}, s32[128,1]{0,1:T(1,128)}, u32[]{:S(2)}) copy-start(s32[128,1]{0,1:T(1,128)} %param.15) | copy-start | bytes 1540
  31.6 53.4 %copy-start.4 = (s32[4]{0:T(128)}, s32[4]{0:T(128)S(1)}, u32[]{:S(2)}) copy-start(s32[4]{0:T(128)S(1)} %pad_add_fusion.place) | copy-start | bytes 52
  32.4 1.1 copy-start.5
  33.5 1.1 copy-start.6
  47.6 20.8 %collective-permute-start = (bf16[784,896]{1,0:T(8,128)(2,1)}, bf16[784,896]{1,0:T(8,128)(2,1)}, u32[]{:S(2)}, u32[]{:S(2)}) collective-permute-start(bf16[784,896]{1,0:T(8,128)(2,1)} %copy-done.5), channel_id=1, source_target_pairs={{0,1},{1,0},{2,3},{3,2},{4,7},{5,6},{6,5},{7,4},{8,9},{9,8},{10,11... | collective-permute-start | bytes 4214792 | tf_op jit(solution)/shard_map/ppermute | solution.py:64
  68.4 43.0 %collective-permute-start.2 = (bf16[784,896]{1,0:T(8,128)(2,1)}, bf16[784,896]{1,0:T(8,128)(2,1)}, u32[]{:S(2)}, u32[]{:S(2)}) collective-permute-start(bf16[784,896]{1,0:T(8,128)(2,1)} %collective-permute-done.near), channel_id=1, source_target_pairs={{0,3},{1,2},{2,1},{3,0},{4,5},{5,4},{6,7},{7,6},{8,11},{9,10},{10,... | collective-permute-start | bytes 4214792 | tf_op jit(solution)/shard_map/ppermute | solution.py:64
  81.2 29.5 %collective-permute-start.1 = (bf16[656,896]{1,0:T(8,128)(2,1)}, bf16[656,896]{1,0:T(8,128)(2,1)}, u32[]{:S(2)}, u32[]{:S(2)}) collective-permute-start(bf16[656,896]{1,0:T(8,128)(2,1)} %copy-done.6), channel_id=1, source_target_pairs={{0,3},{1,2},{2,1},{3,0},{4,5},{5,4},{6,7},{7,6},{8,11},{9,10},{10,... | collective-permute-start | bytes 3526664 | tf_op jit(solution)/shard_map/ppermute | solution.py:64
  131.6 1.5 copy-start.1
  134.9 29.3 %all-to-all-start.1 = ((bf16[128,2,896]{2,1,0:T(2,128)(2,1)}), bf16[128,2,896]{2,1,0:T(2,128)(2,1)S(1)}, u32[]{:S(2)}, u32[]{:S(2)}) async-start(bf16[128,2,896]{2,1,0:T(2,128)(2,1)} %reshape.95), calls=%async_computation.1 | async-start | bytes 917504 | tf_op jit(solution)/shard_map/all_to_all | solution.py:293
  166.0 27.2 %all-to-all-start.2 = ((bf16[512,2,128]{2,1,0:T(2,128)(2,1)}), bf16[512,2,128]{2,1,0:T(2,128)(2,1)S(1)}, u32[]{:S(2)}, u32[]{:S(2)}) async-start(bf16[512,2,128]{2,1,0:T(2,128)(2,1)} %bitcast.10), calls=%async_computation.2 | async-start | bytes 524288 | tf_op jit(solution)/shard_map/all_to_all | solution.py:312
Sparse Core Ops, SparseCore 0:
  47.7 50.8 all-gather.1

commit v8 on v7

--- a/solution.py
+++ b/solution.py
@@ -68,34 +68,44 @@
     return lax.ppermute(value, ALL, [(at, at ^ 4) for at in range(512)])
 
 
-def pack_kernel(place, context, residual, small, near, side):
-    near[0:TOK, :] = context[...]
-    side[0:TOK, :] = context[...]
-    for out, row, target in ((near, 512, 1), (near, 640, 3), (side, 512, 2)):
+def pack_kernel(place, context, residual, small, near, rest, side):
+    for out, row, target in ((near, 0, 1), (near, 128, 3), (side, 512, 2)):
         start = pl.multiple_of(place[target] * QUARTER, 128)
         out[row : row + 128, :] = residual[:, pl.ds(start, QUARTER)]
-    near[768:784, :] = small[...]
+    near[256:272, :] = small[...]
+    near[272:400, :] = context[0:128, :]
+    rest[...] = context[128:TOK, :]
+    side[0:TOK, :] = context[...]
     side[640:656, :] = small[...]
 
 
 def project_kernel(
-    place, context, near, side, far, weight, res, hidden, squares, ctx, tails, blocks, sems
+    place, context, near, near_rest, side, far, far_rest, weight, res, hidden, squares,
+    ctx, tails, blocks, sems,
 ):
     def fetch(source, target, at):
         return pltpu.make_async_copy(source, target, sems.at[at])
 
-    copies = []
-    for index, piece in enumerate((context, near, side, far)):
+    pieces = (
+        ((context, 0, 0, TOK),),
+        ((near, 272, 0, 128), (near_rest, 0, 128, 384)),
+        ((side, 0, 0, TOK),),
+        ((far, 272, 0, 128), (far_rest, 0, 128, 384)),
+    )
+    copies, used = [], 0
+    for index, parts in enumerate(pieces):
         start = pl.multiple_of(place[index] * QUARTER, QUARTER)
-        copies.append(
-            (
-                fetch(piece.at[pl.ds(0, TOK), :], ctx.at[index], 2 * index),
-                fetch(weight.at[pl.ds(start, QUARTER), :], blocks.at[index], 2 * index + 1),
+        group = [fetch(weight.at[pl.ds(start, QUARTER), :], blocks.at[index], used)]
+        used += 1
+        for piece, row, to, count in parts:
+            group.append(
+                fetch(piece.at[pl.ds(row, count), :], ctx.at[index, pl.ds(to, count), :], used)
             )
-        )
+            used += 1
+        copies.append(group)
     ends = [
-        fetch(piece.at[pl.ds(row, 128), :], tails.at[index], 8 + index)
-        for index, (piece, row) in enumerate(((res, 0), (near, 512), (side, 512), (far, 640)))
+        fetch(piece.at[pl.ds(row, 128), :], tails.at[index], used + index)
+        for index, (piece, row) in enumerate(((res, 0), (near, 0), (side, 512), (far, 128)))
     ]
     for pair_of in copies:
         for copy in pair_of:
@@ -196,14 +206,15 @@
         [partial_sq.reshape(4, 128), jnp.pad(doc_lengths.astype(BF), ((0, 0), (0, 96)))], axis=0
     )
     small = jnp.pad(small, ((0, 11), (0, QUARTER - 128)))
-    to_near, to_side = pl.pallas_call(
+    to_near, to_rest, to_side = pl.pallas_call(
         pack_kernel,
         out_shape=(
-            jax.ShapeDtypeStruct((784, QUARTER), BF),
+            jax.ShapeDtypeStruct((400, QUARTER), BF),
+            jax.ShapeDtypeStruct((384, QUARTER), BF),
             jax.ShapeDtypeStruct((656, QUARTER), BF),
         ),
         in_specs=[SMEM] + [VMEM] * 3,
-        out_specs=(pl.BlockSpec(), pl.BlockSpec()),
+        out_specs=(pl.BlockSpec(),) * 3,
         compiler_params=params(),
         cost_estimate=cost(0, 6_000_000),
         name="pack",
@@ -214,12 +225,13 @@
         jnp.broadcast_to(block[None], (8, 56, QUARTER)), ALL, 0, 0,
         axis_index_groups=groups("line"), tiled=True,
     ).reshape(HALF, QUARTER)
-    plane, _, _ = lax.optimization_barrier((plane, to_near, to_side))
+    plane, near, _, _ = lax.optimization_barrier((plane, near, to_rest, to_side))
     plane = lax.all_gather(plane, ALL, axis=0, axis_index_groups=groups("ring"), tiled=True)
-    near, late_side = lax.optimization_barrier((near, to_side))
-    far, side = pair(near, 1), pair(late_side, 1)
-
-    tails = [(x, small), (near_x, near[-16:]), (side_x, side[-16:]), (far_x, far[-16:])]
+    near_rest, far = pair(to_rest, 0), pair(near, 1)
+    near_rest, late_side = lax.optimization_barrier((near_rest, to_side))
+    far_rest, side = pair(near_rest, 1), pair(late_side, 1)
+
+    tails = [(x, small), (near_x, near[256:272]), (side_x, side[-16:]), (far_x, far[256:272])]
     member_sq = sum((tail[:4, :128].astype(F32) for _, tail in tails[1:]), small[:4, :128].astype(F32))
     lens = jnp.zeros((4, 32), F32)
     for at, tail in tails:
@@ -264,18 +276,18 @@
             jax.ShapeDtypeStruct((TOK, QUARTER), F32),
             jax.ShapeDtypeStruct((8, 128), F32),
         ),
-        in_specs=[SMEM] + [pl.BlockSpec(memory_space=pl.ANY)] * 6,
+        in_specs=[SMEM] + [pl.BlockSpec(memory_space=pl.ANY)] * 8,
         out_specs=(VMEM, VMEM),
         scratch_shapes=[
             pltpu.VMEM((4, TOK, QUARTER), BF),
             pltpu.VMEM((4, 128, QUARTER), BF),
             pltpu.VMEM((4, QUARTER, QUARTER), BF),
-            pltpu.SemaphoreType.DMA((12,)),
+            pltpu.SemaphoreType.DMA((14,)),
         ],
         compiler_params=params(54),
         cost_estimate=cost(2 * TOK * QUARTER * 3584, 13_000_000),
         name="project",
-    )(place, context, near, side, far, plane, res)
+    )(place, context, near, near_rest, side, far, far_rest, plane, res)
 
     slots, doc_sq = pl.pallas_call(
         pool_kernel,

time: 212 us -> 201 us (0.948)
  waiting for transfers between devices: 83.8 us -> 71.1 us
  starting transfers between devices: 55.7 us -> 60.8 us
    all_to_all x1, waiting for transfers between devices: 13 us -> 1.02 us  [body(): lax.all_to_all(jnp.broadcast_to(block[None], (8, 56, QUARTER)), ALL, 0, 0...]
    ppermute x3 -> x5, starting transfers between devices: 16.6 us -> 22.5 us  [pair(): return lax.ppermute(value, ALL, pairs)]
    ppermute x3 -> x5, waiting for transfers between devices: 43.8 us -> 42.1 us  [pair(): return lax.ppermute(value, ALL, pairs)]
  transfers between devices with their start and end apart: 9 -> 11, of which waited for: 6 -> 10; matrix products, arithmetic and copies ran while one was open for 4% -> 3% of each run, Pallas kernels for 0% -> 0%
where the time goes in v8:
time: 201 us
  waiting for transfers between devices  71.1 us (35%)
  starting transfers between devices  60.8 us (30%)
  blocking collectives  29.8 us (15%)
  between operations  14.4 us (7%)
  Pallas kernels  12.2 us (6%)
  local copies, waits for them, and re-layouts  7.71 us (4%)
  other arithmetic  4.15 us (2%)
    ppermute x5, waiting for transfers between devices, pair(): return lax.ppermute(value, ALL, pairs)  42.1 us
    ppermute x5, starting transfers between devices, pair(): return lax.ppermute(value, ALL, pairs)  22.5 us
    all_to_all x1, waiting for transfers between devices, body(): lax.all_to_all(partial, ALL, split_axis=0, concat_axis=0, tiled=True)  15.5 us
    all_to_all x1, starting transfers between devices, body(): lax.all_to_all(slots.reshape(DOCS, 2, QUARTER), DP, split_axis=0, concat_...  11 us
    all_to_all x1, starting transfers between devices, body(): lax.all_to_all(partial, ALL, split_axis=0, concat_axis=0, tiled=True)  10.8 us
    pmax x1, blocking collectives, body(): return (scores, lax.pmax(best[0], 'tensor'))  10.6 us
    psum x1, blocking collectives, body(): slot_sq = lax.psum(doc_sq, 'tensor')[:2].reshape(SLOTS)  10.1 us
    psum x1, blocking collectives, body(): lax.psum(squares, 'tensor')  9.19 us
  transfers between devices with their start and end apart: 11, of which 10 were waited for; matrix products, arithmetic and copies ran while one was open for 3% of the time, Pallas kernels for 0%

profile of v8, /device:TPU:2, one launch (start us, length us, event | category | flops | bytes accessed | tf_op | source)
XLA Modules:
  0.0 200.5 jit_solution(14113993254797515799)
XLA Ops:
  7.2 6.2 %collective-permute-start = (bf16[28,896]{1,0:T(8,128)(2,1)}, bf16[28,896]{1,0:T(8,128)(2,1)S(1)}, u32[]{:S(2)}, u32[]{:S(2)}) collective-permute-start(bf16[28,896]{1,0:T(8,128)(2,1)} %bitcast.25), channel_id=1, source_target_pairs={{0,0},{1,128},{2,256},{3,384},{4,4},{5,20},{6,36},{7,52},{8,8},{9,... | collective-permute-start | bytes 150536 | tf_op jit(solution)/shard_map/ppermute | solution.py:196
  13.4 3.4 %collective-permute-start.1 = (bf16[28,896]{1,0:T(8,128)(2,1)}, bf16[28,896]{1,0:T(8,128)(2,1)S(1)}, u32[]{:S(2)}, u32[]{:S(2)}) collective-permute-start(bf16[28,896]{1,0:T(8,128)(2,1)} %bitcast.26), channel_id=1, source_target_pairs={{0,4},{1,20},{2,36},{3,52},{4,0},{5,128},{6,256},{7,384},{8,68},{9... | collective-permute-start | bytes 150536 | tf_op jit(solution)/shard_map/ppermute | solution.py:197
  16.8 6.3 %collective-permute-done.1 = bf16[28,896]{1,0:T(8,128)(2,1)S(1)} collective-permute-done((bf16[28,896]{1,0:T(8,128)(2,1)}, bf16[28,896]{1,0:T(8,128)(2,1)S(1)}, u32[]{:S(2)}, u32[]{:S(2)}) %collective-permute-start.1) | collective-permute-done | bytes 50208 | tf_op jit(solution)/shard_map/ppermute | solution.py:197
  23.3 1.0 broadcast_in_dim.89
  24.2 6.9 %all-to-all-start = ((bf16[8,56,896]{2,1,0:T(8,128)(2,1)}), bf16[8,56,896]{2,1,0:T(8,128)(2,1)}, u32[]{:S(2)}, u32[]{:S(2)}) async-start(bf16[8,56,896]{2,1,0:T(8,128)(2,1)} %broadcast_in_dim.89), calls=%async_computation | async-start | bytes 1605632 | tf_op jit(solution)/shard_map/all_to_all | solution.py:224
  32.4 1.0 copy-done.5
  33.4 1.9 collective-permute-start.2
  35.3 11.2 %collective-permute-done.2.near = bf16[400,896]{1,0:T(8,128)(2,1)S(1)} collective-permute-done((bf16[400,896]{1,0:T(8,128)(2,1)S(1)}, bf16[400,896]{1,0:T(8,128)(2,1)S(1)}, u32[]{:S(2)}, u32[]{:S(2)}) %collective-permute-start.2) | collective-permute-done | bytes 716832 | tf_op jit(solution)/shard_map/ppermute | solution.py:64
  46.6 1.0 all-to-all-done
  47.6 1.9 collective-permute-start.3
  49.5 11.0 %collective-permute-done.3.near_rest = bf16[384,896]{1,0:T(8,128)(2,1)} collective-permute-done((bf16[384,896]{1,0:T(8,128)(2,1)S(1)}, bf16[384,896]{1,0:T(8,128)(2,1)}, u32[]{:S(2)}, u32[]{:S(2)}) %collective-permute-start.3) | collective-permute-done | bytes 688160 | tf_op jit(solution)/shard_map/ppermute | solution.py:64
  60.5 12.8 %collective-permute-start.4 = (bf16[656,896]{1,0:T(8,128)(2,1)}, bf16[656,896]{1,0:T(8,128)(2,1)}, u32[]{:S(2)}, u32[]{:S(2)}) collective-permute-start(bf16[656,896]{1,0:T(8,128)(2,1)} %copy-done.5), channel_id=1, source_target_pairs={{0,3},{1,2},{2,1},{3,0},{4,5},{5,4},{6,7},{7,6},{8,11},{9,10},{10,... | collective-permute-start | bytes 3526664 | tf_op jit(solution)/shard_map/ppermute | solution.py:64
  74.5 1.9 collective-permute-start.5
  76.4 0.8 dynamic_slice.7
  77.3 3.9 %collective-permute-start.6 = (bf16[384,896]{1,0:T(8,128)(2,1)}, bf16[384,896]{1,0:T(8,128)(2,1)}, u32[]{:S(2)}, u32[]{:S(2)}) collective-permute-start(bf16[384,896]{1,0:T(8,128)(2,1)} %collective-permute-done.3.near_rest), channel_id=1, source_target_pairs={{0,3},{1,2},{2,1},{3,0},{4,5},{5,4},{6,7},{7,6},{8,11},{9,10},{10,... | collective-permute-start | bytes 2064392 | tf_op jit(solution)/shard_map/ppermute | solution.py:64
  81.2 6.6 %collective-permute-done.4.side = bf16[656,896]{1,0:T(8,128)(2,1)} collective-permute-done((bf16[656,896]{1,0:T(8,128)(2,1)}, bf16[656,896]{1,0:T(8,128)(2,1)}, u32[]{:S(2)}, u32[]{:S(2)}) %collective-permute-start.4) | collective-permute-done | bytes 1175584 | tf_op jit(solution)/shard_map/ppermute | solution.py:64
  88.5 6.9 %collective-permute-done.5.far = bf16[400,896]{1,0:T(8,128)(2,1)S(1)} collective-permute-done((bf16[400,896]{1,0:T(8,128)(2,1)S(1)}, bf16[400,896]{1,0:T(8,128)(2,1)S(1)}, u32[]{:S(2)}, u32[]{:S(2)}) %collective-permute-start.5) | collective-permute-done | bytes 716832 | tf_op jit(solution)/shard_map/ppermute | solution.py:64
  96.4 6.4 %collective-permute-done.6.far_rest = bf16[384,896]{1,0:T(8,128)(2,1)} collective-permute-done((bf16[384,896]{1,0:T(8,128)(2,1)}, bf16[384,896]{1,0:T(8,128)(2,1)}, u32[]{:S(2)}, u32[]{:S(2)}) %collective-permute-start.6) | collective-permute-done | bytes 688160 | tf_op jit(solution)/shard_map/ppermute | solution.py:64
  103.0 9.1 %project.1 = (f32[512,896]{1,0:T(8,128)}, f32[8,128]{1,0:T(8,128)}) custom-call(s32[4]{0:T(128)} %copy-done.4, bf16[512,896]{1,0:T(8,128)(2,1)} %context.3, bf16[400,896]{1,0:T(8,128)(2,1)} %copy-done.9, bf16[384,896]{1,0:T(8,128)(2,1)} %collective-permute-done.3.near_rest, bf16[656,896]{1,0:T(8,128)(2,1)} %collective-permute-done.4.side, ...), custom_call_target="tpu_custom_call" | custom-call | flops 3288334336 | bytes 13000000 | tf_op jit(solution)/shard_map/project/pallas_call | solution.py:273
  112.1 9.2 %psum.14.total = f32[8,128]{1,0:T(8,128)S(1)} all-reduce(f32[8,128]{1,0:T(8,128)} %get-tuple-element.23), channel_id=1, replica_groups=mesh['z'=8,'y'=8,'core'=2,'tensor'=4] {'tensor'}, use_global_device_ids=true, to_apply=%region_5.6 | all-reduce | flops 1024 | bytes 8192 | tf_op jit(solution)/shard_map/psum | solution.py:303
  121.4 1.5 copy-done.1
  122.9 0.8 pool.1
  123.7 1.0 reshape.95
  124.7 11.0 %all-to-all-start.1 = ((bf16[128,2,896]{2,1,0:T(2,128)(2,1)}), bf16[128,2,896]{2,1,0:T(2,128)(2,1)S(1)}, u32[]{:S(2)}, u32[]{:S(2)}) async-start(bf16[128,2,896]{2,1,0:T(2,128)(2,1)} %reshape.95), calls=%async_computation.1 | async-start | bytes 917504 | tf_op jit(solution)/shard_map/all_to_all | solution.py:305
  136.5 1.4 rsqrt_select_fusion.factor
  137.9 10.1 %psum.15 = f32[8,128]{1,0:T(8,128)S(1)} all-reduce(f32[8,128]{1,0:T(8,128)S(1)} %get-tuple-element.25), channel_id=1, replica_groups=mesh['z'=8,'y'=8,'core'=2,'tensor'=4] {'tensor'}, use_global_device_ids=true, to_apply=%region_7.8 | all-reduce | flops 1024 | bytes 8192 | tf_op jit(solution)/shard_map/psum | solution.py:309
  148.0 6.0 %all-to-all-done.1 = bf16[128,2,896]{2,1,0:T(2,128)(2,1)S(1)} async-done(((bf16[128,2,896]{2,1,0:T(2,128)(2,1)}), bf16[128,2,896]{2,1,0:T(2,128)(2,1)S(1)}, u32[]{:S(2)}, u32[]{:S(2)}) %all-to-all-start.1) | async-done | bytes 458784 | tf_op jit(solution)/shard_map/all_to_all | solution.py:305
  154.9 0.9 copy.12
  155.8 10.8 %all-to-all-start.2 = ((bf16[512,2,128]{2,1,0:T(2,128)(2,1)}), bf16[512,2,128]{2,1,0:T(2,128)(2,1)S(1)}, u32[]{:S(2)}, u32[]{:S(2)}) async-start(bf16[512,2,128]{2,1,0:T(2,128)(2,1)} %bitcast.10), calls=%async_computation.2 | async-start | bytes 524288 | tf_op jit(solution)/shard_map/all_to_all | solution.py:324
  166.7 15.5 %all-to-all-done.2 = bf16[512,2,128]{2,1,0:T(2,128)(2,1)S(1)} async-done(((bf16[512,2,128]{2,1,0:T(2,128)(2,1)}), bf16[512,2,128]{2,1,0:T(2,128)(2,1)S(1)}, u32[]{:S(2)}, u32[]{:S(2)}) %all-to-all-start.2) | async-done | bytes 262176 | tf_op jit(solution)/shard_map/all_to_all | solution.py:324
  182.2 0.9 home.1
  183.1 10.6 %pmax.7 = f32[128]{0:T(128)} all-reduce(f32[128]{0:T(128)S(1)} %slice_bitcast_fusion.1), channel_id=1, replica_groups=mesh['z'=8,'y'=8,'core'=2,'tensor'=4] {'tensor'}, use_global_device_ids=true, to_apply=%region_10.11 | all-reduce | flops 128 | bytes 1024 | tf_op jit(solution)/shard_map/pmax | solution.py:338
  (71 shorter events, 6.2 us)
Async XLA Ops:
  7.2 24.1 %copy-start = (bf16[1,512,896]{2,1,0:T(8,128)(2,1)S(1)}, bf16[1,512,896]{2,1,0:T(8,128)(2,1)}, u32[]{:S(2)}) copy-start(bf16[1,512,896]{2,1,0:T(8,128)(2,1)} %param.13) | copy-start | bytes 2752516
  7.2 9.6 %collective-permute-start = (bf16[28,896]{1,0:T(8,128)(2,1)}, bf16[28,896]{1,0:T(8,128)(2,1)S(1)}, u32[]{:S(2)}, u32[]{:S(2)}) collective-permute-start(bf16[28,896]{1,0:T(8,128)(2,1)} %bitcast.25), channel_id=1, source_target_pairs={{0,0},{1,128},{2,256},{3,384},{4,4},{5,20},{6,36},{7,52},{8,8},{9,... | collective-permute-start | bytes 150536 | tf_op jit(solution)/shard_map/ppermute | solution.py:196
  13.4 9.8 %collective-permute-start.1 = (bf16[28,896]{1,0:T(8,128)(2,1)}, bf16[28,896]{1,0:T(8,128)(2,1)S(1)}, u32[]{:S(2)}, u32[]{:S(2)}) collective-permute-start(bf16[28,896]{1,0:T(8,128)(2,1)} %bitcast.26), channel_id=1, source_target_pairs={{0,4},{1,20},{2,36},{3,52},{4,0},{5,128},{6,256},{7,384},{8,68},{9... | collective-permute-start | bytes 150536 | tf_op jit(solution)/shard_map/ppermute | solution.py:197
  23.2 8.3 %copy-start.11 = (s32[1,32]{1,0:T(1,128)S(1)}, s32[1,32]{1,0:T(1,128)}, u32[]{:S(2)}) copy-start(s32[1,32]{1,0:T(1,128)} %param.14) | copy-start | bytes 388
  23.2 8.4 %copy-start.2 = (bf16[128,3584]{1,0:T(8,128)(2,1)S(1)}, bf16[128,3584]{1,0:T(8,128)(2,1)}, u32[]{:S(2)}) copy-start(bf16[128,3584]{1,0:T(8,128)(2,1)} %residual.1) | copy-start | bytes 2752516
  23.2 8.4 %copy-start.3 = (bf16[512,896]{1,0:T(8,128)(2,1)S(1)}, bf16[512,896]{1,0:T(8,128)(2,1)}, u32[]{:S(2)}) copy-start(bf16[512,896]{1,0:T(8,128)(2,1)} %context.3) | copy-start | bytes 2752516
  24.2 23.3 %all-to-all-start = ((bf16[8,56,896]{2,1,0:T(8,128)(2,1)}), bf16[8,56,896]{2,1,0:T(8,128)(2,1)}, u32[]{:S(2)}, u32[]{:S(2)}) async-start(bf16[8,56,896]{2,1,0:T(8,128)(2,1)} %broadcast_in_dim.89), calls=%async_computation | async-start | bytes 1605632 | tf_op jit(solution)/shard_map/all_to_all | solution.py:224
  31.2 71.8 %all-gather.2.cloned.1.call-start = ((), (), s32[]{:S(2)}) async-start(), calls=%async_computation.3 | async-start | bytes 7225344 | tf_op jit(solution)/shard_map/all_gather | solution.py:229
  31.2 42.2 %copy-start.6 = (s32[128]{0:T(128)S(1)}, s32[128]{0:T(128)}, u32[]{:S(2)}) copy-start(s32[128]{0:T(128)} %param.17) | copy-start | bytes 1540
  31.2 42.2 %copy-start.7 = (s32[128]{0:T(128)S(1)}, s32[128]{0:T(128)}, u32[]{:S(2)}) copy-start(s32[128]{0:T(128)} %param.16) | copy-start | bytes 1540
  31.2 42.2 %copy-start.8 = (s32[128,1]{0,1:T(1,128)S(1)}, s32[128,1]{0,1:T(1,128)}, u32[]{:S(2)}) copy-start(s32[128,1]{0,1:T(1,128)} %param.15) | copy-start | bytes 1540
  31.7 71.3 %copy-start.4 = (s32[4]{0:T(128)}, s32[4]{0:T(128)S(1)}, u32[]{:S(2)}) copy-start(s32[4]{0:T(128)S(1)} %pad_add_fusion.place) | copy-start | bytes 52
  32.4 1.0 copy-start.5
  33.4 13.1 %collective-permute-start.2 = (bf16[400,896]{1,0:T(8,128)(2,1)S(1)}, bf16[400,896]{1,0:T(8,128)(2,1)S(1)}, u32[]{:S(2)}, u32[]{:S(2)}) collective-permute-start(bf16[400,896]{1,0:T(8,128)(2,1)S(1)} %get-tuple-element.15), channel_id=1, source_target_pairs={{0,1},{1,0},{2,3},{3,2},{4,7},{5,6},{6,5},{7,4},{8,9},{9,8},{10,11... | collective-permute-start | bytes 2150408 | tf_op jit(solution)/shard_map/ppermute | solution.py:64
  46.6 56.4 %copy-start.9 = (bf16[400,896]{1,0:T(8,128)(2,1)}, bf16[400,896]{1,0:T(8,128)(2,1)S(1)}, u32[]{:S(2)}) copy-start(bf16[400,896]{1,0:T(8,128)(2,1)S(1)} %collective-permute-done.2.near) | copy-start | bytes 2150404
  47.6 12.9 %collective-permute-start.3 = (bf16[384,896]{1,0:T(8,128)(2,1)S(1)}, bf16[384,896]{1,0:T(8,128)(2,1)}, u32[]{:S(2)}, u32[]{:S(2)}) collective-permute-start(bf16[384,896]{1,0:T(8,128)(2,1)S(1)} %get-tuple-element.16), channel_id=1, source_target_pairs={{0,1},{1,0},{2,3},{3,2},{4,7},{5,6},{6,5},{7,4},{8,9},{9,8},{10,11... | collective-permute-start | bytes 2064392 | tf_op jit(solution)/shard_map/ppermute | solution.py:64
  60.5 27.3 %collective-permute-start.4 = (bf16[656,896]{1,0:T(8,128)(2,1)}, bf16[656,896]{1,0:T(8,128)(2,1)}, u32[]{:S(2)}, u32[]{:S(2)}) collective-permute-start(bf16[656,896]{1,0:T(8,128)(2,1)} %copy-done.5), channel_id=1, source_target_pairs={{0,3},{1,2},{2,1},{3,0},{4,5},{5,4},{6,7},{7,6},{8,11},{9,10},{10,... | collective-permute-start | bytes 3526664 | tf_op jit(solution)/shard_map/ppermute | solution.py:64
  74.5 20.9 %collective-permute-start.5 = (bf16[400,896]{1,0:T(8,128)(2,1)S(1)}, bf16[400,896]{1,0:T(8,128)(2,1)S(1)}, u32[]{:S(2)}, u32[]{:S(2)}) collective-permute-start(bf16[400,896]{1,0:T(8,128)(2,1)S(1)} %collective-permute-done.2.near), channel_id=1, source_target_pairs={{0,3},{1,2},{2,1},{3,0},{4,5},{5,4},{6,7},{7,6},{8,11},{9,10},{10,... | collective-permute-start | bytes 2150408 | tf_op jit(solution)/shard_map/ppermute | solution.py:64
  77.3 25.6 %collective-permute-start.6 = (bf16[384,896]{1,0:T(8,128)(2,1)}, bf16[384,896]{1,0:T(8,128)(2,1)}, u32[]{:S(2)}, u32[]{:S(2)}) collective-permute-start(bf16[384,896]{1,0:T(8,128)(2,1)} %collective-permute-done.3.near_rest), channel_id=1, source_target_pairs={{0,3},{1,2},{2,1},{3,0},{4,5},{5,4},{6,7},{7,6},{8,11},{9,10},{10,... | collective-permute-start | bytes 2064392 | tf_op jit(solution)/shard_map/ppermute | solution.py:64
  95.4 7.6 %copy-start.10 = (bf16[400,896]{1,0:T(8,128)(2,1)}, bf16[400,896]{1,0:T(8,128)(2,1)S(1)}, u32[]{:S(2)}) copy-start(bf16[400,896]{1,0:T(8,128)(2,1)S(1)} %collective-permute-done.5.far) | copy-start | bytes 2150404
  121.4 1.5 copy-start.1
  124.7 29.3 %all-to-all-start.1 = ((bf16[128,2,896]{2,1,0:T(2,128)(2,1)}), bf16[128,2,896]{2,1,0:T(2,128)(2,1)S(1)}, u32[]{:S(2)}, u32[]{:S(2)}) async-start(bf16[128,2,896]{2,1,0:T(2,128)(2,1)} %reshape.95), calls=%async_computation.1 | async-start | bytes 917504 | tf_op jit(solution)/shard_map/all_to_all | solution.py:305
  155.8 26.4 %all-to-all-start.2 = ((bf16[512,2,128]{2,1,0:T(2,128)(2,1)}), bf16[512,2,128]{2,1,0:T(2,128)(2,1)S(1)}, u32[]{:S(2)}, u32[]{:S(2)}) async-start(bf16[512,2,128]{2,1,0:T(2,128)(2,1)} %bitcast.10), calls=%async_computation.2 | async-start | bytes 524288 | tf_op jit(solution)/shard_map/all_to_all | solution.py:324
Sparse Core Ops, SparseCore 0:
  47.7 55.2 all-gather.1

commit v9 on v8

--- a/solution.py
+++ b/solution.py
@@ -36,12 +36,11 @@
     return [(z, y, c, x) for z in range(8) for y in range(8) for c in range(2) for x in range(4)]
 
 
-def spread(flip):
+def spread():
     pairs = []
     for z, y, core, x in grid():
-        to = core ^ flip
-        to_z, to_y = placed(to, 2 * x + z % 2, y)
-        pairs.append((device(z, y, core, x), device(to_z, to_y, to, z // 2)))
+        to_z, to_y = placed(core, 2 * x + z % 2, y)
+        pairs.append((device(z, y, core, x), device(to_z, to_y, core, z // 2)))
     return pairs
 
 
@@ -193,11 +192,11 @@
     place = jnp.stack([x, near_x, side_x, far_x]).astype(jnp.int32)
 
     weight = out_weight.T
-    keep = lax.ppermute(weight, ALL, spread(0))
-    cross = lax.ppermute(weight, ALL, spread(1))
+    twin = core_swap(weight)
     block = jnp.concatenate(
-        [jnp.where(first, keep, cross), jnp.where(first, cross, keep)], axis=0
-    )
+        [jnp.where(first, weight, twin), jnp.where(first, twin, weight)], axis=0
+    )
+    block = lax.ppermute(block, ALL, spread())
 
     resident = members[0]
     resident_f = resident.astype(F32)

time: 201 us -> 203 us (level)
  waiting for transfers between devices: 71.1 us -> 78.6 us
  starting transfers between devices: 60.8 us -> 56.1 us
  blocking collectives: 29.8 us -> 27.5 us
    all_gather x1, waiting for transfers between devices: 0.09 us -> 5.36 us  [body(): lax.all_gather(plane, ALL, axis=0, axis_index_groups=groups('ring'), tile...]
    all_to_all x1, starting transfers between devices: 6.92 us -> 4.41 us  [body(): lax.all_to_all(jnp.broadcast_to(block[None], (8, 56, QUARTER)), ALL, 0, 0...]
    all_to_all x1, starting transfers between devices: 11 us -> 13.3 us  [body(): lax.all_to_all(slots.reshape(DOCS, 2, QUARTER), DP, split_axis=0, concat_...]
  transfers between devices with their start and end apart: 11 -> 11, of which waited for: 10 -> 11; matrix products, arithmetic and copies ran while one was open for 3% -> 3% of each run, Pallas kernels for 0% -> 0%
where the time goes in v9:
time: 203 us; the launch traced here: 202 us
  waiting for transfers between devices  78.6 us (39%)
  starting transfers between devices  56.1 us (28%)
  blocking collectives  27.5 us (14%)
  between operations  14.4 us (7%)
  Pallas kernels  12.2 us (6%)
  local copies, waits for them, and re-layouts  7.71 us (4%)
  other arithmetic  4.98 us (2%)
    ppermute x5, waiting for transfers between devices, pair(): return lax.ppermute(value, ALL, pairs)  42.1 us
    ppermute x5, starting transfers between devices, pair(): return lax.ppermute(value, ALL, pairs)  21.3 us
    all_to_all x1, waiting for transfers between devices, body(): lax.all_to_all(partial, ALL, split_axis=0, concat_axis=0, tiled=True)  15.5 us
    all_to_all x1, starting transfers between devices, body(): lax.all_to_all(slots.reshape(DOCS, 2, QUARTER), DP, split_axis=0, concat_...  13.3 us
    pmax x1, blocking collectives, body(): return (scores, lax.pmax(best[0], 'tensor'))  10.6 us
    pallas_call x1, Pallas kernels, body(): pl.pallas_call(project_kernel, out_shape=(jax.ShapeDtypeStruct((TOK, QUAR...  9.1 us
    all_to_all x1, starting transfers between devices, body(): lax.all_to_all(partial, ALL, split_axis=0, concat_axis=0, tiled=True)  8.9 us
    psum x1, blocking collectives, body(): lax.psum(squares, 'tensor')  8.74 us
  transfers between devices with their start and end apart: 11, of which 11 were waited for; matrix products, arithmetic and copies ran while one was open for 3% of the time, Pallas kernels for 0%

profile of v9, /device:TPU:2, one launch (start us, length us, event | category | flops | bytes accessed | tf_op | source)
XLA Modules:
  0.0 201.8 jit_solution(11397924311284066635)
XLA Ops:
  7.2 2.1 %collective-permute-start = (bf16[28,896]{1,0:T(8,128)(2,1)}, bf16[28,896]{1,0:T(8,128)(2,1)S(1)}, u32[]{:S(2)}, u32[]{:S(2)}) collective-permute-start(bf16[28,896]{1,0:T(8,128)(2,1)} %bitcast.25), channel_id=1, source_target_pairs={{0,4},{1,5},{2,6},{3,7},{4,0},{5,1},{6,2},{7,3},{8,12},{9,13},{10,... | collective-permute-start | bytes 150536 | tf_op jit(solution)/shard_map/ppermute | solution.py:67
  9.2 1.4 collective-permute-done
  11.6 6.2 %collective-permute-start.1 = (bf16[56,896]{1,0:T(8,128)(2,1)S(1)}, bf16[56,896]{1,0:T(8,128)(2,1)S(1)}, u32[]{:S(2)}, u32[]{:S(2)}) collective-permute-start(bf16[56,896]{1,0:T(8,128)(2,1)S(1)} %pad_maximum_fusion), channel_id=1, source_target_pairs={{0,0},{1,128},{2,256},{3,384},{4,4},{5,20},{6,36},{7,52},{8,8},{9,... | collective-permute-start | bytes 301064 | tf_op jit(solution)/shard_map/ppermute | solution.py:199
  17.8 5.3 %collective-permute-done.1 = bf16[56,896]{1,0:T(8,128)(2,1)S(1)} collective-permute-done((bf16[56,896]{1,0:T(8,128)(2,1)S(1)}, bf16[56,896]{1,0:T(8,128)(2,1)S(1)}, u32[]{:S(2)}, u32[]{:S(2)}) %collective-permute-start.1) | collective-permute-done | bytes 100384 | tf_op jit(solution)/shard_map/ppermute | solution.py:199
  23.1 1.0 broadcast_in_dim.89
  24.0 4.4 %all-to-all-start = ((bf16[8,56,896]{2,1,0:T(8,128)(2,1)}), bf16[8,56,896]{2,1,0:T(8,128)(2,1)}, u32[]{:S(2)}, u32[]{:S(2)}) async-start(bf16[8,56,896]{2,1,0:T(8,128)(2,1)} %broadcast_in_dim.89), calls=%async_computation | async-start | bytes 1605632 | tf_op jit(solution)/shard_map/all_to_all | solution.py:223
  29.7 1.0 copy-done.5
  30.7 1.9 collective-permute-start.2
  32.6 11.2 %collective-permute-done.2.near = bf16[400,896]{1,0:T(8,128)(2,1)S(1)} collective-permute-done((bf16[400,896]{1,0:T(8,128)(2,1)S(1)}, bf16[400,896]{1,0:T(8,128)(2,1)S(1)}, u32[]{:S(2)}, u32[]{:S(2)}) %collective-permute-start.2) | collective-permute-done | bytes 716832 | tf_op jit(solution)/shard_map/ppermute | solution.py:63
  43.9 1.0 all-to-all-done
  44.9 1.9 collective-permute-start.3
  46.8 11.0 %collective-permute-done.3.near_rest = bf16[384,896]{1,0:T(8,128)(2,1)} collective-permute-done((bf16[384,896]{1,0:T(8,128)(2,1)S(1)}, bf16[384,896]{1,0:T(8,128)(2,1)}, u32[]{:S(2)}, u32[]{:S(2)}) %collective-permute-start.3) | collective-permute-done | bytes 688160 | tf_op jit(solution)/shard_map/ppermute | solution.py:63
  57.8 11.6 %collective-permute-start.4 = (bf16[656,896]{1,0:T(8,128)(2,1)}, bf16[656,896]{1,0:T(8,128)(2,1)}, u32[]{:S(2)}, u32[]{:S(2)}) collective-permute-start(bf16[656,896]{1,0:T(8,128)(2,1)} %copy-done.5), channel_id=1, source_target_pairs={{0,3},{1,2},{2,1},{3,0},{4,5},{5,4},{6,7},{7,6},{8,11},{9,10},{10,... | collective-permute-start | bytes 3526664 | tf_op jit(solution)/shard_map/ppermute | solution.py:63
  70.6 1.9 collective-permute-start.5
  73.4 3.9 %collective-permute-start.6 = (bf16[384,896]{1,0:T(8,128)(2,1)}, bf16[384,896]{1,0:T(8,128)(2,1)}, u32[]{:S(2)}, u32[]{:S(2)}) collective-permute-start(bf16[384,896]{1,0:T(8,128)(2,1)} %collective-permute-done.3.near_rest), channel_id=1, source_target_pairs={{0,3},{1,2},{2,1},{3,0},{4,5},{5,4},{6,7},{7,6},{8,11},{9,10},{10,... | collective-permute-start | bytes 2064392 | tf_op jit(solution)/shard_map/ppermute | solution.py:63
  77.3 6.6 %collective-permute-done.4.side = bf16[656,896]{1,0:T(8,128)(2,1)} collective-permute-done((bf16[656,896]{1,0:T(8,128)(2,1)}, bf16[656,896]{1,0:T(8,128)(2,1)}, u32[]{:S(2)}, u32[]{:S(2)}) %collective-permute-start.4) | collective-permute-done | bytes 1175584 | tf_op jit(solution)/shard_map/ppermute | solution.py:63
  84.6 6.9 %collective-permute-done.5.far = bf16[400,896]{1,0:T(8,128)(2,1)S(1)} collective-permute-done((bf16[400,896]{1,0:T(8,128)(2,1)S(1)}, bf16[400,896]{1,0:T(8,128)(2,1)S(1)}, u32[]{:S(2)}, u32[]{:S(2)}) %collective-permute-start.5) | collective-permute-done | bytes 716832 | tf_op jit(solution)/shard_map/ppermute | solution.py:63
  92.5 6.4 %collective-permute-done.6.far_rest = bf16[384,896]{1,0:T(8,128)(2,1)} collective-permute-done((bf16[384,896]{1,0:T(8,128)(2,1)}, bf16[384,896]{1,0:T(8,128)(2,1)}, u32[]{:S(2)}, u32[]{:S(2)}) %collective-permute-start.6) | collective-permute-done | bytes 688160 | tf_op jit(solution)/shard_map/ppermute | solution.py:63
  99.0 5.4 %all-gather.2.cloned.1.call-done.weight = bf16[3584,896]{1,0:T(8,128)(2,1)} async-done(((bf16[448,896]{1,0:T(8,128)(2,1)}), bf16[3584,896]{1,0:T(8,128)(2,1)}) %all-gather.2.cloned.1.call-update) | async-done | bytes 6422544 | tf_op jit(solution)/shard_map/all_gather | solution.py:228
  104.3 9.1 %project.1 = (f32[512,896]{1,0:T(8,128)}, f32[8,128]{1,0:T(8,128)}) custom-call(s32[4]{0:T(128)} %copy-done.4, bf16[512,896]{1,0:T(8,128)(2,1)} %context.3, bf16[400,896]{1,0:T(8,128)(2,1)} %copy-done.9, bf16[384,896]{1,0:T(8,128)(2,1)} %collective-permute-done.3.near_rest, bf16[656,896]{1,0:T(8,128)(2,1)} %collective-permute-done.4.side, ...), custom_call_target="tpu_custom_call" | custom-call | flops 3288334336 | bytes 13000000 | tf_op jit(solution)/shard_map/project/pallas_call | solution.py:272
  113.4 8.7 %psum.14.total = f32[8,128]{1,0:T(8,128)S(1)} all-reduce(f32[8,128]{1,0:T(8,128)} %get-tuple-element.23), channel_id=1, replica_groups=mesh['z'=8,'y'=8,'core'=2,'tensor'=4] {'tensor'}, use_global_device_ids=true, to_apply=%region_5.6 | all-reduce | flops 1024 | bytes 8192 | tf_op jit(solution)/shard_map/psum | solution.py:302
  122.3 1.5 copy-done.1
  124.6 1.0 reshape.95
  125.5 13.3 %all-to-all-start.1 = ((bf16[128,2,896]{2,1,0:T(2,128)(2,1)}), bf16[128,2,896]{2,1,0:T(2,128)(2,1)S(1)}, u32[]{:S(2)}, u32[]{:S(2)}) async-start(bf16[128,2,896]{2,1,0:T(2,128)(2,1)} %reshape.95), calls=%async_computation.1 | async-start | bytes 917504 | tf_op jit(solution)/shard_map/all_to_all | solution.py:304
  139.7 1.4 rsqrt_select_fusion.factor
  141.1 8.2 %psum.15 = f32[8,128]{1,0:T(8,128)S(1)} all-reduce(f32[8,128]{1,0:T(8,128)S(1)} %get-tuple-element.25), channel_id=1, replica_groups=mesh['z'=8,'y'=8,'core'=2,'tensor'=4] {'tensor'}, use_global_device_ids=true, to_apply=%region_7.8 | all-reduce | flops 1024 | bytes 8192 | tf_op jit(solution)/shard_map/psum | solution.py:308
  149.3 7.9 %all-to-all-done.1 = bf16[128,2,896]{2,1,0:T(2,128)(2,1)S(1)} async-done(((bf16[128,2,896]{2,1,0:T(2,128)(2,1)}), bf16[128,2,896]{2,1,0:T(2,128)(2,1)S(1)}, u32[]{:S(2)}, u32[]{:S(2)}) %all-to-all-start.1) | async-done | bytes 458784 | tf_op jit(solution)/shard_map/all_to_all | solution.py:304
  158.1 0.9 copy.12
  159.0 8.9 %all-to-all-start.2 = ((bf16[512,2,128]{2,1,0:T(2,128)(2,1)}), bf16[512,2,128]{2,1,0:T(2,128)(2,1)S(1)}, u32[]{:S(2)}, u32[]{:S(2)}) async-start(bf16[512,2,128]{2,1,0:T(2,128)(2,1)} %bitcast.10), calls=%async_computation.2 | async-start | bytes 524288 | tf_op jit(solution)/shard_map/all_to_all | solution.py:323
  168.0 15.5 %all-to-all-done.2 = bf16[512,2,128]{2,1,0:T(2,128)(2,1)S(1)} async-done(((bf16[512,2,128]{2,1,0:T(2,128)(2,1)}), bf16[512,2,128]{2,1,0:T(2,128)(2,1)S(1)}, u32[]{:S(2)}, u32[]{:S(2)}) %all-to-all-start.2) | async-done | bytes 262176 | tf_op jit(solution)/shard_map/all_to_all | solution.py:323
  183.6 0.9 home.1
  184.4 10.6 %pmax.7 = f32[128]{0:T(128)} all-reduce(f32[128]{0:T(128)S(1)} %slice_bitcast_fusion.1), channel_id=1, replica_groups=mesh['z'=8,'y'=8,'core'=2,'tensor'=4] {'tensor'}, use_global_device_ids=true, to_apply=%region_10.11 | all-reduce | flops 128 | bytes 1024 | tf_op jit(solution)/shard_map/pmax | solution.py:337
  (71 shorter events, 8.6 us)
Async XLA Ops:
  7.2 21.4 %copy-start = (bf16[1,512,896]{2,1,0:T(8,128)(2,1)S(1)}, bf16[1,512,896]{2,1,0:T(8,128)(2,1)}, u32[]{:S(2)}) copy-start(bf16[1,512,896]{2,1,0:T(8,128)(2,1)} %param.13) | copy-start | bytes 2752516
  7.2 3.5 %collective-permute-start = (bf16[28,896]{1,0:T(8,128)(2,1)}, bf16[28,896]{1,0:T(8,128)(2,1)S(1)}, u32[]{:S(2)}, u32[]{:S(2)}) collective-permute-start(bf16[28,896]{1,0:T(8,128)(2,1)} %bitcast.25), channel_id=1, source_target_pairs={{0,4},{1,5},{2,6},{3,7},{4,0},{5,1},{6,2},{7,3},{8,12},{9,13},{10,... | collective-permute-start | bytes 150536 | tf_op jit(solution)/shard_map/ppermute | solution.py:67
  11.5 17.3 %copy-start.11 = (s32[1,32]{1,0:T(1,128)S(1)}, s32[1,32]{1,0:T(1,128)}, u32[]{:S(2)}) copy-start(s32[1,32]{1,0:T(1,128)} %param.14) | copy-start | bytes 388
  11.5 17.4 %copy-start.2 = (bf16[128,3584]{1,0:T(8,128)(2,1)S(1)}, bf16[128,3584]{1,0:T(8,128)(2,1)}, u32[]{:S(2)}) copy-start(bf16[128,3584]{1,0:T(8,128)(2,1)} %residual.1) | copy-start | bytes 2752516
  11.5 17.4 %copy-start.3 = (bf16[512,896]{1,0:T(8,128)(2,1)S(1)}, bf16[512,896]{1,0:T(8,128)(2,1)}, u32[]{:S(2)}) copy-start(bf16[512,896]{1,0:T(8,128)(2,1)} %context.3) | copy-start | bytes 2752516
  11.6 11.5 %collective-permute-start.1 = (bf16[56,896]{1,0:T(8,128)(2,1)S(1)}, bf16[56,896]{1,0:T(8,128)(2,1)S(1)}, u32[]{:S(2)}, u32[]{:S(2)}) collective-permute-start(bf16[56,896]{1,0:T(8,128)(2,1)S(1)} %pad_maximum_fusion), channel_id=1, source_target_pairs={{0,0},{1,128},{2,256},{3,384},{4,4},{5,20},{6,36},{7,52},{8,8},{9,... | collective-permute-start | bytes 301064 | tf_op jit(solution)/shard_map/ppermute | solution.py:199
  24.0 20.8 %all-to-all-start = ((bf16[8,56,896]{2,1,0:T(8,128)(2,1)}), bf16[8,56,896]{2,1,0:T(8,128)(2,1)}, u32[]{:S(2)}, u32[]{:S(2)}) async-start(bf16[8,56,896]{2,1,0:T(8,128)(2,1)} %broadcast_in_dim.89), calls=%async_computation | async-start | bytes 1605632 | tf_op jit(solution)/shard_map/all_to_all | solution.py:223
  28.4 75.9 %all-gather.2.cloned.1.call-start = ((), (), s32[]{:S(2)}) async-start(), calls=%async_computation.3 | async-start | bytes 7225344 | tf_op jit(solution)/shard_map/all_gather | solution.py:228
  28.5 41.0 %copy-start.6 = (s32[128]{0:T(128)S(1)}, s32[128]{0:T(128)}, u32[]{:S(2)}) copy-start(s32[128]{0:T(128)} %param.17) | copy-start | bytes 1540
  28.5 41.0 %copy-start.7 = (s32[128]{0:T(128)S(1)}, s32[128]{0:T(128)}, u32[]{:S(2)}) copy-start(s32[128]{0:T(128)} %param.16) | copy-start | bytes 1540
  28.5 41.0 %copy-start.8 = (s32[128,1]{0,1:T(1,128)S(1)}, s32[128,1]{0,1:T(1,128)}, u32[]{:S(2)}) copy-start(s32[128,1]{0,1:T(1,128)} %param.15) | copy-start | bytes 1540
  28.9 75.4 %copy-start.4 = (s32[4]{0:T(128)}, s32[4]{0:T(128)S(1)}, u32[]{:S(2)}) copy-start(s32[4]{0:T(128)S(1)} %pad_add_fusion.place) | copy-start | bytes 52
  29.7 1.0 copy-start.5
  30.7 13.1 %collective-permute-start.2 = (bf16[400,896]{1,0:T(8,128)(2,1)S(1)}, bf16[400,896]{1,0:T(8,128)(2,1)S(1)}, u32[]{:S(2)}, u32[]{:S(2)}) collective-permute-start(bf16[400,896]{1,0:T(8,128)(2,1)S(1)} %get-tuple-element.15), channel_id=1, source_target_pairs={{0,1},{1,0},{2,3},{3,2},{4,7},{5,6},{6,5},{7,4},{8,9},{9,8},{10,11... | collective-permute-start | bytes 2150408 | tf_op jit(solution)/shard_map/ppermute | solution.py:63
  43.8 60.5 %copy-start.9 = (bf16[400,896]{1,0:T(8,128)(2,1)}, bf16[400,896]{1,0:T(8,128)(2,1)S(1)}, u32[]{:S(2)}) copy-start(bf16[400,896]{1,0:T(8,128)(2,1)S(1)} %collective-permute-done.2.near) | copy-start | bytes 2150404
  44.9 12.9 %collective-permute-start.3 = (bf16[384,896]{1,0:T(8,128)(2,1)S(1)}, bf16[384,896]{1,0:T(8,128)(2,1)}, u32[]{:S(2)}, u32[]{:S(2)}) collective-permute-start(bf16[384,896]{1,0:T(8,128)(2,1)S(1)} %get-tuple-element.16), channel_id=1, source_target_pairs={{0,1},{1,0},{2,3},{3,2},{4,7},{5,6},{6,5},{7,4},{8,9},{9,8},{10,11... | collective-permute-start | bytes 2064392 | tf_op jit(solution)/shard_map/ppermute | solution.py:63
  57.8 26.1 %collective-permute-start.4 = (bf16[656,896]{1,0:T(8,128)(2,1)}, bf16[656,896]{1,0:T(8,128)(2,1)}, u32[]{:S(2)}, u32[]{:S(2)}) collective-permute-start(bf16[656,896]{1,0:T(8,128)(2,1)} %copy-done.5), channel_id=1, source_target_pairs={{0,3},{1,2},{2,1},{3,0},{4,5},{5,4},{6,7},{7,6},{8,11},{9,10},{10,... | collective-permute-start | bytes 3526664 | tf_op jit(solution)/shard_map/ppermute | solution.py:63
  70.6 20.9 %collective-permute-start.5 = (bf16[400,896]{1,0:T(8,128)(2,1)S(1)}, bf16[400,896]{1,0:T(8,128)(2,1)S(1)}, u32[]{:S(2)}, u32[]{:S(2)}) collective-permute-start(bf16[400,896]{1,0:T(8,128)(2,1)S(1)} %collective-permute-done.2.near), channel_id=1, source_target_pairs={{0,3},{1,2},{2,1},{3,0},{4,5},{5,4},{6,7},{7,6},{8,11},{9,10},{10,... | collective-permute-start | bytes 2150408 | tf_op jit(solution)/shard_map/ppermute | solution.py:63
  73.4 25.6 %collective-permute-start.6 = (bf16[384,896]{1,0:T(8,128)(2,1)}, bf16[384,896]{1,0:T(8,128)(2,1)}, u32[]{:S(2)}, u32[]{:S(2)}) collective-permute-start(bf16[384,896]{1,0:T(8,128)(2,1)} %collective-permute-done.3.near_rest), channel_id=1, source_target_pairs={{0,3},{1,2},{2,1},{3,0},{4,5},{5,4},{6,7},{7,6},{8,11},{9,10},{10,... | collective-permute-start | bytes 2064392 | tf_op jit(solution)/shard_map/ppermute | solution.py:63
  91.5 12.8 %copy-start.10 = (bf16[400,896]{1,0:T(8,128)(2,1)}, bf16[400,896]{1,0:T(8,128)(2,1)S(1)}, u32[]{:S(2)}) copy-start(bf16[400,896]{1,0:T(8,128)(2,1)S(1)} %collective-permute-done.5.far) | copy-start | bytes 2150404
  122.3 1.5 copy-start.1
  125.5 31.6 %all-to-all-start.1 = ((bf16[128,2,896]{2,1,0:T(2,128)(2,1)}), bf16[128,2,896]{2,1,0:T(2,128)(2,1)S(1)}, u32[]{:S(2)}, u32[]{:S(2)}) async-start(bf16[128,2,896]{2,1,0:T(2,128)(2,1)} %reshape.95), calls=%async_computation.1 | async-start | bytes 917504 | tf_op jit(solution)/shard_map/all_to_all | solution.py:304
  159.0 24.5 %all-to-all-start.2 = ((bf16[512,2,128]{2,1,0:T(2,128)(2,1)}), bf16[512,2,128]{2,1,0:T(2,128)(2,1)S(1)}, u32[]{:S(2)}, u32[]{:S(2)}) async-start(bf16[512,2,128]{2,1,0:T(2,128)(2,1)} %bitcast.10), calls=%async_computation.2 | async-start | bytes 524288 | tf_op jit(solution)/shard_map/all_to_all | solution.py:323
Sparse Core Ops, SparseCore 0:
  45.0 59.2 all-gather.1

commit v10 on v8

--- a/solution.py
+++ b/solution.py
@@ -284,7 +284,7 @@
             pltpu.VMEM((4, QUARTER, QUARTER), BF),
             pltpu.SemaphoreType.DMA((14,)),
         ],
-        compiler_params=params(54),
+        compiler_params=params(50),
         cost_estimate=cost(2 * TOK * QUARTER * 3584, 13_000_000),
         name="project",
     )(place, context, near, near_rest, side, far, far_rest, plane, res)

time: 201 us -> 202 us (level)
    unnamed x24 -> x22, local copies, waits for them, and re-layouts: 2.58 us -> 4.54 us
where the time goes in v10:
time: 202 us; the launch traced here: 201 us
  waiting for transfers between devices  70.3 us (35%)
  starting transfers between devices  61 us (30%)
  blocking collectives  29.6 us (15%)
  between operations  14.4 us (7%)
  Pallas kernels  11.7 us (6%)
  local copies, waits for them, and re-layouts  8.99 us (4%)
  other arithmetic  4.84 us (2%)
    ppermute x5, waiting for transfers between devices, pair(): return lax.ppermute(value, ALL, pairs)  41.4 us
    ppermute x5, starting transfers between devices, pair(): return lax.ppermute(value, ALL, pairs)  22.4 us
    all_to_all x1, waiting for transfers between devices, body(): lax.all_to_all(partial, ALL, split_axis=0, concat_axis=0, tiled=True)  15.5 us
    all_to_all x1, starting transfers between devices, body(): lax.all_to_all(slots.reshape(DOCS, 2, QUARTER), DP, split_axis=0, concat_...  11.2 us
    all_to_all x1, starting transfers between devices, body(): lax.all_to_all(partial, ALL, split_axis=0, concat_axis=0, tiled=True)  10.8 us
    pmax x1, blocking collectives, body(): return (scores, lax.pmax(best[0], 'tensor'))  10.5 us
    psum x1, blocking collectives, body(): slot_sq = lax.psum(doc_sq, 'tensor')[:2].reshape(SLOTS)  10.1 us
    psum x1, blocking collectives, body(): lax.psum(squares, 'tensor')  8.91 us
  transfers between devices with their start and end apart: 11, of which 10 were waited for; matrix products, arithmetic and copies ran while one was open for 3% of the time, Pallas kernels for 0%

profile of v10, /device:TPU:2, one launch (start us, length us, event | category | flops | bytes accessed | tf_op | source)
XLA Modules:
  0.0 201.2 jit_solution(6101395924321615759)
XLA Ops:
  7.2 6.2 %collective-permute-start = (bf16[28,896]{1,0:T(8,128)(2,1)}, bf16[28,896]{1,0:T(8,128)(2,1)S(1)}, u32[]{:S(2)}, u32[]{:S(2)}) collective-permute-start(bf16[28,896]{1,0:T(8,128)(2,1)} %bitcast.25), channel_id=1, source_target_pairs={{0,0},{1,128},{2,256},{3,384},{4,4},{5,20},{6,36},{7,52},{8,8},{9,... | collective-permute-start | bytes 150536 | tf_op jit(solution)/shard_map/ppermute | solution.py:196
  13.4 3.4 %collective-permute-start.1 = (bf16[28,896]{1,0:T(8,128)(2,1)}, bf16[28,896]{1,0:T(8,128)(2,1)S(1)}, u32[]{:S(2)}, u32[]{:S(2)}) collective-permute-start(bf16[28,896]{1,0:T(8,128)(2,1)} %bitcast.26), channel_id=1, source_target_pairs={{0,4},{1,20},{2,36},{3,52},{4,0},{5,128},{6,256},{7,384},{8,68},{9... | collective-permute-start | bytes 150536 | tf_op jit(solution)/shard_map/ppermute | solution.py:197
  16.8 6.3 %collective-permute-done.1 = bf16[28,896]{1,0:T(8,128)(2,1)S(1)} collective-permute-done((bf16[28,896]{1,0:T(8,128)(2,1)}, bf16[28,896]{1,0:T(8,128)(2,1)S(1)}, u32[]{:S(2)}, u32[]{:S(2)}) %collective-permute-start.1) | collective-permute-done | bytes 50208 | tf_op jit(solution)/shard_map/ppermute | solution.py:197
  23.3 1.0 broadcast_in_dim.89
  24.2 6.9 %all-to-all-start = ((bf16[8,56,896]{2,1,0:T(8,128)(2,1)}), bf16[8,56,896]{2,1,0:T(8,128)(2,1)}, u32[]{:S(2)}, u32[]{:S(2)}) async-start(bf16[8,56,896]{2,1,0:T(8,128)(2,1)} %broadcast_in_dim.89), calls=%async_computation | async-start | bytes 1605632 | tf_op jit(solution)/shard_map/all_to_all | solution.py:224
  32.4 1.0 copy-done.6
  33.4 1.9 collective-permute-start.2
  35.4 11.3 %collective-permute-done.2.near = bf16[400,896]{1,0:T(8,128)(2,1)} collective-permute-done((bf16[400,896]{1,0:T(8,128)(2,1)S(1)}, bf16[400,896]{1,0:T(8,128)(2,1)}, u32[]{:S(2)}, u32[]{:S(2)}) %collective-permute-start.2) | collective-permute-done | bytes 716832 | tf_op jit(solution)/shard_map/ppermute | solution.py:64
  46.7 0.9 all-to-all-done
  47.6 1.9 collective-permute-start.3
  49.5 11.0 %collective-permute-done.3.near_rest = bf16[384,896]{1,0:T(8,128)(2,1)} collective-permute-done((bf16[384,896]{1,0:T(8,128)(2,1)S(1)}, bf16[384,896]{1,0:T(8,128)(2,1)}, u32[]{:S(2)}, u32[]{:S(2)}) %collective-permute-start.3) | collective-permute-done | bytes 688160 | tf_op jit(solution)/shard_map/ppermute | solution.py:64
  60.6 12.8 %collective-permute-start.4 = (bf16[656,896]{1,0:T(8,128)(2,1)}, bf16[656,896]{1,0:T(8,128)(2,1)}, u32[]{:S(2)}, u32[]{:S(2)}) collective-permute-start(bf16[656,896]{1,0:T(8,128)(2,1)} %copy-done.6), channel_id=1, source_target_pairs={{0,3},{1,2},{2,1},{3,0},{4,5},{5,4},{6,7},{7,6},{8,11},{9,10},{10,... | collective-permute-start | bytes 3526664 | tf_op jit(solution)/shard_map/ppermute | solution.py:64
  73.8 1.9 collective-permute-start.5
  76.5 3.9 %collective-permute-start.6 = (bf16[384,896]{1,0:T(8,128)(2,1)}, bf16[384,896]{1,0:T(8,128)(2,1)}, u32[]{:S(2)}, u32[]{:S(2)}) collective-permute-start(bf16[384,896]{1,0:T(8,128)(2,1)} %collective-permute-done.3.near_rest), channel_id=1, source_target_pairs={{0,3},{1,2},{2,1},{3,0},{4,5},{5,4},{6,7},{7,6},{8,11},{9,10},{10,... | collective-permute-start | bytes 2064392 | tf_op jit(solution)/shard_map/ppermute | solution.py:64
  81.2 6.6 %collective-permute-done.4.side = bf16[656,896]{1,0:T(8,128)(2,1)} collective-permute-done((bf16[656,896]{1,0:T(8,128)(2,1)}, bf16[656,896]{1,0:T(8,128)(2,1)}, u32[]{:S(2)}, u32[]{:S(2)}) %collective-permute-start.4) | collective-permute-done | bytes 1175584 | tf_op jit(solution)/shard_map/ppermute | solution.py:64
  88.5 6.9 %collective-permute-done.5.far = bf16[400,896]{1,0:T(8,128)(2,1)S(1)} collective-permute-done((bf16[400,896]{1,0:T(8,128)(2,1)}, bf16[400,896]{1,0:T(8,128)(2,1)S(1)}, u32[]{:S(2)}, u32[]{:S(2)}) %collective-permute-start.5) | collective-permute-done | bytes 716832 | tf_op jit(solution)/shard_map/ppermute | solution.py:64
  95.3 0.9 copy-done.4
  97.2 5.6 %collective-permute-done.6.far_rest = bf16[384,896]{1,0:T(8,128)(2,1)} collective-permute-done((bf16[384,896]{1,0:T(8,128)(2,1)}, bf16[384,896]{1,0:T(8,128)(2,1)}, u32[]{:S(2)}, u32[]{:S(2)}) %collective-permute-start.6) | collective-permute-done | bytes 688160 | tf_op jit(solution)/shard_map/ppermute | solution.py:64
  103.1 1.1 copy-done.5
  104.2 8.7 %project.1 = (f32[512,896]{1,0:T(8,128)}, f32[8,128]{1,0:T(8,128)S(1)}) custom-call(s32[4]{0:T(128)S(1)} %pad_add_fusion.place, bf16[512,896]{1,0:T(8,128)(2,1)S(1)} %copy-done.3, bf16[400,896]{1,0:T(8,128)(2,1)} %collective-permute-done.2.near, bf16[384,896]{1,0:T(8,128)(2,1)} %collective-permute-done.3.near_rest, ...), custom_call_target="tpu_custom_call" | custom-call | flops 3288334336 | bytes 13000000 | tf_op jit(solution)/shard_map/project/pallas_call | solution.py:273
  112.9 8.9 %psum.14.total = f32[8,128]{1,0:T(8,128)S(1)} all-reduce(f32[8,128]{1,0:T(8,128)S(1)} %get-tuple-element.23), channel_id=1, replica_groups=mesh['z'=8,'y'=8,'core'=2,'tensor'=4] {'tensor'}, use_global_device_ids=true, to_apply=%region_5.6 | all-reduce | flops 1024 | bytes 8192 | tf_op jit(solution)/shard_map/psum | solution.py:303
  121.9 1.5 copy-done.1
  124.2 1.0 reshape.95
  125.2 11.2 %all-to-all-start.1 = ((bf16[128,2,896]{2,1,0:T(2,128)(2,1)}), bf16[128,2,896]{2,1,0:T(2,128)(2,1)S(1)}, u32[]{:S(2)}, u32[]{:S(2)}) async-start(bf16[128,2,896]{2,1,0:T(2,128)(2,1)} %reshape.95), calls=%async_computation.1 | async-start | bytes 917504 | tf_op jit(solution)/shard_map/all_to_all | solution.py:305
  137.2 1.4 rsqrt_select_fusion.factor
  138.6 10.1 %psum.15 = f32[8,128]{1,0:T(8,128)S(1)} all-reduce(f32[8,128]{1,0:T(8,128)S(1)} %get-tuple-element.25), channel_id=1, replica_groups=mesh['z'=8,'y'=8,'core'=2,'tensor'=4] {'tensor'}, use_global_device_ids=true, to_apply=%region_7.8 | all-reduce | flops 1024 | bytes 8192 | tf_op jit(solution)/shard_map/psum | solution.py:309
  148.7 5.9 %all-to-all-done.1 = bf16[128,2,896]{2,1,0:T(2,128)(2,1)S(1)} async-done(((bf16[128,2,896]{2,1,0:T(2,128)(2,1)}), bf16[128,2,896]{2,1,0:T(2,128)(2,1)S(1)}, u32[]{:S(2)}, u32[]{:S(2)}) %all-to-all-start.1) | async-done | bytes 458784 | tf_op jit(solution)/shard_map/all_to_all | solution.py:305
  155.5 0.9 copy.12
  156.4 10.8 %all-to-all-start.2 = ((bf16[512,2,128]{2,1,0:T(2,128)(2,1)}), bf16[512,2,128]{2,1,0:T(2,128)(2,1)S(1)}, u32[]{:S(2)}, u32[]{:S(2)}) async-start(bf16[512,2,128]{2,1,0:T(2,128)(2,1)} %bitcast.10), calls=%async_computation.2 | async-start | bytes 524288 | tf_op jit(solution)/shard_map/all_to_all | solution.py:324
  167.4 15.5 %all-to-all-done.2 = bf16[512,2,128]{2,1,0:T(2,128)(2,1)S(1)} async-done(((bf16[512,2,128]{2,1,0:T(2,128)(2,1)}), bf16[512,2,128]{2,1,0:T(2,128)(2,1)S(1)}, u32[]{:S(2)}, u32[]{:S(2)}) %all-to-all-start.2) | async-done | bytes 262176 | tf_op jit(solution)/shard_map/all_to_all | solution.py:324
  182.9 0.9 home.1
  183.8 10.5 %pmax.7 = f32[128]{0:T(128)} all-reduce(f32[128]{0:T(128)S(1)} %slice_bitcast_fusion.1), channel_id=1, replica_groups=mesh['z'=8,'y'=8,'core'=2,'tensor'=4] {'tensor'}, use_global_device_ids=true, to_apply=%region_10.11 | all-reduce | flops 128 | bytes 1024 | tf_op jit(solution)/shard_map/pmax | solution.py:338
  (69 shorter events, 7.9 us)
Async XLA Ops:
  7.2 24.1 %copy-start = (bf16[1,512,896]{2,1,0:T(8,128)(2,1)S(1)}, bf16[1,512,896]{2,1,0:T(8,128)(2,1)}, u32[]{:S(2)}) copy-start(bf16[1,512,896]{2,1,0:T(8,128)(2,1)} %param.13) | copy-start | bytes 2752516
  7.2 9.6 %collective-permute-start = (bf16[28,896]{1,0:T(8,128)(2,1)}, bf16[28,896]{1,0:T(8,128)(2,1)S(1)}, u32[]{:S(2)}, u32[]{:S(2)}) collective-permute-start(bf16[28,896]{1,0:T(8,128)(2,1)} %bitcast.25), channel_id=1, source_target_pairs={{0,0},{1,128},{2,256},{3,384},{4,4},{5,20},{6,36},{7,52},{8,8},{9,... | collective-permute-start | bytes 150536 | tf_op jit(solution)/shard_map/ppermute | solution.py:196
  13.4 9.8 %collective-permute-start.1 = (bf16[28,896]{1,0:T(8,128)(2,1)}, bf16[28,896]{1,0:T(8,128)(2,1)S(1)}, u32[]{:S(2)}, u32[]{:S(2)}) collective-permute-start(bf16[28,896]{1,0:T(8,128)(2,1)} %bitcast.26), channel_id=1, source_target_pairs={{0,4},{1,20},{2,36},{3,52},{4,0},{5,128},{6,256},{7,384},{8,68},{9... | collective-permute-start | bytes 150536 | tf_op jit(solution)/shard_map/ppermute | solution.py:197
  23.2 8.3 %copy-start.10 = (s32[1,32]{1,0:T(1,128)S(1)}, s32[1,32]{1,0:T(1,128)}, u32[]{:S(2)}) copy-start(s32[1,32]{1,0:T(1,128)} %param.14) | copy-start | bytes 388
  23.2 8.5 %copy-start.2 = (bf16[128,3584]{1,0:T(8,128)(2,1)S(1)}, bf16[128,3584]{1,0:T(8,128)(2,1)}, u32[]{:S(2)}) copy-start(bf16[128,3584]{1,0:T(8,128)(2,1)} %residual.1) | copy-start | bytes 2752516
  23.2 8.4 %copy-start.3 = (bf16[512,896]{1,0:T(8,128)(2,1)S(1)}, bf16[512,896]{1,0:T(8,128)(2,1)}, u32[]{:S(2)}) copy-start(bf16[512,896]{1,0:T(8,128)(2,1)} %context.3) | copy-start | bytes 2752516
  24.2 23.3 %all-to-all-start = ((bf16[8,56,896]{2,1,0:T(8,128)(2,1)}), bf16[8,56,896]{2,1,0:T(8,128)(2,1)}, u32[]{:S(2)}, u32[]{:S(2)}) async-start(bf16[8,56,896]{2,1,0:T(8,128)(2,1)} %broadcast_in_dim.89), calls=%async_computation | async-start | bytes 1605632 | tf_op jit(solution)/shard_map/all_to_all | solution.py:224
  31.2 71.9 %all-gather.2.cloned.1.call-start = ((), (), s32[]{:S(2)}) async-start(), calls=%async_computation.3 | async-start | bytes 7225344 | tf_op jit(solution)/shard_map/all_gather | solution.py:229
  31.2 42.1 %copy-start.7 = (s32[128]{0:T(128)S(1)}, s32[128]{0:T(128)}, u32[]{:S(2)}) copy-start(s32[128]{0:T(128)} %param.17) | copy-start | bytes 1540
  31.2 42.1 %copy-start.8 = (s32[128]{0:T(128)S(1)}, s32[128]{0:T(128)}, u32[]{:S(2)}) copy-start(s32[128]{0:T(128)} %param.16) | copy-start | bytes 1540
  31.2 42.1 %copy-start.9 = (s32[128,1]{0,1:T(1,128)S(1)}, s32[128,1]{0,1:T(1,128)}, u32[]{:S(2)}) copy-start(s32[128,1]{0,1:T(1,128)} %param.15) | copy-start | bytes 1540
  32.4 1.0 copy-start.6
  33.4 13.2 %collective-permute-start.2 = (bf16[400,896]{1,0:T(8,128)(2,1)S(1)}, bf16[400,896]{1,0:T(8,128)(2,1)}, u32[]{:S(2)}, u32[]{:S(2)}) collective-permute-start(bf16[400,896]{1,0:T(8,128)(2,1)S(1)} %get-tuple-element.15), channel_id=1, source_target_pairs={{0,1},{1,0},{2,3},{3,2},{4,7},{5,6},{6,5},{7,4},{8,9},{9,8},{10,11... | collective-permute-start | bytes 2150408 | tf_op jit(solution)/shard_map/ppermute | solution.py:64
  47.6 12.9 %collective-permute-start.3 = (bf16[384,896]{1,0:T(8,128)(2,1)S(1)}, bf16[384,896]{1,0:T(8,128)(2,1)}, u32[]{:S(2)}, u32[]{:S(2)}) collective-permute-start(bf16[384,896]{1,0:T(8,128)(2,1)S(1)} %get-tuple-element.16), channel_id=1, source_target_pairs={{0,1},{1,0},{2,3},{3,2},{4,7},{5,6},{6,5},{7,4},{8,9},{9,8},{10,11... | collective-permute-start | bytes 2064392 | tf_op jit(solution)/shard_map/ppermute | solution.py:64
  60.6 27.2 %collective-permute-start.4 = (bf16[656,896]{1,0:T(8,128)(2,1)}, bf16[656,896]{1,0:T(8,128)(2,1)}, u32[]{:S(2)}, u32[]{:S(2)}) collective-permute-start(bf16[656,896]{1,0:T(8,128)(2,1)} %copy-done.6), channel_id=1, source_target_pairs={{0,3},{1,2},{2,1},{3,0},{4,5},{5,4},{6,7},{7,6},{8,11},{9,10},{10,... | collective-permute-start | bytes 3526664 | tf_op jit(solution)/shard_map/ppermute | solution.py:64
  73.8 21.6 %collective-permute-start.5 = (bf16[400,896]{1,0:T(8,128)(2,1)}, bf16[400,896]{1,0:T(8,128)(2,1)S(1)}, u32[]{:S(2)}, u32[]{:S(2)}) collective-permute-start(bf16[400,896]{1,0:T(8,128)(2,1)} %collective-permute-done.2.near), channel_id=1, source_target_pairs={{0,3},{1,2},{2,1},{3,0},{4,5},{5,4},{6,7},{7,6},{8,11},{9,10},{10,... | collective-permute-start | bytes 2150408 | tf_op jit(solution)/shard_map/ppermute | solution.py:64
  76.5 26.3 %collective-permute-start.6 = (bf16[384,896]{1,0:T(8,128)(2,1)}, bf16[384,896]{1,0:T(8,128)(2,1)}, u32[]{:S(2)}, u32[]{:S(2)}) collective-permute-start(bf16[384,896]{1,0:T(8,128)(2,1)} %collective-permute-done.3.near_rest), channel_id=1, source_target_pairs={{0,3},{1,2},{2,1},{3,0},{4,5},{5,4},{6,7},{7,6},{8,11},{9,10},{10,... | collective-permute-start | bytes 2064392 | tf_op jit(solution)/shard_map/ppermute | solution.py:64
  95.3 0.9 copy-start.4
  103.1 1.1 copy-start.5
  121.9 1.5 copy-start.1
  125.2 29.5 %all-to-all-start.1 = ((bf16[128,2,896]{2,1,0:T(2,128)(2,1)}), bf16[128,2,896]{2,1,0:T(2,128)(2,1)S(1)}, u32[]{:S(2)}, u32[]{:S(2)}) async-start(bf16[128,2,896]{2,1,0:T(2,128)(2,1)} %reshape.95), calls=%async_computation.1 | async-start | bytes 917504 | tf_op jit(solution)/shard_map/all_to_all | solution.py:305
  156.4 26.4 %all-to-all-start.2 = ((bf16[512,2,128]{2,1,0:T(2,128)(2,1)}), bf16[512,2,128]{2,1,0:T(2,128)(2,1)S(1)}, u32[]{:S(2)}, u32[]{:S(2)}) async-start(bf16[512,2,128]{2,1,0:T(2,128)(2,1)} %bitcast.10), calls=%async_computation.2 | async-start | bytes 524288 | tf_op jit(solution)/shard_map/all_to_all | solution.py:324
Sparse Core Ops, SparseCore 0:
  47.7 55.2 all-gather.1
